TPU v7x, 512 devices: a whole 4x4x16 slice. The times are simulated.
512 devices in a mesh: sub: 64 (over y, z), grp: 8 (over x, core).
Axes of the slice: x: 4, y: 4, z: 16, core: 2. Of those that a mesh axis runs over, the one named last changes fastest.
Arguments:
- schur_inverse: bfloat16 [64, 8, 1024, 1024], P('sub', 'grp'), may hold values from -1 to 4, as said below
- schur: bfloat16 [64, 8, 1024, 1024], P('sub', 'grp'), may hold values from -1 to 4, as said below
- coarse_basis: float32 [64, 8, 8, 1024], P('sub', 'grp'), may hold values from -0.6 to 0.6
- corner_index: int32 [64, 8, 8], P('sub', 'grp'), may hold values from 0 to 255
- coarse_inverse: float32 [256, 256], replicated, may hold values from -1 to 4, as said below
- neighbor_map: int32 [64, 8, 512], P('sub', 'grp'), may hold values from 0 to 511, each once within a row
- load: float32 [64, 8, 1024, 32], P('sub', 'grp'), may hold values from -6 to 6
- previous: bfloat16 [64, 8, 1024, 256], P('sub', 'grp'), may hold values from -7 to 7
- mass: float32 [64, 8, 1024], P('sub', 'grp'), may hold values from 0.5 to 2
Outputs:
- new_block: float32 [64, 8, 1024, 32], P('sub', 'grp')
- multipliers: float32 [64, 8, 512, 32], P('sub', 'grp')
- coefficients: float32 [256, 32], replicated
- factor: float32 [32, 32], replicated
Inputs may be any that keep to these rules, and one draw needn't show every extreme that they name: `corner_index`: each subdomain's 8 corners name coarse dofs. `neighbor_map`: each row is a permutation of the 512 multiplier numbers. `schur_inverse`: each block is symmetric positive definite. `schur`: each block is symmetric positive definite. `coarse_inverse`: symmetric positive definite.
All inputs are finite; a program needn't handle non-finite values.
Results may differ from a plain program's by a relative error of at most 0.005.
Values sent between devices are 32-bit elements; how exact they have to be, the bound alone decides.
No kernel may reach another device: no remote copies, remote signals or barrier semaphores. Data moves between devices by JAX's collectives and lax.ppermute only.
A program may use at most 64 MiB of HBM per device.

v0:
```python
import jax
import jax.numpy as jnp
from jax import lax
from jax.sharding import PartitionSpec as P

ITERS = 3


HI = lax.Precision.HIGHEST


def shifted(shard, axis, by):
    peers = lax.axis_size(axis)
    pairs = [(i, i + by) for i in range(peers) if 0 <= i + by < peers]
    return lax.ppermute(shard, axis, pairs)


def on_device(
    schur_inverse,
    schur,
    coarse_basis,
    corner_index,
    coarse_inverse,
    neighbor_map,
    load,
    previous,
    mass,
):
    inverse_block = schur_inverse[0, 0]
    local_schur = schur[0, 0]
    basis_rows = coarse_basis[0, 0]
    corners = corner_index[0, 0]
    left_map = neighbor_map[0, 0]
    rhs_block = load[0, 0]
    earlier = previous[0, 0].astype(jnp.float32)
    weights = mass[0, 0]
    face = left_map.shape[0]
    coarse_count = coarse_inverse.shape[0]
    total_rows = weights.shape[0] * lax.axis_size("sub") * lax.axis_size("grp")
    position = lax.axis_index("sub")
    active = (position < lax.axis_size("sub") - 1).astype(jnp.float32)
    inverse_map = jnp.zeros((face,), jnp.int32).at[left_map].set(jnp.arange(face, dtype=jnp.int32))
    selector = (corners[:, None] == jnp.arange(coarse_count, dtype=jnp.int32)[None, :]).astype(
        jnp.float32
    )
    scaled = weights[:, None] / total_rows

    def to_boundary(multi):
        arriving = shifted(multi[0], "sub", 1)
        return jnp.concatenate([-arriving[left_map], multi[0]], axis=0)

    def to_dual(field):
        send = field[:face][inverse_map]
        after = shifted(send, "sub", -1)
        return ((field[face:] - after) * active,)

    def solve_local(t):
        local = jnp.dot(inverse_block, t.astype(jnp.bfloat16), preferred_element_type=jnp.float32)
        corner_terms = jnp.dot(basis_rows, t, precision=HI)
        spread = jnp.dot(selector.T, corner_terms, precision=HI)
        coarse_rhs = lax.psum(spread, ("sub", "grp"))
        coarse = jnp.dot(coarse_inverse, coarse_rhs, precision=HI)
        picked = jnp.dot(selector, coarse, precision=HI)
        return local + jnp.dot(basis_rows.T, picked, precision=HI)

    def precondition(r):
        spread = 0.5 * to_boundary(r)
        values = jnp.dot(
            local_schur, spread.astype(jnp.bfloat16), preferred_element_type=jnp.float32
        )
        return jax.tree.map(lambda item: 0.5 * item, to_dual(values))

    def axpy(base_field, factor_cols, other):
        return jax.tree.map(lambda a, b: a + factor_cols * b, base_field, other)

    rhs = to_dual(solve_local(rhs_block))
    lam = jax.tree.map(jnp.zeros_like, rhs)
    resid = rhs

    def column_dot(a, b):
        return lax.psum(jnp.sum(a * b, axis=0), ("sub", "grp"))

    precond = precondition(resid)
    direction = precond
    inner = column_dot(resid[0], precond[0])
    for step in range(ITERS):
        image = to_dual(solve_local(to_boundary(direction)))
        alpha = inner / column_dot(direction[0], image[0])
        lam = axpy(lam, alpha, direction)
        resid = axpy(resid, -alpha, image)
        if step + 1 < ITERS:
            precond = precondition(resid)
            inner_next = column_dot(resid[0], precond[0])
            direction = axpy(precond, inner_next / inner, direction)
            inner = inner_next
    primal = solve_local(rhs_block - to_boundary(lam))
    first = lax.psum(jnp.dot(earlier.T, scaled * primal, precision=HI), ("sub", "grp"))
    projected = primal - jnp.dot(earlier, first, precision=HI)
    second = lax.psum(jnp.dot(earlier.T, scaled * projected, precision=HI), ("sub", "grp"))
    coefficients = first + second
    final = projected - jnp.dot(earlier, second, precision=HI)
    gram_block = lax.psum(jnp.dot(final.T, scaled * final, precision=HI), ("sub", "grp"))
    lower = jnp.linalg.cholesky(gram_block)
    solved = lax.linalg.triangular_solve(
        lower, final, left_side=False, lower=True, transpose_a=True
    )
    return (solved[None, None], lam[0][None, None], coefficients, lower)


def solution(mesh):
    return jax.shard_map(
        on_device,
        mesh=mesh,
        in_specs=(
            P("sub", "grp", None, None),
            P("sub", "grp", None, None),
            P("sub", "grp", None, None),
            P("sub", "grp", None),
            P(),
            P("sub", "grp", None),
            P("sub", "grp", None, None),
            P("sub", "grp", None, None),
            P("sub", "grp", None),
        ),
        out_specs=(P("sub", "grp", None, None), P("sub", "grp", None, None), P(), P()),
        check_vma=False,
    )
```

profile of v0, /device:TPU:1, one launch (start us, length us, event | category | flops | bytes accessed | tf_op | source)
XLA Modules:
  0.0 1463.9 jit_solution(17263260884273037305)
XLA Ops:
  3.0 111.4 %psum.98 = f32[256,32]{1,0:T(8,128)S(1)} all-reduce(f32[256,32]{1,0:T(8,128)S(1)} %fusion.119), channel_id=1, replica_groups=mesh['sub'=64,'grp'=8] {'sub','grp'}, use_global_device_ids=true, to_apply=%region_0.0 | all-reduce | flops 8192 | bytes 65536 | tf_op jit(solution)/shard_map/psum | solution.py:61
  117.6 1.6 fusion.25
  119.4 2.4 scatter_custom_fusion
  123.0 1.3 collective-permute-start
  124.3 3.7 collective-permute-done
  128.0 2.6 collective-permute-start.1
  130.7 1.3 collective-permute-done.1
  133.3 2.3 fusion.16
  136.9 1.3 collective-permute-start.2
  138.2 4.0 collective-permute-done.2
  142.3 3.4 collective-permute-start.3
  145.6 1.3 collective-permute-done.3
  148.8 108.1 %psum.100 = f32[256,32]{1,0:T(8,128)S(1)} all-reduce(f32[256,32]{1,0:T(8,128)S(1)} %fusion.126), channel_id=1, replica_groups=mesh['sub'=64,'grp'=8] {'sub','grp'}, use_global_device_ids=true, to_apply=%region_4.0 | all-reduce | flops 8192 | bytes 65536 | tf_op jit(solution)/shard_map/psum | solution.py:61
  259.9 1.3 collective-permute-start.4
  261.2 4.0 collective-permute-done.4
  265.3 101.6 %all-reduce = (f32[32]{0:T(128)S(1)}, f32[32]{0:T(128)S(1)}) all-reduce(f32[32]{0:T(128)S(1)} %get-tuple-element.5, f32[32]{0:T(128)S(1)} %get-tuple-element.4), channel_id=1, replica_groups=mesh['sub'=64,'grp'=8] {'sub','grp'}, use_global_device_ids=true, to_apply=%region_3.0 | all-reduce | flops 64 | bytes 512 | tf_op jit(solution)/shard_map/psum | solution.py:81
  367.0 1.8 collective-permute-start.5
  368.8 1.3 collective-permute-done.5
  371.4 2.3 fusion.19
  375.0 1.3 collective-permute-start.6
  376.3 4.0 collective-permute-done.6
  380.5 105.2 %psum.102 = f32[32]{0:T(128)S(1)} all-reduce(f32[32]{0:T(128)S(1)} %multiply_reduce_fusion.2), channel_id=1, replica_groups=mesh['sub'=64,'grp'=8] {'sub','grp'}, use_global_device_ids=true, to_apply=%region_8.0 | all-reduce | flops 32 | bytes 256 | tf_op jit(solution)/shard_map/psum | solution.py:81
  485.7 3.7 collective-permute-start.7
  489.4 1.3 collective-permute-done.7
  492.6 102.0 %psum.103 = f32[256,32]{1,0:T(8,128)S(1)} all-reduce(f32[256,32]{1,0:T(8,128)S(1)} %fusion.124), channel_id=1, replica_groups=mesh['sub'=64,'grp'=8] {'sub','grp'}, use_global_device_ids=true, to_apply=%region_9.0 | all-reduce | flops 8192 | bytes 65536 | tf_op jit(solution)/shard_map/psum | solution.py:61
  597.5 1.3 collective-permute-start.8
  598.8 4.0 collective-permute-done.8
  602.9 102.3 %psum.104 = f32[32]{0:T(128)S(1)} all-reduce(f32[32]{0:T(128)S(1)} %multiply_reduce_fusion.1), channel_id=1, replica_groups=mesh['sub'=64,'grp'=8] {'sub','grp'}, use_global_device_ids=true, to_apply=%region_11.0 | all-reduce | flops 32 | bytes 256 | tf_op jit(solution)/shard_map/psum | solution.py:81
  705.3 1.6 collective-permute-start.9
  706.9 1.3 collective-permute-done.9
  709.5 2.3 fusion.22
  713.1 1.3 collective-permute-start.10
  714.4 4.0 collective-permute-done.10
  718.6 104.7 %psum.105 = f32[32]{0:T(128)S(1)} all-reduce(f32[32]{0:T(128)S(1)} %multiply_reduce_fusion), channel_id=1, replica_groups=mesh['sub'=64,'grp'=8] {'sub','grp'}, use_global_device_ids=true, to_apply=%region_13.0 | all-reduce | flops 32 | bytes 256 | tf_op jit(solution)/shard_map/psum | solution.py:81
  823.3 3.5 collective-permute-start.11
  826.9 1.3 collective-permute-done.11
  830.0 101.9 %psum.106 = f32[256,32]{1,0:T(8,128)S(1)} all-reduce(f32[256,32]{1,0:T(8,128)S(1)} %fusion.122), channel_id=1, replica_groups=mesh['sub'=64,'grp'=8] {'sub','grp'}, use_global_device_ids=true, to_apply=%region_14.0 | all-reduce | flops 8192 | bytes 65536 | tf_op jit(solution)/shard_map/psum | solution.py:61
  934.9 1.3 collective-permute-start.12
  936.2 4.0 collective-permute-done.12
  940.3 101.8 %psum.107 = f32[32]{0:T(128)S(1)} all-reduce(f32[32]{0:T(128)S(1)} %fusion.78), channel_id=1, replica_groups=mesh['sub'=64,'grp'=8] {'sub','grp'}, use_global_device_ids=true, to_apply=%region_16.0 | all-reduce | flops 32 | bytes 256 | tf_op jit(solution)/shard_map/psum | solution.py:81
  1042.3 1.6 collective-permute-start.13
  1043.9 1.3 collective-permute-done.13
  1047.1 104.3 %psum.108 = f32[256,32]{1,0:T(8,128)S(1)} all-reduce(f32[256,32]{1,0:T(8,128)S(1)} %fusion.120), channel_id=1, replica_groups=mesh['sub'=64,'grp'=8] {'sub','grp'}, use_global_device_ids=true, to_apply=%region_17.0 | all-reduce | flops 8192 | bytes 65536 | tf_op jit(solution)/shard_map/psum | solution.py:61
  1153.4 100.1 %psum.109 = f32[256,32]{0,1:T(8,128)S(1)} all-reduce(f32[256,32]{0,1:T(8,128)S(1)} %convolution_bitcast_fusion.3), channel_id=1, replica_groups=mesh['sub'=64,'grp'=8] {'sub','grp'}, use_global_device_ids=true, to_apply=%region_18.0 | all-reduce | flops 8192 | bytes 65536 | tf_op jit(solution)/shard_map/psum | solution.py:97
  1254.4 99.4 %psum.110 = f32[256,32]{0,1:T(8,128)S(1)} all-reduce(f32[256,32]{0,1:T(8,128)S(1)} %convolution_bitcast_fusion.2), channel_id=1, replica_groups=mesh['sub'=64,'grp'=8] {'sub','grp'}, use_global_device_ids=true, to_apply=%region_19.0 | all-reduce | flops 8192 | bytes 65536 | tf_op jit(solution)/shard_map/psum | solution.py:99
  1355.2 100.4 %psum.111 = f32[32,32]{0,1:T(8,128)S(1)} all-reduce(f32[32,32]{0,1:T(8,128)S(1)} %fusion.53), channel_id=1, replica_groups=mesh['sub'=64,'grp'=8] {'sub','grp'}, use_global_device_ids=true, to_apply=%region_20.0 | all-reduce | flops 1024 | bytes 8192 | tf_op jit(solution)/shard_map/psum | solution.py:102
  1455.6 2.9 cholesky.16
  1460.5 2.4 custom-call.6
  (139 shorter events, 38.7 us)
Async XLA Ops:
  0.6 116.9 %copy-start = (bf16[1,1,1024,1024]{3,2,1,0:T(8,128)(2,1)S(1)}, bf16[1,1,1024,1024]{3,2,1,0:T(8,128)(2,1)}, u32[]{:S(2)}) copy-start(bf16[1,1,1024,1024]{3,2,1,0:T(8,128)(2,1)} %param.9) | copy-start | bytes 6291460
  0.6 118.7 %copy-start.8 = (s32[1,1,512]{2,1,0:T(1,128)S(1)}, s32[1,1,512]{2,1,0:T(1,128)}, u32[]{:S(2)}) copy-start(s32[1,1,512]{2,1,0:T(1,128)} %param.14) | copy-start | bytes 6148
  123.0 5.0 collective-permute-start
  128.0 3.9 collective-permute-start.1
  136.8 11.5 copy-start.3
  136.8 11.7 copy-start.6
  136.8 120.2 %copy-start.2 = (f32[256,256]{1,0:T(8,128)S(1)}, f32[256,256]{1,0:T(8,128)}, u32[]{:S(2)}) copy-start(f32[256,256]{1,0:T(8,128)} %param.13) | copy-start | bytes 786436
  136.9 5.3 collective-permute-start.2
  142.3 4.7 collective-permute-start.3
  259.9 5.3 collective-permute-start.4
  367.0 3.1 collective-permute-start.5
  375.0 5.3 collective-permute-start.6
  485.7 5.0 collective-permute-start.7
  597.5 5.3 collective-permute-start.8
  705.3 2.9 collective-permute-start.9
  713.1 5.3 collective-permute-start.10
  823.3 4.8 collective-permute-start.11
  933.6 110.3 %copy-start.7 = (f32[1,1,1024]{2,1,0:T(1,128)S(1)}, f32[1,1,1024]{2,1,0:T(1,128)}, u32[]{:S(2)}) copy-start(f32[1,1,1024]{2,1,0:T(1,128)} %param.17) | copy-start | bytes 12292
  934.8 111.7 %copy-start.4 = (f32[1,1,1024,32]{2,3,1,0:T(8,128)S(1)}, f32[1,1,1024,32]{2,3,1,0:T(8,128)}, u32[]{:S(2)}) copy-start(f32[1,1,1024,32]{2,3,1,0:T(8,128)} %param.15) | copy-start | bytes 393220
  934.9 5.3 collective-permute-start.12
  1042.3 110.0 %copy-start.5 = (f32[512,32]{0,1:T(8,128)}, f32[512,32]{0,1:T(8,128)S(1)}, u32[]{:S(2)}) copy-start(f32[512,32]{0,1:T(8,128)S(1)} %multiply_add_fusion) | copy-start | bytes 196612
  1042.3 2.9 collective-permute-start.13
  1046.4 106.6 %copy-start.1 = (bf16[1,1,1024,256]{3,2,1,0:T(8,128)(2,1)S(1)}, bf16[1,1,1024,256]{3,2,1,0:T(8,128)(2,1)}, u32[]{:S(2)}) copy-start(bf16[1,1,1024,256]{3,2,1,0:T(8,128)(2,1)} %param.16) | copy-start | bytes 1572868
where the time goes:
time: 1470 us; the launch traced here: 1460 us
  blocking collectives  1340 us (91%)
  waiting for transfers between devices  37.1 us (3%)
  starting transfers between devices  27.2 us (2%)
  matrix products  25.6 us (2%)
  local copies, waits for them, and re-layouts  20.3 us (1%)
    psum x5, blocking collectives, solve_local(): coarse_rhs = lax.psum(spread, ('sub', 'grp'))  528 us
    psum x5, blocking collectives, column_dot(): return lax.psum(jnp.sum(a * b, axis=0), ('sub', 'grp'))  516 us
    psum x1, blocking collectives, on_device(): lax.psum(jnp.dot(final.T, scaled * final, precision=HI), ('sub', 'grp'))  100 us
    psum x1, blocking collectives, on_device(): lax.psum(jnp.dot(earlier.T, scaled * primal, precision=HI), ('sub', 'grp'))  100 us
    psum x1, blocking collectives, on_device(): lax.psum(jnp.dot(earlier.T, scaled * projected, precision=HI), ('sub', 'g...  99.4 us
    ppermute x14, waiting for transfers between devices, shifted(): return lax.ppermute(shard, axis, pairs)  37.1 us
  transfers between devices with their start and end apart: 14, of which 14 were waited for; matrix products, arithmetic and copies ran while one was open for 0% of the time, Pallas kernels for 0%

commit v1 on v0

v1 whole, which is shorter than its diff:
```python
import jax
import jax.numpy as jnp
import numpy as np
from jax import lax
from jax.experimental import pallas as pl
from jax.experimental.pallas import tpu as pltpu
from jax.sharding import Mesh, PartitionSpec as P

HI = lax.Precision.HIGHEST
F32 = jnp.float32
BF16 = jnp.bfloat16
RED = ("y", "x", "c")
LEVELS = 6
LANE = 128


def nn(a, b):
    return jnp.dot(a, b, precision=HI, preferred_element_type=F32)


def nt(a, b):
    return lax.dot_general(
        a, b, (((1,), (1,)), ((), ())), precision=HI, preferred_element_type=F32
    )


def lane_sum(a):
    return jnp.sum(a, axis=1, keepdims=True)


def call(kernel, outs, scratch=()):
    return pl.pallas_call(
        kernel,
        out_shape=outs,
        scratch_shapes=list(scratch),
        compiler_params=pltpu.CompilerParams(vmem_limit_bytes=48 * 1024 * 1024),
    )


def split_dot(t, mat):
    high = t.astype(BF16).astype(F32)
    both = jnp.concatenate([high, t - high], axis=0).astype(BF16)
    wide = jnp.dot(both, mat, preferred_element_type=F32)
    rows = t.shape[0]
    return wide[:rows] + wide[rows:]


def to_order(nm_col, face):
    return (nm_col == lax.broadcasted_iota(jnp.int32, (face, face), 1)).astype(F32)


def from_order(nm_row, face):
    return (nm_row == lax.broadcasted_iota(jnp.int32, (face, face), 0)).astype(F32)


def start_kernel(inv_ref, load_ref, basis_ref, nm_ref, corner_ref, sl_ref, sr_ref, cl_ref):
    face = nm_ref.shape[0]
    cols = load_ref.shape[1]
    corners = basis_ref.shape[0]
    rows = cols + corners
    load = jnp.transpose(load_ref[...])
    basis = basis_ref[...]
    order = to_order(nm_ref[...], face)
    wide = split_dot(load, inv_ref[...])
    left = nn(jnp.concatenate([wide[:, :face], basis[:, :face]], axis=0), order)
    sl_ref[0:rows, :] = left
    sr_ref[0:cols, :] = wide[:, face:]
    sr_ref[cols:rows, :] = basis[:, face:]
    for ref in (sl_ref, sr_ref):
        ref[rows : rows + 8, :] = jnp.zeros((8, face), F32)
        ref[rows : rows + 1, 0:corners] = corner_ref[...].astype(F32)
    cl_ref[...] = nt(load, basis)


def order_kernel(inv_ref, schur_ref, prev_ref, nm_col_ref, nm_row_ref, mass_ref,
                 inv_out, schur_out, prev_out, mass_out, *, total):
    face = nm_col_ref.shape[0]
    order32 = to_order(nm_col_ref[...], face)
    order = order32.astype(BF16)
    back = from_order(nm_row_ref[...], face).astype(BF16)
    for src, dst in ((inv_ref, inv_out), (schur_ref, schur_out)):
        dst[:, face:] = src[:, face:]
        dst[:, :face] = jnp.dot(src[:, :face], order, preferred_element_type=F32).astype(BF16)
        dst[:face, :] = jnp.dot(back, dst[:face, :], preferred_element_type=F32).astype(BF16)
    prev_out[face:, :] = prev_ref[face:, :]
    prev_out[:face, :] = jnp.dot(back, prev_ref[:face, :], preferred_element_type=F32).astype(BF16)
    mass = mass_ref[...] / total
    mass_out[:, face:] = mass[:, face:]
    mass_out[:, :face] = nn(jnp.broadcast_to(mass[:, :face], (8, face)), order32)[0:1]


def step_kernel(sl_ref, sr_ref, nl_ref, pr_ref, mask_ref, mat_ref, t_ref, ol_ref, or_ref,
                *, cols, width, scale):
    face = sl_ref.shape[1]
    new = width + 16
    rows = cols + new
    old = cols + width
    for lanes, own, other, shift in (
        (slice(0, face), sl_ref, pr_ref, 0),
        (slice(face, 2 * face), sr_ref, nl_ref, 16),
    ):
        keep = mask_ref[0:1, lanes]
        t_ref[0:cols, lanes] = (own[0:cols, :] - other[0:cols, :]) * keep
        edge = jnp.zeros((8, face), F32)
        mine = jnp.concatenate([edge, own[cols:old, :], edge], axis=0)
        blank = jnp.zeros((16, face), F32)
        theirs = other[cols:old, :]
        theirs = jnp.concatenate([theirs, blank] if shift == 0 else [blank, theirs], axis=0)
        t_ref[cols:rows, lanes] = (mine - theirs) * keep
    v = split_dot(t_ref[...], mat_ref[...])
    if scale != 1.0:
        v = v * scale
    ids = jnp.concatenate(
        [
            pr_ref[old : old + 8, 0:8],
            sl_ref[old : old + 8, 0:width],
            nl_ref[old : old + 8, width - 8 : width],
        ],
        axis=1,
    )
    for ref, lanes in ((ol_ref, slice(0, face)), (or_ref, slice(face, 2 * face))):
        ref[0:rows, :] = v[:, lanes]
        ref[rows : rows + 8, :] = jnp.zeros((8, face), F32)
        ref[rows : rows + 8, 0:new] = ids


def one_hot(ids, count):
    dof = lax.broadcasted_iota(jnp.int32, (count, ids.shape[1]), 0).astype(F32)
    return (ids == dof).astype(F32)


def pack(ref, at, matrix):
    half = matrix.shape[0] // 2
    ref[at : at + half, :] = matrix[:half, :half]
    ref[at + half : at + 2 * half, :] = matrix[half:, :half]
    ref[at + 2 * half : at + 3 * half, :] = matrix[half:, half:]


def unpack(ref, at):
    half = LANE
    a = ref[at : at + half, :]
    b = ref[at + half : at + 2 * half, :]
    c = ref[at + 2 * half : at + 3 * half, :]
    return jnp.concatenate(
        [jnp.concatenate([a, jnp.transpose(b)], axis=1), jnp.concatenate([b, c], axis=1)], axis=0
    )


def moment_kernel(sl0_ref, cl_ref, gram_ref, *refs, cols, count):
    out = refs[-1]
    half = count // 2
    tri = 3 * half

    def put(at, block):
        out[at : at + cols, :] = block[:, :half]
        out[at + cols : at + 2 * cols, :] = block[:, half:]

    base = 4 * tri
    own = sl0_ref.shape[0] - cols - 8
    put(base, nt(cl_ref[...], one_hot(sl0_ref[cols + own : cols + own + 1, 0:own], count)))
    sums = []
    for k in range(3):
        t_ref, l_ref, r_ref = refs[3 * k : 3 * k + 3]
        rows, double = t_ref.shape
        face = double // 2
        width = rows - cols
        spot = one_hot(l_ref[rows : rows + 1, 0:width], count)
        tl, tr = t_ref[cols:rows, :face], t_ref[cols:rows, face:]
        inner = nt(tl, l_ref[cols:rows, :]) + nt(tr, r_ref[cols:rows, :])
        pack(out, k * tri, nt(nn(spot, inner), spot))
        cross = nt(l_ref[0:cols, :], tl) + nt(r_ref[0:cols, :], tr)
        put(base + 2 * cols * (k + 1), nt(cross, spot))
        sums.append(
            lane_sum(t_ref[0:cols, :face] * l_ref[0:cols, :])
            + lane_sum(t_ref[0:cols, face:] * r_ref[0:cols, :])
        )
    pack(out, 3 * tri, gram_ref[...])
    at = base + 8 * cols
    out[at:, :] = jnp.zeros((out.shape[0] - at, LANE), F32)
    lane = lax.broadcasted_iota(jnp.int32, (cols, LANE), 1)
    block = jnp.zeros((cols, LANE), F32)
    for k in range(3):
        block = jnp.where(lane == k, sums[k], block)
    out[at : at + cols, :] = block


def combine_kernel(sums_ref, coarse_ref, ids_ref, mass_ref, prev_ref, *refs, cols, count):
    half = count // 2
    tri = 3 * half
    base = 4 * tri
    sl0, sr0 = refs[0:2]
    level = [None] + [refs[2 + 3 * k : 5 + 3 * k] for k in range(LEVELS)]
    out_ref, field_ref, dual_ref, scal_ref = refs[2 + 3 * LEVELS :]
    face = sl0.shape[1]

    def get(at):
        return jnp.concatenate([sums_ref[at : at + cols, :], sums_ref[at + cols : at + 2 * cols, :]], axis=1)

    m0, m1, m2 = (unpack(sums_ref, k * tri) for k in range(3))
    coarse = coarse_ref[...]
    c_load, w0x, w1x, w2x = (get(base + 2 * cols * k) for k in range(4))
    at = base + 8 * cols
    s0, s1, s2 = (sums_ref[at : at + cols, k : k + 1] for k in range(3))
    g0 = nn(c_load, coarse)
    m0g0, m1g0, m2g0 = nn(g0, m0), nn(g0, m1), nn(g0, m2)
    c0 = w0x + m0g0
    g1 = nn(c0, coarse)
    m0g1, m1g1 = nn(g1, m0), nn(g1, m1)
    rz0 = s0 + lane_sum(2.0 * w0x * g0 + g0 * m0g0)
    del0 = s1 + lane_sum(2.0 * w1x * g0 + g0 * m1g0 + c0 * g1)
    nu0 = s2 + lane_sum(2.0 * w2x * g0 + g0 * m2g0 + 2.0 * w1x * g1 + 2.0 * g1 * m1g0 + g1 * m0g1)
    al0 = rz0 / del0
    be1 = (rz0 - 2.0 * al0 * del0 + al0 * al0 * nu0) / rz0
    cz1 = c0 - al0 * (w1x + m1g0 + m0g1)
    gz1 = nn(cz1, coarse)
    cm = (
        (1.0 + be1) * (w1x + m1g0)
        - al0 * (m1g1 + w2x + m2g0)
        + nn(gz1, m0)
        + be1 * m0g1
    )
    gm = nn(cm, coarse)
    spot = one_hot(ids_ref[0:1, :], count)
    local = nn(jnp.concatenate([g0, g1, gz1, gm], axis=0), spot)

    def coef(k, n):
        width = 8 * (2 * k + 1)
        first = 8 * (LEVELS - k)
        return local[: n * cols, first : first + width]

    def spread(k, ref, n, lanes):
        width = 8 * (2 * k + 1)
        wide = nn(coef(k, n), ref[cols : cols + width, lanes])
        return [wide[i * cols : (i + 1) * cols] for i in range(n)]

    def fields(b2, b4, b6, lanes):
        x2, x4, x6 = (b[0:cols, lanes] for b in (b2, b4, b6))
        p20, p21, p2z = spread(2, b2, 3, lanes)
        p40, p41 = spread(4, b4, 2, lanes)
        (p60,) = spread(6, b6, 1, lanes)
        z0 = x2 + p20
        n0 = x4 + p40 + p21
        z1 = z0 - al0 * n0
        n1 = x4 + p40 - al0 * (x6 + p60 + p41) + p2z
        return z0, z1, n1 + be1 * n0

    left, right, whole = slice(0, face), slice(face, 2 * face), slice(0, face)
    t1, t2, t3, t4, t5, t6 = (level[k][0] for k in range(1, 7))
    z0, z1, m = fields(t2, t4, t6, right)
    _, _, m_left = fields(t2, t4, t6, left)
    p10, p11, p1z = spread(1, t1, 3, right)
    p30, p31 = spread(3, t3, 2, right)
    (p50,) = spread(5, t5, 1, right)
    x1, x3, x5 = (ref[0:cols, right] for ref in (t1, t3, t5))
    d = x1 + p10
    w0 = x3 + p30 + p11
    w1 = x3 + p30 - al0 * (x5 + p50 + p31) + p1z
    r1 = d - al0 * w0
    q1 = w1 + be1 * w0
    p1 = z1 + be1 * z0
    for side, (own, pos, lanes) in enumerate(((sl0, 1, left), (sr0, 2, right))):
        u = fields(level[2][pos], level[4][pos], level[6][pos], whole)
        corner = spread(0, own, 4, whole)
        field_ref[0:cols, lanes] = own[0:cols, :] + corner[0]
        for i in range(3):
            field_ref[(i + 1) * cols : (i + 2) * cols, lanes] = u[i] + corner[i + 1]
        mu = lane_sum((m if side else m_left) * u[2])
        mm = mu if side == 0 else mm + mu
    for i, item in enumerate((z0, z1, m)):
        dual_ref[i * cols : (i + 1) * cols, :] = item
    moments = (
        lane_sum(r1 * z1), lane_sum(r1 * m), lane_sum(q1 * z1), lane_sum(q1 * m),
        lane_sum(r1 * p1), lane_sum(p1 * q1), lane_sum(z1 * w1), lane_sum(m * w1), mm,
    )
    lane = lax.broadcasted_iota(jnp.int32, (cols, LANE), 1)
    block = jnp.zeros((cols, LANE), F32)
    for k, item in enumerate(moments):
        block = jnp.where(lane == k, item, block)
    field = field_ref[...]
    scaled = field * mass_ref[...]
    tq = nn(scaled, prev_ref[...].astype(F32))
    out_ref[0 : 4 * cols, :] = tq[:, :half]
    out_ref[4 * cols : 8 * cols, :] = tq[:, half:]
    out_ref[8 * cols : 12 * cols, :] = nt(scaled, field)
    out_ref[12 * cols : 13 * cols, :] = block
    out_ref[13 * cols :, :] = jnp.zeros((out_ref.shape[0] - 13 * cols, LANE), F32)
    block = jnp.zeros((cols, LANE), F32)
    for k, item in enumerate((al0, be1, lane_sum(cm * gm))):
        block = jnp.where(lane == k, item, block)
    scal_ref[...] = block


def final_kernel(sums_ref, early_ref, scal_ref, field_ref, dual_ref, prev_ref, nm_ref,
                 block_ref, multi_ref, coef_ref, factor_ref, *, cols, count):
    half = count // 2
    tri = 3 * half
    face = dual_ref.shape[1]
    at = 12 * cols
    r1z1, r1m, q1z1, q1m, r1p1, p1q1, z1w1, mw1, mm = (
        sums_ref[at : at + cols, k : k + 1] for k in range(9)
    )
    al0, be1, extra = (scal_ref[:, k : k + 1] for k in range(3))
    mfm = mm + extra
    al1 = r1p1 / p1q1
    z2q1 = q1z1 - al1 * q1m
    be2 = -z2q1 / p1q1
    rz2 = r1z1 - al1 * (r1m + q1z1) + al1 * al1 * q1m
    z2fz2 = z1w1 - 2.0 * al1 * mw1 + al1 * al1 * mfm
    al2 = rz2 / (z2fz2 + 2.0 * be2 * z2q1 + be2 * be2 * p1q1)
    along = al1 + al2 * be2
    parts = (al0 + along * be1, along + al2, -al1 * al2)
    multi = sum(y * dual_ref[i * cols : (i + 1) * cols, :] for i, y in enumerate(parts))
    multi_ref[...] = jnp.transpose(multi)
    weights = [jnp.ones((cols, 1), F32)] + [-y for y in parts]
    primal = sum(y * field_ref[i * cols : (i + 1) * cols, :] for i, y in enumerate(weights))
    g1 = sum(
        y
        * jnp.concatenate(
            [sums_ref[i * cols : (i + 1) * cols, :], sums_ref[(4 + i) * cols : (5 + i) * cols, :]],
            axis=1,
        )
        for i, y in enumerate(weights)
    )
    row = lax.broadcasted_iota(jnp.int32, (cols, cols), 0)
    col = lax.broadcasted_iota(jnp.int32, (cols, cols), 1)
    eye = (row == col).astype(F32)
    across = [jnp.sum(y * eye, axis=0, keepdims=True) for y in weights]
    gram = jnp.zeros((cols, cols), F32)
    for i in range(4):
        for j in range(4):
            tile = sums_ref[(8 + i) * cols : (9 + i) * cols, j * cols : (j + 1) * cols]
            gram = gram + weights[i] * tile * across[j]
    basis = unpack(early_ref, 3 * tri)
    c = 2.0 * g1 - nn(g1, basis)
    coef_ref[...] = jnp.transpose(c)
    gram = gram - nt(c, g1) - nt(g1, c) + nt(nn(c, basis), c)
    gram = 0.5 * (gram + jnp.transpose(gram))
    final = primal - nt(c, prev_ref[...].astype(F32))
    work = jnp.concatenate([gram, eye], axis=1)
    index = lax.broadcasted_iota(jnp.int32, (cols, 1), 0)
    pivots = jnp.zeros((cols, 1), F32)
    for k in range(cols):
        pivot = work[k : k + 1, k : k + 1]
        pivots = jnp.where(index == k, pivot, pivots)
        times = jnp.where(index > k, work[:, k : k + 1], 0.0) / pivot
        work = work - times * work[k : k + 1, :]
    work = work / jnp.sqrt(pivots)
    factor_ref[...] = jnp.transpose(jnp.where(row <= col, work[:, :cols], 0.0))
    solved = nn(work[:, cols:], final)
    left = nn(solved[:, :face], from_order(nm_ref[...], face))
    block_ref[:face, :] = jnp.transpose(left)
    block_ref[face:, :] = jnp.transpose(solved[:, face:])


def over_all(rows, n_red, n_z):
    part = rows.shape[0] // n_red
    mine = lax.all_to_all(rows.reshape(n_red, part, LANE), RED, 0, 0, tiled=True)
    mine = jnp.sum(mine, axis=0)
    peers = lax.all_to_all(jnp.broadcast_to(mine[None], (n_z, part, LANE)), "z", 0, 0, tiled=True)
    mine = jnp.sum(peers, axis=0)
    full = lax.all_to_all(jnp.broadcast_to(mine[None], (n_red, part, LANE)), RED, 0, 0, tiled=True)
    return full.reshape(n_red * part, LANE)


def up(count, unit):
    return -(-count // unit) * unit


def solution(mesh):
    n_sub, n_grp = mesh.shape["sub"], mesh.shape["grp"]
    n_y = min(4, n_sub)
    n_z = n_sub // n_y
    n_c = 2
    n_x = n_grp // n_c
    fine = Mesh(np.asarray(mesh.devices).reshape(n_y, n_z, n_x, n_c), ("y", "z", "x", "c"))
    n_red = n_y * n_x * n_c
    along = ("y", "z")
    ahead = [(i, i + 1) for i in range(n_sub - 1)]
    behind = [(i + 1, i) for i in range(n_sub - 1)]

    def on_device(schur_inverse, schur, coarse_basis, corner_index, coarse_inverse, neighbor_map,
                  load, previous, mass):
        inverse_block, schur_block, basis = schur_inverse[0, 0], schur[0, 0], coarse_basis[0, 0]
        corners, nm = corner_index[0, 0], neighbor_map[0, 0]
        rhs, earlier, weights = load[0, 0], previous[0, 0], mass[0, 0]
        rows, cols = rhs.shape
        face = nm.shape[0]
        count = coarse_inverse.shape[0]
        total = rows * n_sub * n_grp
        own = corners.shape[0]
        position = lax.axis_index(along)
        nm_row, nm_col = nm[None, :], nm[:, None]
        side = jnp.arange(2 * face) < face
        mask = jnp.where(side, position > 0, position < n_sub - 1).astype(F32)[None, :]
        mask = jnp.broadcast_to(mask, (8, 2 * face))

        def shape(*dims):
            return jax.ShapeDtypeStruct(dims, F32)

        sl, sr, cl = call(
            start_kernel, (shape(cols + own + 8, face), shape(cols + own + 8, face), shape(cols, own))
        )(inverse_block, rhs, basis, nm_col, corners[None, :])
        inv_p, schur_p, prev_p, mass_p = call(
            lambda *refs: order_kernel(*refs, total=total),
            (
                jax.ShapeDtypeStruct((rows, rows), BF16),
                jax.ShapeDtypeStruct((rows, rows), BF16),
                jax.ShapeDtypeStruct(earlier.shape, BF16),
                shape(1, rows),
            ),
        )(inverse_block, schur_block, earlier, nm_col, nm_row, weights[None, :])
        wide = earlier.astype(F32)
        gram = jnp.dot(wide.T, (weights / total)[:, None] * wide, precision=HI)

        chain = [sl, sr]
        width = own
        for k in range(1, LEVELS + 1):
            nl = lax.ppermute(sl, along, behind)
            pr = lax.ppermute(sr, along, ahead)
            odd = k % 2 == 1
            out = cols + width + 16
            t, sl, sr = call(
                lambda *refs, width=width, odd=odd: step_kernel(
                    *refs, cols=cols, width=width, scale=0.25 if odd else 1.0
                ),
                (shape(out, 2 * face), shape(out + 8, face), shape(out + 8, face)),
            )(sl, sr, nl, pr, mask, schur_p if odd else inv_p)
            chain += [t, sl, sr]
            width += 16
            if k == 3:
                size = up(6 * count + 9 * cols, 8 * n_red)
                first = call(
                    lambda *refs: moment_kernel(*refs, cols=cols, count=count), shape(size, LANE)
                )(chain[0], cl, gram, *chain[2:11])
                first = over_all(first, n_red, n_z)
        ids = sl[cols + width : cols + width + 8, :LANE]
        size = up(13 * cols, 8 * n_red)
        second, field, dual, scal = call(
            lambda *refs: combine_kernel(*refs, cols=cols, count=count),
            (shape(size, LANE), shape(4 * cols, rows), shape(3 * cols, face), shape(cols, LANE)),
        )(first, coarse_inverse, ids, mass_p, prev_p, *chain)
        second = over_all(second, n_red, n_z)
        block, multi, coefficients, factor = call(
            lambda *refs: final_kernel(*refs, cols=cols, count=count),
            (shape(rows, cols), shape(face, cols), shape(count, cols), shape(cols, cols)),
        )(second, first, scal, field, dual, prev_p, nm_row)
        return block[None, None], multi[None, None], coefficients, factor

    split = (along, ("x", "c"))
    return jax.shard_map(
        on_device,
        mesh=fine,
        in_specs=(
            P(*split, None, None),
            P(*split, None, None),
            P(*split, None, None),
            P(*split, None),
            P(),
            P(*split, None),
            P(*split, None, None),
            P(*split, None, None),
            P(*split, None),
        ),
        out_specs=(P(*split, None, None), P(*split, None, None), P(), P()),
        check_vma=False,
    )
```

time: 1470 us -> 258 us (0.18)
  blocking collectives: 1340 us -> 132 us
  Pallas kernels: 0 us -> 26.5 us
  matrix products: 25.6 us -> 0.91 us
  waiting for transfers between devices: 37.1 us -> 13.4 us
  starting transfers between devices: 27.2 us -> 46 us
    psum x13 -> x0, blocking collectives: 1340 us -> none  [the longest x5 528 us: solve_local(): coarse_rhs = lax.psum(spread, ('sub', 'grp'))]
    all_to_all x0 -> x5, blocking collectives: none -> 132 us  [the longest x2 76.6 us: over_all(): lax.all_to_all(rows.reshape(n_red, part, LANE), RED, 0, 0, tiled=True)]
    unnamed x18 -> x122, local copies, waits for them, and re-layouts: 0.1 us -> 32.8 us
    pallas_call x0 -> x11, Pallas kernels: none -> 26.5 us  [the longest x1 7.11 us: on_device(): call(lambda *refs: combine_kernel(*refs, cols=cols, count=count), (shape(...]
    dot_general x38 -> x1, matrix products: 24.7 us -> 0.91 us  [on_device(): gram = jnp.dot(wide.T, (weights / total)[:, None] * wide, precision=HI)]
    ppermute x14 -> x12, waiting for transfers between devices: 37.1 us -> 13.4 us  [the longest x6 7.69 us: on_device(): nl = lax.ppermute(sl, along, behind)]
    gather x28 -> x0, local copies, waits for them, and re-layouts: 15.9 us -> none  [the longest x14 7.97 us: to_dual(): send = field[:face][inverse_map]]
    ppermute x14 -> x12, starting transfers between devices: 27.2 us -> 35.3 us  [the longest x6 27.3 us: on_device(): pr = lax.ppermute(sr, along, ahead)]
  transfers between devices with their start and end apart: 14 -> 13, of which waited for: 14 -> 9; matrix products, arithmetic and copies ran while one was open for 0% -> 0% of each run, Pallas kernels for 0% -> 3%
where the time goes in v1:
time: 258 us; the launch traced here: 256 us
  blocking collectives  132 us (51%)
  starting transfers between devices  46 us (18%)
  local copies, waits for them, and re-layouts  34.9 us (14%)
  Pallas kernels  26.5 us (10%)
  waiting for transfers between devices  13.4 us (5%)
    all_to_all x2, blocking collectives, over_all(): lax.all_to_all(rows.reshape(n_red, part, LANE), RED, 0, 0, tiled=True)  76.6 us
    all_to_all x2, blocking collectives, over_all(): lax.all_to_all(jnp.broadcast_to(mine[None], (n_z, part, LANE)), 'z', 0, 0...  40.4 us
    unnamed x122, local copies, waits for them, and re-layouts  32.8 us
    ppermute x6, starting transfers between devices, on_device(): pr = lax.ppermute(sr, along, ahead)  27.3 us
    all_to_all x1, blocking collectives, over_all(): lax.all_to_all(jnp.broadcast_to(mine[None], (n_red, part, LANE)), RED, 0,...  14.6 us
    all_to_all x1, starting transfers between devices, over_all(): lax.all_to_all(jnp.broadcast_to(mine[None], (n_red, part, LANE)), RED, 0,...  10.7 us
    ppermute x6, starting transfers between devices, on_device(): nl = lax.ppermute(sl, along, behind)  7.99 us
    ppermute x6, waiting for transfers between devices, on_device(): nl = lax.ppermute(sl, along, behind)  7.69 us
  transfers between devices with their start and end apart: 13, of which 9 were waited for; matrix products, arithmetic and copies ran while one was open for 0% of the time, Pallas kernels for 3%

profile of v1, /device:TPU:1, one launch (start us, length us, event | category | flops | bytes accessed | tf_op | source)
XLA Modules:
  0.0 255.9 jit_solution(1112057495883740749)
XLA Ops:
  1.5 1.1 copy.25
  2.7 1.6 copy-done.4
  5.7 1.2 shard_map.120
  6.9 1.3 collective-permute-start
  8.2 5.0 %collective-permute-start.1 = (f32[48,512]{1,0:T(8,128)S(1)}, f32[48,512]{1,0:T(8,128)S(1)}, u32[]{:S(2)}, u32[]{:S(2)}) collective-permute-start(f32[48,512]{1,0:T(8,128)S(1)} %get-tuple-element.39.refs_1_.refs_6_), channel_id=1, source_target_pairs={{0,8},{8,16},{16,24},{24,32},{32,40},{40,48},{48,56},{56,64},{64,7... | collective-permute-start | bytes 294920 | tf_op jit(solution)/shard_map/ppermute | solution.py:419
  13.3 5.3 %shard_map.121 = (bf16[1024,1024]{1,0:T(8,128)(2,1)S(1)}, bf16[1024,1024]{1,0:T(8,128)(2,1)S(1)}, bf16[1024,256]{1,0:T(8,128)(2,1)S(1)}, f32[1,1024]{1,0:T(1,128)S(1)}) custom-call(bf16[1024,1024]{1,0:T(8,128)(2,1)} %bitcast.25, bf16[1024,1024]{1,0:T(8,128)(2,1)} %bitcast.40, bf16[1024,256]{1,0:T(8,128)(2,1)S(1)} %bitcast.27, ...), custom_call_target="tpu_custom_call" | custom-call | tf_op jit(solution)/shard_map/pallas_call | solution.py:403
  20.0 1.3 collective-permute-start.2
  21.3 4.2 %collective-permute-start.3 = (f32[64,512]{1,0:T(8,128)S(1)}, f32[64,512]{1,0:T(8,128)S(1)}, u32[]{:S(2)}, u32[]{:S(2)}) collective-permute-start(f32[64,512]{1,0:T(8,128)S(1)} %get-tuple-element.43.refs_1_.refs_5_.refs_9_), channel_id=1, source_target_pairs={{0,8},{8,16},{16,24},{24,32},{32,40},{40,48},{48,56},{56,64},{64,7... | collective-permute-start | bytes 393224 | tf_op jit(solution)/shard_map/ppermute | solution.py:419
  25.9 1.5 collective-permute-done.3.refs_3_
  27.9 1.4 collective-permute-start.4
  29.4 4.4 %collective-permute-start.5 = (f32[80,512]{1,0:T(8,128)S(1)}, f32[80,512]{1,0:T(8,128)S(1)}, u32[]{:S(2)}, u32[]{:S(2)}) collective-permute-start(f32[80,512]{1,0:T(8,128)S(1)} %get-tuple-element.47.refs_1_.refs_8_.refs_12_), channel_id=1, source_target_pairs={{0,8},{8,16},{16,24},{24,32},{32,40},{40,48},{48,56},{56,64},{64,7... | collective-permute-start | bytes 491528 | tf_op jit(solution)/shard_map/ppermute | solution.py:419
  34.7 1.4 collective-permute-done.5.refs_3_
  36.7 3.7 %shard_map.125 = f32[2048,128]{1,0:T(8,128)S(1)} custom-call(f32[48,512]{1,0:T(8,128)S(1)} %copy-done.33, f32[32,8]{1,0:T(8,128)S(1)} %copy-done.54, f32[256,256]{1,0:T(8,128)S(1)} %convolution_bitcast_fusion.refs_2_, f32[56,1024]{1,0:T(8,128)S(1)} %get-tuple-element.41.refs_3_.refs_7_, f32[64,512]{1,0:T(8,128)S(1)} %get-tuple-element.42.refs_0_.refs_4_.refs_8_, ...), custom_call_target="tpu_custom_call" | custom-call | tf_op jit(solution)/shard_map/pallas_call | solution.py:432
  40.4 43.5 %all_to_all.30 = f32[32,64,128]{2,1,0:T(8,128)} all-to-all(f32[32,64,128]{2,1,0:T(8,128)S(1)} %bitcast.28), channel_id=1, replica_groups=mesh['y'=4,'z'=16,'x'=4,'c'=2] {'y','x','c'}, dimensions={0} | all-to-all | bytes 2097152 | tf_op jit(solution)/shard_map/all_to_all | solution.py:357
  84.0 1.3 reduce_sum.36
  85.3 25.4 %all_to_all.31 = f32[16,64,128]{2,1,0:T(8,128)S(1)} all-to-all(f32[16,64,128]{2,1,0:T(8,128)S(1)} %broadcast_in_dim.25), channel_id=1, replica_groups=mesh['y'=4,'z'=16,'x'=4,'c'=2] {'z'}, dimensions={0} | all-to-all | bytes 1048576 | tf_op jit(solution)/shard_map/all_to_all | solution.py:359
  110.7 1.1 broadcast_in_dim.26
  111.8 10.7 %all-to-all-start.2 = ((f32[32,64,128]{2,1,0:T(8,128)}), f32[32,64,128]{2,1,0:T(8,128)S(1)}, u32[]{:S(2)}, u32[]{:S(2)}) async-start(f32[32,64,128]{2,1,0:T(8,128)} %broadcast_in_dim.26), calls=%async_computation.2 | async-start | bytes 2097152 | tf_op jit(solution)/shard_map/all_to_all | solution.py:361
  122.6 1.4 collective-permute-start.6
  124.0 4.0 %collective-permute-start.7 = (f32[96,512]{1,0:T(8,128)S(1)}, f32[96,512]{1,0:T(8,128)S(1)}, u32[]{:S(2)}, u32[]{:S(2)}) collective-permute-start(f32[96,512]{1,0:T(8,128)S(1)} %get-tuple-element.50.refs_11_.refs_1_.refs_15_), channel_id=1, source_target_pairs={{0,8},{8,16},{16,24},{24,32},{32,40},{40,48},{48,56},{56,64},{64,7... | collective-permute-start | bytes 589832 | tf_op jit(solution)/shard_map/ppermute | solution.py:419
  128.0 2.7 %collective-permute-done.6.refs_2_ = f32[96,512]{1,0:T(8,128)S(1)} collective-permute-done((f32[96,512]{1,0:T(8,128)S(1)}, f32[96,512]{1,0:T(8,128)S(1)}, u32[]{:S(2)}, u32[]{:S(2)}) %collective-permute-start.6) | collective-permute-done | bytes 196640 | tf_op jit(solution)/shard_map/ppermute | solution.py:418
  133.8 1.3 collective-permute-start.8
  135.1 4.9 %collective-permute-start.9 = (f32[112,512]{1,0:T(8,128)S(1)}, f32[112,512]{1,0:T(8,128)S(1)}, u32[]{:S(2)}, u32[]{:S(2)}) collective-permute-start(f32[112,512]{1,0:T(8,128)S(1)} %get-tuple-element.52.refs_1_.refs_18_), channel_id=1, source_target_pairs={{0,8},{8,16},{16,24},{24,32},{32,40},{40,48},{48,56},{56,64},{64,7... | collective-permute-start | bytes 688136 | tf_op jit(solution)/shard_map/ppermute | solution.py:419
  140.0 2.3 collective-permute-done.8.refs_2_
  144.7 1.3 collective-permute-start.10
  146.0 4.8 %collective-permute-start.11 = (f32[128,512]{1,0:T(8,128)S(1)}, f32[128,512]{1,0:T(8,128)S(1)}, u32[]{:S(2)}, u32[]{:S(2)}) collective-permute-start(f32[128,512]{1,0:T(8,128)S(1)} %get-tuple-element.54.refs_1_.refs_21_), channel_id=1, source_target_pairs={{0,8},{8,16},{16,24},{24,32},{32,40},{40,48},{48,56},{56,64},{64,7... | collective-permute-start | bytes 786440 | tf_op jit(solution)/shard_map/ppermute | solution.py:419
  150.8 2.3 collective-permute-done.10.refs_2_
  153.1 1.0 collective-permute-done.11.refs_3_
  157.1 1.0 copy-done.2
  158.2 0.9 copy-done.11
  160.0 1.0 copy-done.15
  161.0 1.0 copy-done.17
  163.8 0.9 copy-done.23
  164.7 0.9 copy-done.25
  165.7 0.9 copy-done.27
  166.6 0.9 copy-done.29
  167.5 0.9 copy-done.31
  169.4 1.0 copy-done.39
  170.4 1.0 copy-done.41
  172.3 1.0 copy-done.45
  173.3 1.0 copy-done.47
  174.2 0.9 copy-done.48
  175.2 7.1 %shard_map.129 = (f32[512,128]{1,0:T(8,128)S(1)}, f32[128,1024]{1,0:T(8,128)S(1)}, f32[96,512]{1,0:T(8,128)S(1)}, f32[32,128]{1,0:T(8,128)S(1)}) custom-call(f32[2048,128]{1,0:T(8,128)} %bitcast.23, f32[256,256]{1,0:T(8,128)S(1)} %copy-done.48, f32[8,128]{1,0:T(8,128)S(1)} %slice.3.refs_2_, f32[1,1024]{1,0:T(1,128)S(1)} %get-tuple-element.56.refs_3_, ...), custom_call_target="tpu_custom_call" | custom-call | tf_op jit(solution)/shard_map/pallas_call | solution.py:438
  184.4 33.1 %all_to_all.32 = f32[32,16,128]{2,1,0:T(8,128)S(1)} all-to-all(f32[32,16,128]{2,1,0:T(8,128)S(1)} %bitcast.33), channel_id=1, replica_groups=mesh['y'=4,'z'=16,'x'=4,'c'=2] {'y','x','c'}, dimensions={0} | all-to-all | bytes 524288 | tf_op jit(solution)/shard_map/all_to_all | solution.py:357
  217.5 15.0 %all_to_all.33 = f32[16,16,128]{2,1,0:T(8,128)S(1)} all-to-all(f32[16,16,128]{2,1,0:T(8,128)S(1)} %broadcast_in_dim.50), channel_id=1, replica_groups=mesh['y'=4,'z'=16,'x'=4,'c'=2] {'z'}, dimensions={0} | all-to-all | bytes 262144 | tf_op jit(solution)/shard_map/all_to_all | solution.py:359
  232.6 14.6 %all_to_all.34 = f32[32,16,128]{2,1,0:T(8,128)S(1)} all-to-all(f32[32,16,128]{2,1,0:T(8,128)S(1)} %broadcast_in_dim.51), channel_id=1, replica_groups=mesh['y'=4,'z'=16,'x'=4,'c'=2] {'y','x','c'}, dimensions={0} | all-to-all | bytes 524288 | tf_op jit(solution)/shard_map/all_to_all | solution.py:361
  247.2 0.9 copy-done.50
  248.1 5.6 %shard_map.130 = (f32[1024,32]{1,0:T(8,128)S(1)}, f32[512,32]{1,0:T(8,128)S(1)}, f32[256,32]{1,0:T(8,128)S(1)}, f32[32,32]{1,0:T(8,128)}) custom-call(f32[512,128]{1,0:T(8,128)S(1)} %bitcast.30, f32[2048,128]{1,0:T(8,128)S(1)} %bitcast.24, f32[32,128]{1,0:T(8,128)S(1)} %copy-done.56, f32[128,1024]{1,0:T(8,128)S(1)} %copy-done.37, f32[96,512]{1,0:T(8,128)S(1)} %copy-done.50, ...), custom_call_target="tpu_custom_call" | custom-call | tf_op jit(solution)/shard_map/pallas_call | solution.py:443
  (130 shorter events, 23.5 us)
Async XLA Ops:
  0.6 12.6 %copy-start.52 = (s32[1,1,512]{2,1,0:T(1,128)S(1)}, s32[1,1,512]{2,1,0:T(1,128)}, u32[]{:S(2)}) copy-start(s32[1,1,512]{2,1,0:T(1,128)} %param.14) | copy-start | bytes 6148
  0.6 12.6 %copy-start.57 = (f32[1,1,1024]{2,1,0:T(1,128)S(1)}, f32[1,1,1024]{2,1,0:T(1,128)}, u32[]{:S(2)}) copy-start(f32[1,1,1024]{2,1,0:T(1,128)} %param.17) | copy-start | bytes 12292
  0.7 12.6 %copy-start.5 = (bf16[1,1,1024,256]{3,2,1,0:T(8,128)(2,1)S(1)}, bf16[1,1,1024,256]{3,2,1,0:T(8,128)(2,1)}, u32[]{:S(2)}) copy-start(bf16[1,1,1024,256]{3,2,1,0:T(8,128)(2,1)} %param.16) | copy-start | bytes 1572868
  2.7 1.6 copy-start.4
  6.9 11.7 %copy-start.53 = (f32[32,8]{1,0:T(8,128)}, f32[32,8]{1,0:T(8,128)S(1)}, u32[]{:S(2)}) copy-start(f32[32,8]{1,0:T(8,128)S(1)} %get-tuple-element.38.refs_1_) | copy-start | bytes 3076
  6.9 12.6 %copy-start.32 = (f32[48,512]{1,0:T(8,128)}, f32[48,512]{1,0:T(8,128)S(1)}, u32[]{:S(2)}) copy-start(f32[48,512]{1,0:T(8,128)S(1)} %get-tuple-element.37.refs_0_.refs_5_) | copy-start | bytes 294916
  6.9 12.6 %copy-start.42 = (f32[48,512]{1,0:T(8,128)}, f32[48,512]{1,0:T(8,128)S(1)}, u32[]{:S(2)}) copy-start(f32[48,512]{1,0:T(8,128)S(1)} %get-tuple-element.39.refs_1_.refs_6_) | copy-start | bytes 294916
  6.9 12.5 %collective-permute-start = (f32[48,512]{1,0:T(8,128)S(1)}, f32[48,512]{1,0:T(8,128)S(1)}, u32[]{:S(2)}, u32[]{:S(2)}) collective-permute-start(f32[48,512]{1,0:T(8,128)S(1)} %get-tuple-element.37.refs_0_.refs_5_), channel_id=1, source_target_pairs={{8,0},{16,8},{24,16},{32,24},{40,32},{48,40},{56,48},{64,56},{72,6... | collective-permute-start | bytes 294920 | tf_op jit(solution)/shard_map/ppermute | solution.py:418
  8.2 11.2 %collective-permute-start.1 = (f32[48,512]{1,0:T(8,128)S(1)}, f32[48,512]{1,0:T(8,128)S(1)}, u32[]{:S(2)}, u32[]{:S(2)}) collective-permute-start(f32[48,512]{1,0:T(8,128)S(1)} %get-tuple-element.39.refs_1_.refs_6_), channel_id=1, source_target_pairs={{0,8},{8,16},{16,24},{24,32},{32,40},{40,48},{48,56},{56,64},{64,7... | collective-permute-start | bytes 294920 | tf_op jit(solution)/shard_map/ppermute | solution.py:419
  19.4 16.7 %copy-start = (bf16[1024,1024]{1,0:T(8,128)(2,1)}, bf16[1024,1024]{1,0:T(8,128)(2,1)S(1)}, u32[]{:S(2)}) copy-start(bf16[1024,1024]{1,0:T(8,128)(2,1)S(1)} %get-tuple-element.40.refs_5_) | copy-start | bytes 6291460
  19.4 16.7 %copy-start.8 = (f32[8,1024]{1,0:T(8,128)}, f32[8,1024]{1,0:T(8,128)S(1)}, u32[]{:S(2)}) copy-start(f32[8,1024]{1,0:T(8,128)S(1)} %broadcast_in_dim.24.refs_4_) | copy-start | bytes 98308
  20.0 16.7 %copy-start.18 = (f32[64,512]{1,0:T(8,128)}, f32[64,512]{1,0:T(8,128)S(1)}, u32[]{:S(2)}) copy-start(f32[64,512]{1,0:T(8,128)S(1)} %get-tuple-element.42.refs_0_.refs_4_.refs_8_) | copy-start | bytes 393220
  20.0 16.7 %copy-start.20 = (f32[64,512]{1,0:T(8,128)}, f32[64,512]{1,0:T(8,128)S(1)}, u32[]{:S(2)}) copy-start(f32[64,512]{1,0:T(8,128)S(1)} %get-tuple-element.43.refs_1_.refs_5_.refs_9_) | copy-start | bytes 393220
  20.0 16.7 %copy-start.26 = (f32[56,1024]{1,0:T(8,128)}, f32[56,1024]{1,0:T(8,128)S(1)}, u32[]{:S(2)}) copy-start(f32[56,1024]{1,0:T(8,128)S(1)} %get-tuple-element.41.refs_3_.refs_7_) | copy-start | bytes 688132
  20.0 5.9 %collective-permute-start.2 = (f32[64,512]{1,0:T(8,128)S(1)}, f32[64,512]{1,0:T(8,128)S(1)}, u32[]{:S(2)}, u32[]{:S(2)}) collective-permute-start(f32[64,512]{1,0:T(8,128)S(1)} %get-tuple-element.42.refs_0_.refs_4_.refs_8_), channel_id=1, source_target_pairs={{8,0},{16,8},{24,16},{32,24},{40,32},{48,40},{56,48},{64,56},{72,6... | collective-permute-start | bytes 393224 | tf_op jit(solution)/shard_map/ppermute | solution.py:418
  21.3 6.1 %collective-permute-start.3 = (f32[64,512]{1,0:T(8,128)S(1)}, f32[64,512]{1,0:T(8,128)S(1)}, u32[]{:S(2)}, u32[]{:S(2)}) collective-permute-start(f32[64,512]{1,0:T(8,128)S(1)} %get-tuple-element.43.refs_1_.refs_5_.refs_9_), channel_id=1, source_target_pairs={{0,8},{8,16},{16,24},{24,32},{32,40},{40,48},{48,56},{56,64},{64,7... | collective-permute-start | bytes 393224 | tf_op jit(solution)/shard_map/ppermute | solution.py:419
  27.9 12.5 %copy-start.10 = (f32[80,512]{1,0:T(8,128)}, f32[80,512]{1,0:T(8,128)S(1)}, u32[]{:S(2)}) copy-start(f32[80,512]{1,0:T(8,128)S(1)} %get-tuple-element.46.refs_0_.refs_7_.refs_11_) | copy-start | bytes 491524
  27.9 12.5 %copy-start.12 = (f32[80,512]{1,0:T(8,128)}, f32[80,512]{1,0:T(8,128)S(1)}, u32[]{:S(2)}) copy-start(f32[80,512]{1,0:T(8,128)S(1)} %get-tuple-element.47.refs_1_.refs_8_.refs_12_) | copy-start | bytes 491524
  27.9 12.5 %copy-start.16 = (f32[72,1024]{1,0:T(8,128)}, f32[72,1024]{1,0:T(8,128)S(1)}, u32[]{:S(2)}) copy-start(f32[72,1024]{1,0:T(8,128)S(1)} %get-tuple-element.45.refs_6_.refs_10_) | copy-start | bytes 884740
  27.9 8.8 %copy-start.33 = (f32[48,512]{1,0:T(8,128)S(1)}, f32[48,512]{1,0:T(8,128)}, u32[]{:S(2)}) copy-start(f32[48,512]{1,0:T(8,128)} %copy-done.32) | copy-start | bytes 294916
  27.9 8.8 %copy-start.54 = (f32[32,8]{1,0:T(8,128)S(1)}, f32[32,8]{1,0:T(8,128)}, u32[]{:S(2)}) copy-start(f32[32,8]{1,0:T(8,128)} %copy-done.53) | copy-start | bytes 3076
  27.9 6.8 %collective-permute-start.4 = (f32[80,512]{1,0:T(8,128)S(1)}, f32[80,512]{1,0:T(8,128)S(1)}, u32[]{:S(2)}, u32[]{:S(2)}) collective-permute-start(f32[80,512]{1,0:T(8,128)S(1)} %get-tuple-element.46.refs_0_.refs_7_.refs_11_), channel_id=1, source_target_pairs={{8,0},{16,8},{24,16},{32,24},{40,32},{48,40},{56,48},{64,56},{72,6... | collective-permute-start | bytes 491528 | tf_op jit(solution)/shard_map/ppermute | solution.py:418
  29.4 6.7 %collective-permute-start.5 = (f32[80,512]{1,0:T(8,128)S(1)}, f32[80,512]{1,0:T(8,128)S(1)}, u32[]{:S(2)}, u32[]{:S(2)}) collective-permute-start(f32[80,512]{1,0:T(8,128)S(1)} %get-tuple-element.47.refs_1_.refs_8_.refs_12_), channel_id=1, source_target_pairs={{0,8},{8,16},{16,24},{24,32},{32,40},{40,48},{48,56},{56,64},{64,7... | collective-permute-start | bytes 491528 | tf_op jit(solution)/shard_map/ppermute | solution.py:419
  36.7 47.3 %copy-start.14 = (f32[88,1024]{1,0:T(8,128)}, f32[88,1024]{1,0:T(8,128)S(1)}, u32[]{:S(2)}) copy-start(f32[88,1024]{1,0:T(8,128)S(1)} %get-tuple-element.48.refs_9_.refs_13_) | copy-start | bytes 1081348
  111.8 45.3 %all-to-all-start.2 = ((f32[32,64,128]{2,1,0:T(8,128)}), f32[32,64,128]{2,1,0:T(8,128)S(1)}, u32[]{:S(2)}, u32[]{:S(2)}) async-start(f32[32,64,128]{2,1,0:T(8,128)} %broadcast_in_dim.26), calls=%async_computation.2 | async-start | bytes 2097152 | tf_op jit(solution)/shard_map/all_to_all | solution.py:361
  122.6 20.7 %copy-start.1 = (bf16[1024,1024]{1,0:T(8,128)(2,1)S(1)}, bf16[1024,1024]{1,0:T(8,128)(2,1)}, u32[]{:S(2)}) copy-start(bf16[1024,1024]{1,0:T(8,128)(2,1)} %copy-done) | copy-start | bytes 6291460
  122.6 8.2 %collective-permute-start.6 = (f32[96,512]{1,0:T(8,128)S(1)}, f32[96,512]{1,0:T(8,128)S(1)}, u32[]{:S(2)}, u32[]{:S(2)}) collective-permute-start(f32[96,512]{1,0:T(8,128)S(1)} %get-tuple-element.49.refs_10_.refs_0_.refs_14_), channel_id=1, source_target_pairs={{8,0},{16,8},{24,16},{32,24},{40,32},{48,40},{56,48},{64,56},{72,6... | collective-permute-start | bytes 589832 | tf_op jit(solution)/shard_map/ppermute | solution.py:418
  124.0 7.6 %collective-permute-start.7 = (f32[96,512]{1,0:T(8,128)S(1)}, f32[96,512]{1,0:T(8,128)S(1)}, u32[]{:S(2)}, u32[]{:S(2)}) collective-permute-start(f32[96,512]{1,0:T(8,128)S(1)} %get-tuple-element.50.refs_11_.refs_1_.refs_15_), channel_id=1, source_target_pairs={{0,8},{8,16},{16,24},{24,32},{32,40},{40,48},{48,56},{56,64},{64,7... | collective-permute-start | bytes 589832 | tf_op jit(solution)/shard_map/ppermute | solution.py:419
  133.8 19.2 %copy-start.28 = (f32[112,512]{1,0:T(8,128)}, f32[112,512]{1,0:T(8,128)S(1)}, u32[]{:S(2)}) copy-start(f32[112,512]{1,0:T(8,128)S(1)} %get-tuple-element.51.refs_0_.refs_17_) | copy-start | bytes 688132
  133.8 21.1 %copy-start.30 = (f32[112,512]{1,0:T(8,128)}, f32[112,512]{1,0:T(8,128)S(1)}, u32[]{:S(2)}) copy-start(f32[112,512]{1,0:T(8,128)S(1)} %get-tuple-element.52.refs_1_.refs_18_) | copy-start | bytes 688132
  133.8 8.5 %collective-permute-start.8 = (f32[112,512]{1,0:T(8,128)S(1)}, f32[112,512]{1,0:T(8,128)S(1)}, u32[]{:S(2)}, u32[]{:S(2)}) collective-permute-start(f32[112,512]{1,0:T(8,128)S(1)} %get-tuple-element.51.refs_0_.refs_17_), channel_id=1, source_target_pairs={{8,0},{16,8},{24,16},{32,24},{40,32},{48,40},{56,48},{64,56},{72,6... | collective-permute-start | bytes 688136 | tf_op jit(solution)/shard_map/ppermute | solution.py:418
  135.1 8.1 %collective-permute-start.9 = (f32[112,512]{1,0:T(8,128)S(1)}, f32[112,512]{1,0:T(8,128)S(1)}, u32[]{:S(2)}, u32[]{:S(2)}) collective-permute-start(f32[112,512]{1,0:T(8,128)S(1)} %get-tuple-element.52.refs_1_.refs_18_), channel_id=1, source_target_pairs={{0,8},{8,16},{16,24},{24,32},{32,40},{40,48},{48,56},{56,64},{64,7... | collective-permute-start | bytes 688136 | tf_op jit(solution)/shard_map/ppermute | solution.py:419
  144.7 11.7 %copy-start.22 = (f32[128,512]{1,0:T(8,128)}, f32[128,512]{1,0:T(8,128)S(1)}, u32[]{:S(2)}) copy-start(f32[128,512]{1,0:T(8,128)S(1)} %get-tuple-element.53.refs_0_.refs_20_) | copy-start | bytes 786436
  144.7 11.7 %copy-start.24 = (f32[128,512]{1,0:T(8,128)}, f32[128,512]{1,0:T(8,128)S(1)}, u32[]{:S(2)}) copy-start(f32[128,512]{1,0:T(8,128)S(1)} %get-tuple-element.54.refs_1_.refs_21_) | copy-start | bytes 786436
  144.7 8.3 %collective-permute-start.10 = (f32[128,512]{1,0:T(8,128)S(1)}, f32[128,512]{1,0:T(8,128)S(1)}, u32[]{:S(2)}, u32[]{:S(2)}) collective-permute-start(f32[128,512]{1,0:T(8,128)S(1)} %get-tuple-element.53.refs_0_.refs_20_), channel_id=1, source_target_pairs={{8,0},{16,8},{24,16},{32,24},{40,32},{48,40},{56,48},{64,56},{72,6... | collective-permute-start | bytes 786440 | tf_op jit(solution)/shard_map/ppermute | solution.py:418
  146.0 8.0 %collective-permute-start.11 = (f32[128,512]{1,0:T(8,128)S(1)}, f32[128,512]{1,0:T(8,128)S(1)}, u32[]{:S(2)}, u32[]{:S(2)}) collective-permute-start(f32[128,512]{1,0:T(8,128)S(1)} %get-tuple-element.54.refs_1_.refs_21_), channel_id=1, source_target_pairs={{0,8},{8,16},{16,24},{24,32},{32,40},{40,48},{48,56},{56,64},{64,7... | collective-permute-start | bytes 786440 | tf_op jit(solution)/shard_map/ppermute | solution.py:419
  157.1 1.0 copy-start.2
  160.0 1.0 copy-start.15
  161.0 1.0 copy-start.17
  163.8 0.9 copy-start.23
  169.4 1.0 copy-start.39
  170.4 1.0 copy-start.41
  172.3 1.0 copy-start.45
  173.3 1.0 copy-start.47
  184.4 62.8 %copy-start.3 = (f32[32,64,128]{2,1,0:T(8,128)S(1)}, f32[32,64,128]{2,1,0:T(8,128)}, u32[]{:S(2)}) copy-start(f32[32,64,128]{2,1,0:T(8,128)} %copy-done.2) | copy-start | bytes 3145732
  184.4 62.8 %copy-start.7 = (bf16[1024,256]{1,0:T(8,128)(2,1)S(1)}, bf16[1024,256]{1,0:T(8,128)(2,1)}, u32[]{:S(2)}) copy-start(bf16[1024,256]{1,0:T(8,128)(2,1)} %copy-done.6) | copy-start | bytes 1572868
  184.4 62.8 %copy-start.37 = (f32[128,1024]{1,0:T(8,128)S(1)}, f32[128,1024]{1,0:T(8,128)}, u32[]{:S(2)}) copy-start(f32[128,1024]{1,0:T(8,128)} %copy-done.36) | copy-start | bytes 1572868
  184.4 62.8 %copy-start.56 = (f32[32,128]{1,0:T(8,128)S(1)}, f32[32,128]{1,0:T(8,128)}, u32[]{:S(2)}) copy-start(f32[32,128]{1,0:T(8,128)} %copy-done.55) | copy-start | bytes 49156
  (24 other events, 20.0 us)

commit v2 on v1

--- a/solution.py
+++ b/solution.py
@@ -33,7 +33,7 @@
         kernel,
         out_shape=outs,
         scratch_shapes=list(scratch),
-        compiler_params=pltpu.CompilerParams(vmem_limit_bytes=48 * 1024 * 1024),
+        compiler_params=pltpu.CompilerParams(vmem_limit_bytes=12 * 1024 * 1024),
     )
 
 
@@ -45,48 +45,67 @@
     return wide[:rows] + wide[rows:]
 
 
-def to_order(nm_col, face):
-    return (nm_col == lax.broadcasted_iota(jnp.int32, (face, face), 1)).astype(F32)
+def to_order(nm_row, face):
+    nm = jnp.transpose(jnp.broadcast_to(nm_row.astype(F32), (8, face)))[:, 0:1]
+    return (nm == lax.broadcasted_iota(jnp.int32, (face, face), 1).astype(F32)).astype(F32)
 
 
 def from_order(nm_row, face):
     return (nm_row == lax.broadcasted_iota(jnp.int32, (face, face), 0)).astype(F32)
 
 
-def start_kernel(inv_ref, load_ref, basis_ref, nm_ref, corner_ref, sl_ref, sr_ref, cl_ref):
-    face = nm_ref.shape[0]
-    cols = load_ref.shape[1]
+def start_kernel(inv_hbm, load_hbm, basis_hbm, nm_hbm, corner_hbm, sl_ref, sr_ref, cl_ref,
+                 inv_ref, load_ref, basis_ref, nm_ref, corner_ref, sems):
+    pairs = (
+        (nm_hbm, nm_ref), (load_hbm, load_ref), (basis_hbm, basis_ref), (corner_hbm, corner_ref),
+        (inv_hbm, inv_ref),
+    )
+    copies = [pltpu.make_async_copy(src, dst, sems.at[i]) for i, (src, dst) in enumerate(pairs)]
+    for copy in copies:
+        copy.start()
+    for copy in copies[:-1]:
+        copy.wait()
+    face = nm_ref.shape[1]
+    cols = load_ref.shape[0]
     corners = basis_ref.shape[0]
     rows = cols + corners
-    load = jnp.transpose(load_ref[...])
+    load = load_ref[...]
     basis = basis_ref[...]
     order = to_order(nm_ref[...], face)
-    wide = split_dot(load, inv_ref[...])
-    left = nn(jnp.concatenate([wide[:, :face], basis[:, :face]], axis=0), order)
-    sl_ref[0:rows, :] = left
-    sr_ref[0:cols, :] = wide[:, face:]
-    sr_ref[cols:rows, :] = basis[:, face:]
+    cl_ref[...] = nt(load, basis)
     for ref in (sl_ref, sr_ref):
         ref[rows : rows + 8, :] = jnp.zeros((8, face), F32)
         ref[rows : rows + 1, 0:corners] = corner_ref[...].astype(F32)
-    cl_ref[...] = nt(load, basis)
-
-
-def order_kernel(inv_ref, schur_ref, prev_ref, nm_col_ref, nm_row_ref, mass_ref,
-                 inv_out, schur_out, prev_out, mass_out, *, total):
-    face = nm_col_ref.shape[0]
-    order32 = to_order(nm_col_ref[...], face)
-    order = order32.astype(BF16)
-    back = from_order(nm_row_ref[...], face).astype(BF16)
-    for src, dst in ((inv_ref, inv_out), (schur_ref, schur_out)):
-        dst[:, face:] = src[:, face:]
-        dst[:, :face] = jnp.dot(src[:, :face], order, preferred_element_type=F32).astype(BF16)
-        dst[:face, :] = jnp.dot(back, dst[:face, :], preferred_element_type=F32).astype(BF16)
+    sr_ref[cols:rows, :] = basis[:, face:]
+    copies[-1].wait()
+    wide = split_dot(load, inv_ref[...])
+    sr_ref[0:cols, :] = wide[:, face:]
+    sl_ref[0:rows, :] = nn(jnp.concatenate([wide[:, :face], basis[:, :face]], axis=0), order)
+
+
+def matrix_kernel(src, nm_ref, dst):
+    face = nm_ref.shape[1]
+    order = to_order(nm_ref[...], face).astype(BF16)
+    back = from_order(nm_ref[...], face).astype(BF16)
+    dst[:, face:] = src[:, face:]
+    dst[:, :face] = jnp.dot(src[:, :face], order, preferred_element_type=F32).astype(BF16)
+    dst[:face, :] = jnp.dot(back, dst[:face, :], preferred_element_type=F32).astype(BF16)
+
+
+def basis_kernel(prev_ref, nm_ref, mass_ref, prev_out, mass_out, gram_out, *, total):
+    face = nm_ref.shape[1]
+    back = from_order(nm_ref[...], face).astype(BF16)
     prev_out[face:, :] = prev_ref[face:, :]
     prev_out[:face, :] = jnp.dot(back, prev_ref[:face, :], preferred_element_type=F32).astype(BF16)
     mass = mass_ref[...] / total
     mass_out[:, face:] = mass[:, face:]
-    mass_out[:, :face] = nn(jnp.broadcast_to(mass[:, :face], (8, face)), order32)[0:1]
+    left = jnp.broadcast_to(mass[:, :face], (8, face))
+    mass_out[:, :face] = nn(left, to_order(nm_ref[...], face))[0:1]
+    column = jnp.transpose(jnp.broadcast_to(mass, (8, mass.shape[1])))[:, 0:1]
+    wide = prev_ref[...].astype(F32)
+    gram_out[...] = lax.dot_general(
+        wide * column, wide, (((0,), (0,)), ((), ())), precision=HI, preferred_element_type=F32
+    )
 
 
 def step_kernel(sl_ref, sr_ref, nl_ref, pr_ref, mask_ref, mat_ref, t_ref, ol_ref, or_ref,
@@ -129,33 +148,55 @@
     return (ids == dof).astype(F32)
 
 
-def pack(ref, at, matrix):
-    half = matrix.shape[0] // 2
-    ref[at : at + half, :] = matrix[:half, :half]
+def lower(half):
+    row = lax.broadcasted_iota(jnp.int32, (half, half), 0)
+    col = lax.broadcasted_iota(jnp.int32, (half, half), 1)
+    return row, col
+
+
+def pack(ref, k, matrix, diagonals):
+    half = LANE
+    at = 2 * half * k
+    row, col = lower(half)
+    last = matrix[half:, half:]
+    ref[at : at + half, :] = jnp.where(row >= col, matrix[:half, :half], last)
     ref[at + half : at + 2 * half, :] = matrix[half:, :half]
-    ref[at + 2 * half : at + 3 * half, :] = matrix[half:, half:]
-
-
-def unpack(ref, at):
+    ref[diagonals + k : diagonals + k + 1, :] = jnp.sum(
+        jnp.where(row == col, last, 0.0), axis=0, keepdims=True
+    )
+
+
+def unpack(ref, k, diagonals):
     half = LANE
-    a = ref[at : at + half, :]
-    b = ref[at + half : at + 2 * half, :]
-    c = ref[at + 2 * half : at + 3 * half, :]
+    at = 2 * half * k
+    row, col = lower(half)
+    shared = ref[at : at + half, :]
+    flipped = jnp.transpose(shared)
+    cross = ref[at + half : at + 2 * half, :]
+    first = jnp.where(row >= col, shared, flipped)
+    last = jnp.where(row < col, shared, flipped)
+    last = jnp.where(row == col, ref[diagonals + k : diagonals + k + 1, :], last)
     return jnp.concatenate(
-        [jnp.concatenate([a, jnp.transpose(b)], axis=1), jnp.concatenate([b, c], axis=1)], axis=0
+        [
+            jnp.concatenate([first, jnp.transpose(cross)], axis=1),
+            jnp.concatenate([cross, last], axis=1),
+        ],
+        axis=0,
     )
 
 
 def moment_kernel(sl0_ref, cl_ref, gram_ref, *refs, cols, count):
     out = refs[-1]
     half = count // 2
-    tri = 3 * half
 
     def put(at, block):
         out[at : at + cols, :] = block[:, :half]
         out[at + cols : at + 2 * cols, :] = block[:, half:]
 
-    base = 4 * tri
+    base = 8 * half
+    at = base + 8 * cols
+    diagonals = at + cols
+    out[at:, :] = jnp.zeros((out.shape[0] - at, LANE), F32)
     own = sl0_ref.shape[0] - cols - 8
     put(base, nt(cl_ref[...], one_hot(sl0_ref[cols + own : cols + own + 1, 0:own], count)))
     sums = []
@@ -167,16 +208,14 @@
         spot = one_hot(l_ref[rows : rows + 1, 0:width], count)
         tl, tr = t_ref[cols:rows, :face], t_ref[cols:rows, face:]
         inner = nt(tl, l_ref[cols:rows, :]) + nt(tr, r_ref[cols:rows, :])
-        pack(out, k * tri, nt(nn(spot, inner), spot))
+        pack(out, k, nt(nn(spot, inner), spot), diagonals)
         cross = nt(l_ref[0:cols, :], tl) + nt(r_ref[0:cols, :], tr)
         put(base + 2 * cols * (k + 1), nt(cross, spot))
         sums.append(
             lane_sum(t_ref[0:cols, :face] * l_ref[0:cols, :])
             + lane_sum(t_ref[0:cols, face:] * r_ref[0:cols, :])
         )
-    pack(out, 3 * tri, gram_ref[...])
-    at = base + 8 * cols
-    out[at:, :] = jnp.zeros((out.shape[0] - at, LANE), F32)
+    pack(out, 3, gram_ref[...], diagonals)
     lane = lax.broadcasted_iota(jnp.int32, (cols, LANE), 1)
     block = jnp.zeros((cols, LANE), F32)
     for k in range(3):
@@ -184,10 +223,10 @@
     out[at : at + cols, :] = block
 
 
-def combine_kernel(sums_ref, coarse_ref, ids_ref, mass_ref, prev_ref, *refs, cols, count):
+def combine_kernel(sums_ref, coarse_ref, mass_ref, prev_ref, *refs, cols, count):
     half = count // 2
-    tri = 3 * half
-    base = 4 * tri
+    base = 8 * half
+    diagonals = base + 9 * cols
     sl0, sr0 = refs[0:2]
     level = [None] + [refs[2 + 3 * k : 5 + 3 * k] for k in range(LEVELS)]
     out_ref, field_ref, dual_ref, scal_ref = refs[2 + 3 * LEVELS :]
@@ -196,7 +235,7 @@
     def get(at):
         return jnp.concatenate([sums_ref[at : at + cols, :], sums_ref[at + cols : at + 2 * cols, :]], axis=1)
 
-    m0, m1, m2 = (unpack(sums_ref, k * tri) for k in range(3))
+    m0, m1, m2 = (unpack(sums_ref, k, diagonals) for k in range(3))
     coarse = coarse_ref[...]
     c_load, w0x, w1x, w2x = (get(base + 2 * cols * k) for k in range(4))
     at = base + 8 * cols
@@ -220,7 +259,8 @@
         + be1 * m0g1
     )
     gm = nn(cm, coarse)
-    spot = one_hot(ids_ref[0:1, :], count)
+    last = level[LEVELS][1]
+    spot = one_hot(last[last.shape[0] - 8 : last.shape[0] - 7, 0:LANE], count)
     local = nn(jnp.concatenate([g0, g1, gz1, gm], axis=0), spot)
 
     def coef(k, n):
@@ -293,7 +333,6 @@
 def final_kernel(sums_ref, early_ref, scal_ref, field_ref, dual_ref, prev_ref, nm_ref,
                  block_ref, multi_ref, coef_ref, factor_ref, *, cols, count):
     half = count // 2
-    tri = 3 * half
     face = dual_ref.shape[1]
     at = 12 * cols
     r1z1, r1m, q1z1, q1m, r1p1, p1q1, z1w1, mw1, mm = (
@@ -310,7 +349,7 @@
     along = al1 + al2 * be2
     parts = (al0 + along * be1, along + al2, -al1 * al2)
     multi = sum(y * dual_ref[i * cols : (i + 1) * cols, :] for i, y in enumerate(parts))
-    multi_ref[...] = jnp.transpose(multi)
+    multi_ref[...] = multi
     weights = [jnp.ones((cols, 1), F32)] + [-y for y in parts]
     primal = sum(y * field_ref[i * cols : (i + 1) * cols, :] for i, y in enumerate(weights))
     g1 = sum(
@@ -330,9 +369,9 @@
         for j in range(4):
             tile = sums_ref[(8 + i) * cols : (9 + i) * cols, j * cols : (j + 1) * cols]
             gram = gram + weights[i] * tile * across[j]
-    basis = unpack(early_ref, 3 * tri)
+    basis = unpack(early_ref, 3, 8 * half + 9 * cols)
     c = 2.0 * g1 - nn(g1, basis)
-    coef_ref[...] = jnp.transpose(c)
+    coef_ref[...] = c
     gram = gram - nt(c, g1) - nt(g1, c) + nt(nn(c, basis), c)
     gram = 0.5 * (gram + jnp.transpose(gram))
     final = primal - nt(c, prev_ref[...].astype(F32))
@@ -348,18 +387,28 @@
     factor_ref[...] = jnp.transpose(jnp.where(row <= col, work[:, :cols], 0.0))
     solved = nn(work[:, cols:], final)
     left = nn(solved[:, :face], from_order(nm_ref[...], face))
-    block_ref[:face, :] = jnp.transpose(left)
-    block_ref[face:, :] = jnp.transpose(solved[:, face:])
+    block_ref[:, :face] = left
+    block_ref[:, face:] = solved[:, face:]
+
+
+def sum_kernel(parts_ref, out_ref):
+    total = jnp.sum(parts_ref[...], axis=0)
+    for i in range(out_ref.shape[0]):
+        out_ref[i] = total
+
+
+def swap(parts, axes):
+    return lax.all_to_all(parts, axes, 0, 0, tiled=True)
+
+
+def summed(parts, copies):
+    return call(sum_kernel, jax.ShapeDtypeStruct((copies,) + parts.shape[1:], F32))(parts)
 
 
 def over_all(rows, n_red, n_z):
-    part = rows.shape[0] // n_red
-    mine = lax.all_to_all(rows.reshape(n_red, part, LANE), RED, 0, 0, tiled=True)
-    mine = jnp.sum(mine, axis=0)
-    peers = lax.all_to_all(jnp.broadcast_to(mine[None], (n_z, part, LANE)), "z", 0, 0, tiled=True)
-    mine = jnp.sum(peers, axis=0)
-    full = lax.all_to_all(jnp.broadcast_to(mine[None], (n_red, part, LANE)), RED, 0, 0, tiled=True)
-    return full.reshape(n_red * part, LANE)
+    parts = swap(rows.reshape(n_red, rows.shape[0] // n_red, LANE), RED)
+    parts = swap(summed(parts, n_z), "z")
+    return swap(summed(parts, n_red), RED).reshape(rows.shape)
 
 
 def up(count, unit):
@@ -382,14 +431,14 @@
                   load, previous, mass):
         inverse_block, schur_block, basis = schur_inverse[0, 0], schur[0, 0], coarse_basis[0, 0]
         corners, nm = corner_index[0, 0], neighbor_map[0, 0]
-        rhs, earlier, weights = load[0, 0], previous[0, 0], mass[0, 0]
-        rows, cols = rhs.shape
+        rhs, earlier, weights = load[0, 0].T, previous[0, 0], mass[0, 0]
+        cols, rows = rhs.shape
         face = nm.shape[0]
         count = coarse_inverse.shape[0]
         total = rows * n_sub * n_grp
         own = corners.shape[0]
         position = lax.axis_index(along)
-        nm_row, nm_col = nm[None, :], nm[:, None]
+        nm_row = nm[None, :]
         side = jnp.arange(2 * face) < face
         mask = jnp.where(side, position > 0, position < n_sub - 1).astype(F32)[None, :]
         mask = jnp.broadcast_to(mask, (8, 2 * face))
@@ -397,54 +446,80 @@
         def shape(*dims):
             return jax.ShapeDtypeStruct(dims, F32)
 
-        sl, sr, cl = call(
-            start_kernel, (shape(cols + own + 8, face), shape(cols + own + 8, face), shape(cols, own))
-        )(inverse_block, rhs, basis, nm_col, corners[None, :])
-        inv_p, schur_p, prev_p, mass_p = call(
-            lambda *refs: order_kernel(*refs, total=total),
-            (
-                jax.ShapeDtypeStruct((rows, rows), BF16),
-                jax.ShapeDtypeStruct((rows, rows), BF16),
-                jax.ShapeDtypeStruct(earlier.shape, BF16),
-                shape(1, rows),
-            ),
-        )(inverse_block, schur_block, earlier, nm_col, nm_row, weights[None, :])
-        wide = earlier.astype(F32)
-        gram = jnp.dot(wide.T, (weights / total)[:, None] * wide, precision=HI)
-
-        chain = [sl, sr]
-        width = own
-        for k in range(1, LEVELS + 1):
-            nl = lax.ppermute(sl, along, behind)
-            pr = lax.ppermute(sr, along, ahead)
-            odd = k % 2 == 1
+        half = shape(cols + own + 8, face)
+        sl, sr, cl = pl.pallas_call(
+            start_kernel,
+            out_shape=(half, half, shape(cols, own)),
+            in_specs=[pl.BlockSpec(memory_space=pl.ANY)] * 5,
+            scratch_shapes=[
+                pltpu.VMEM((rows, rows), BF16),
+                pltpu.VMEM((cols, rows), F32),
+                pltpu.VMEM((own, rows), F32),
+                pltpu.VMEM((1, face), jnp.int32),
+                pltpu.VMEM((1, own), jnp.int32),
+                pltpu.SemaphoreType.DMA((5,)),
+            ],
+            compiler_params=pltpu.CompilerParams(vmem_limit_bytes=60 * 1024 * 1024),
+        )(inverse_block, rhs, basis, nm_row, corners[None, :])
+        square = jax.ShapeDtypeStruct((rows, rows), BF16)
+
+        def exchange(sl, sr):
+            return lax.ppermute(sl, along, behind), lax.ppermute(sr, along, ahead)
+
+        def step(k, sl, sr, near, mat):
+            width = own + 16 * (k - 1)
             out = cols + width + 16
-            t, sl, sr = call(
-                lambda *refs, width=width, odd=odd: step_kernel(
-                    *refs, cols=cols, width=width, scale=0.25 if odd else 1.0
+            return call(
+                lambda *refs: step_kernel(
+                    *refs, cols=cols, width=width, scale=0.25 if k % 2 == 1 else 1.0
                 ),
                 (shape(out, 2 * face), shape(out + 8, face), shape(out + 8, face)),
-            )(sl, sr, nl, pr, mask, schur_p if odd else inv_p)
-            chain += [t, sl, sr]
-            width += 16
-            if k == 3:
-                size = up(6 * count + 9 * cols, 8 * n_red)
-                first = call(
-                    lambda *refs: moment_kernel(*refs, cols=cols, count=count), shape(size, LANE)
-                )(chain[0], cl, gram, *chain[2:11])
-                first = over_all(first, n_red, n_z)
-        ids = sl[cols + width : cols + width + 8, :LANE]
+            )(sl, sr, *near, mask, mat)
+
+        chain = [sl, sr]
+        near = exchange(sl, sr)
+        schur_p = call(matrix_kernel, square)(schur_block, nm_row)
+        t, sl, sr = step(1, sl, sr, near, schur_p)
+        chain += [t, sl, sr]
+        near = exchange(sl, sr)
+        inv_p = call(matrix_kernel, square)(inverse_block, nm_row)
+        t, sl, sr = step(2, sl, sr, near, inv_p)
+        chain += [t, sl, sr]
+        near = exchange(sl, sr)
+        prev_p, mass_p, gram = call(
+            lambda *refs: basis_kernel(*refs, total=total),
+            (jax.ShapeDtypeStruct(earlier.shape, BF16), shape(1, rows), shape(count, count)),
+        )(earlier, nm_row, weights[None, :])
+        t, sl, sr = step(3, sl, sr, near, schur_p)
+        chain += [t, sl, sr]
+        near = exchange(sl, sr)
+        size = up(4 * count + 9 * cols + 8, 8 * n_red)
+        first = call(
+            lambda *refs: moment_kernel(*refs, cols=cols, count=count), shape(size, LANE)
+        )(chain[0], cl, gram, *chain[2:11])
+        t, sl, sr = step(4, sl, sr, near, inv_p)
+        chain += [t, sl, sr]
+        first, sl, sr = lax.optimization_barrier((first, sl, sr))
+        near = exchange(sl, sr)
+        t, sl, sr = step(5, sl, sr, near, schur_p)
+        chain += [t, sl, sr]
+        near = exchange(sl, sr)
+        t, sl, sr = step(6, sl, sr, near, inv_p)
+        chain += [t, sl, sr]
+        first, sl, sr = lax.optimization_barrier((first, sl, sr))
+        chain[-2:] = [sl, sr]
+        first = over_all(first, n_red, n_z)
         size = up(13 * cols, 8 * n_red)
         second, field, dual, scal = call(
             lambda *refs: combine_kernel(*refs, cols=cols, count=count),
             (shape(size, LANE), shape(4 * cols, rows), shape(3 * cols, face), shape(cols, LANE)),
-        )(first, coarse_inverse, ids, mass_p, prev_p, *chain)
+        )(first, coarse_inverse, mass_p, prev_p, *chain)
         second = over_all(second, n_red, n_z)
         block, multi, coefficients, factor = call(
             lambda *refs: final_kernel(*refs, cols=cols, count=count),
-            (shape(rows, cols), shape(face, cols), shape(count, cols), shape(cols, cols)),
+            (shape(cols, rows), shape(cols, face), shape(cols, count), shape(cols, cols)),
         )(second, first, scal, field, dual, prev_p, nm_row)
-        return block[None, None], multi[None, None], coefficients, factor
+        return block.T[None, None], multi.T[None, None], coefficients.T, factor
 
     split = (along, ("x", "c"))
     return jax.shard_map(

time: 258 us -> 214 us (0.83)
  local copies, waits for them, and re-layouts: 34.9 us -> 0.05 us
  starting transfers between devices: 46 us -> 37.7 us
  blocking collectives: 132 us -> 136 us
    unnamed x122 -> x18, local copies, waits for them, and re-layouts: 32.8 us -> 0.05 us
    all_to_all x1 -> x0, starting transfers between devices: 10.7 us -> none  [over_all(): lax.all_to_all(jnp.broadcast_to(mine[None], (n_red, part, LANE)), RED, 0,...]
    all_to_all x5 -> x6, blocking collectives: 132 us -> 136 us  [swap(): return lax.all_to_all(parts, axes, 0, 0, tiled=True)]
    pallas_call x9 -> x15, Pallas kernels: 15.8 us -> 18.3 us  [the longest x1 5.78 us: on_device(): call(lambda *refs: final_kernel(*refs, cols=cols, count=count), (shape(co...]
  transfers between devices with their start and end apart: 13 -> 12, of which waited for: 9 -> 8; matrix products, arithmetic and copies ran while one was open for 0% -> 0% of each run, Pallas kernels for 3% -> 4%
where the time goes in v2:
time: 214 us
  blocking collectives  136 us (64%)
  starting transfers between devices  37.7 us (18%)
  Pallas kernels  27.5 us (13%)
  waiting for transfers between devices  11.7 us (5%)
    all_to_all x6, blocking collectives, swap(): return lax.all_to_all(parts, axes, 0, 0, tiled=True)  136 us
    ppermute x12, starting transfers between devices, exchange(): return (lax.ppermute(sl, along, behind), lax.ppermute(sr, along, ahead))  37.7 us
    ppermute x12, waiting for transfers between devices, exchange(): return (lax.ppermute(sl, along, behind), lax.ppermute(sr, along, ahead))  11.7 us
    pallas_call x1, Pallas kernels, on_device(): call(lambda *refs: final_kernel(*refs, cols=cols, count=count), (shape(co...  5.78 us
    pallas_call x1, Pallas kernels, on_device(): call(lambda *refs: combine_kernel(*refs, cols=cols, count=count), (shape(...  5.61 us
  transfers between devices with their start and end apart: 12, of which 8 were waited for; matrix products, arithmetic and copies ran while one was open for 0% of the time, Pallas kernels for 4%

profile of v2, /device:TPU:1, one launch (start us, length us, event | category | flops | bytes accessed | tf_op | source)
XLA Modules:
  0.0 213.6 jit_solution(49009248099115361)
XLA Ops:
  0.7 3.6 %shard_map.120 = (f32[48,512]{1,0:T(8,128)}, f32[48,512]{1,0:T(8,128)}, f32[32,8]{1,0:T(8,128)}) custom-call(bf16[1024,1024]{1,0:T(8,128)(2,1)} %bitcast.21, f32[32,1024]{1,0:T(8,128)} %bitcast.36, f32[8,1024]{1,0:T(8,128)} %bitcast.37, s32[1,512]{1,0:T(1,128)} %bitcast.30, s32[1,8]{1,0:T(1,128)} %bitcast.38), custom_call_target="tpu_custom_call" | custom-call | tf_op jit(solution)/shard_map/pallas_call | solution.py:450
  4.2 4.4 %collective-permute-start.1 = (f32[48,512]{1,0:T(8,128)}, f32[48,512]{1,0:T(8,128)S(1)}, u32[]{:S(2)}, u32[]{:S(2)}) collective-permute-start(f32[48,512]{1,0:T(8,128)} %get-tuple-element.45.refs_1_.refs_5_), channel_id=1, source_target_pairs={{0,8},{8,16},{16,24},{24,32},{32,40},{40,48},{48,56},{56,64},{64,7... | collective-permute-start | bytes 294920 | tf_op jit(solution)/shard_map/ppermute | solution.py:467
  8.6 1.3 collective-permute-start
  10.0 0.0 copy-start.2
  10.0 1.5 shard_map.122.refs_5_
  11.5 0.0 copy-start
  11.5 0.0 collective-permute-done.1.refs_3_
  11.5 2.9 %collective-permute-done.refs_2_ = f32[48,512]{1,0:T(8,128)S(1)} collective-permute-done((f32[48,512]{1,0:T(8,128)}, f32[48,512]{1,0:T(8,128)S(1)}, u32[]{:S(2)}, u32[]{:S(2)}) %collective-permute-start) | collective-permute-done | bytes 98336 | tf_op jit(solution)/shard_map/ppermute | solution.py:467
  14.4 0.5 shard_map.123
  14.9 1.3 collective-permute-start.2
  16.2 4.5 %collective-permute-start.3 = (f32[64,512]{1,0:T(8,128)S(1)}, f32[64,512]{1,0:T(8,128)S(1)}, u32[]{:S(2)}, u32[]{:S(2)}) collective-permute-start(f32[64,512]{1,0:T(8,128)S(1)} %get-tuple-element.48.refs_1_.refs_5_.refs_8_), channel_id=1, source_target_pairs={{0,8},{8,16},{16,24},{24,32},{32,40},{40,48},{48,56},{56,64},{64,7... | collective-permute-start | bytes 393224 | tf_op jit(solution)/shard_map/ppermute | solution.py:467
  20.7 1.5 shard_map.124.refs_5_
  22.2 0.0 copy-start.3
  22.2 0.0 copy-start.8
  22.2 0.4 collective-permute-done.3.refs_3_
  22.6 0.5 shard_map.125
  23.1 0.0 copy-start.7
  23.1 1.3 collective-permute-start.4
  24.4 5.1 %collective-permute-start.5 = (f32[80,512]{1,0:T(8,128)S(1)}, f32[80,512]{1,0:T(8,128)S(1)}, u32[]{:S(2)}, u32[]{:S(2)}) collective-permute-start(f32[80,512]{1,0:T(8,128)S(1)} %get-tuple-element.51.refs_1_.refs_8_.refs_11_), channel_id=1, source_target_pairs={{0,8},{8,16},{16,24},{24,32},{32,40},{40,48},{48,56},{56,64},{64,7... | collective-permute-start | bytes 491528 | tf_op jit(solution)/shard_map/ppermute | solution.py:467
  29.5 0.8 collective-permute-done.4.refs_2_
  30.2 1.5 collective-permute-done.5.refs_3_
  31.7 0.6 shard_map.126
  32.3 1.3 collective-permute-start.6
  33.6 5.2 %collective-permute-start.7 = (f32[96,512]{1,0:T(8,128)S(1)}, f32[96,512]{1,0:T(8,128)S(1)}, u32[]{:S(2)}, u32[]{:S(2)}) collective-permute-start(f32[96,512]{1,0:T(8,128)S(1)} %get-tuple-element.54.refs_11_.refs_1_.refs_14_), channel_id=1, source_target_pairs={{0,8},{8,16},{16,24},{24,32},{32,40},{40,48},{48,56},{56,64},{64,7... | collective-permute-start | bytes 589832 | tf_op jit(solution)/shard_map/ppermute | solution.py:467
  38.8 2.1 shard_map.121
  40.9 3.6 %shard_map.127 = f32[1536,128]{1,0:T(8,128)S(1)} custom-call(f32[48,512]{1,0:T(8,128)S(1)} %copy-done.2, f32[32,8]{1,0:T(8,128)S(1)} %copy-done.7, f32[256,256]{1,0:T(8,128)S(1)} %get-tuple-element.44.refs_2_, f32[56,1024]{1,0:T(8,128)S(1)} %get-tuple-element.46.refs_3_.refs_6_, f32[64,512]{1,0:T(8,128)S(1)} %get-tuple-element.47.refs_0_.refs_4_.refs_7_, ...), custom_call_target="tpu_custom_call" | custom-call | tf_op jit(solution)/shard_map/pallas_call | solution.py:497
  44.6 0.0 collective-permute-done.7.refs_3_
  44.6 0.6 shard_map.128
  45.2 1.3 collective-permute-start.8
  46.5 5.2 %collective-permute-start.9 = (f32[112,512]{1,0:T(8,128)S(1)}, f32[112,512]{1,0:T(8,128)S(1)}, u32[]{:S(2)}, u32[]{:S(2)}) collective-permute-start(f32[112,512]{1,0:T(8,128)S(1)} %get-tuple-element.59.refs_1_.refs_17_), channel_id=1, source_target_pairs={{0,8},{8,16},{16,24},{24,32},{32,40},{40,48},{48,56},{56,64},{64,7... | collective-permute-start | bytes 688136 | tf_op jit(solution)/shard_map/ppermute | solution.py:467
  51.7 1.5 collective-permute-done.8.refs_2_
  53.2 1.5 collective-permute-done.9.refs_3_
  54.7 0.7 shard_map.129
  55.4 1.3 collective-permute-start.10
  56.7 5.6 %collective-permute-start.11 = (f32[128,512]{1,0:T(8,128)S(1)}, f32[128,512]{1,0:T(8,128)S(1)}, u32[]{:S(2)}, u32[]{:S(2)}) collective-permute-start(f32[128,512]{1,0:T(8,128)S(1)} %get-tuple-element.61.refs_1_.refs_20_), channel_id=1, source_target_pairs={{0,8},{8,16},{16,24},{24,32},{32,40},{40,48},{48,56},{56,64},{64,7... | collective-permute-start | bytes 786440 | tf_op jit(solution)/shard_map/ppermute | solution.py:467
  62.3 1.8 collective-permute-done.10.refs_2_
  64.1 1.5 collective-permute-done.11.refs_3_
  65.6 0.8 shard_map.130
  66.4 44.6 %all_to_all.30.parts_ref = f32[32,48,128]{2,1,0:T(8,128)S(1)} all-to-all(f32[32,48,128]{2,1,0:T(8,128)S(1)} %bitcast.25), channel_id=1, replica_groups=mesh['y'=4,'z'=16,'x'=4,'c'=2] {'y','x','c'}, dimensions={0} | all-to-all | bytes 1572864 | tf_op jit(solution)/shard_map/all_to_all | solution.py:401
  111.0 0.1 shard_map.131
  111.0 20.9 %all_to_all.31.parts_ref = f32[16,48,128]{2,1,0:T(8,128)S(1)} all-to-all(f32[16,48,128]{2,1,0:T(8,128)S(1)} %shard_map.131), channel_id=1, replica_groups=mesh['y'=4,'z'=16,'x'=4,'c'=2] {'z'}, dimensions={0} | all-to-all | bytes 786432 | tf_op jit(solution)/shard_map/all_to_all | solution.py:401
  131.9 0.1 shard_map.132
  132.0 25.8 %all_to_all.32 = f32[32,48,128]{2,1,0:T(8,128)S(1)} all-to-all(f32[32,48,128]{2,1,0:T(8,128)S(1)} %shard_map.132), channel_id=1, replica_groups=mesh['y'=4,'z'=16,'x'=4,'c'=2] {'y','x','c'}, dimensions={0} | all-to-all | bytes 1572864 | tf_op jit(solution)/shard_map/all_to_all | solution.py:401
  157.8 5.6 %shard_map.133 = (f32[512,128]{1,0:T(8,128)S(1)}, f32[128,1024]{1,0:T(8,128)S(1)}, f32[96,512]{1,0:T(8,128)S(1)}, f32[32,128]{1,0:T(8,128)S(1)}) custom-call(f32[1536,128]{1,0:T(8,128)S(1)} %bitcast.23, f32[256,256]{1,0:T(8,128)S(1)} %copy-done.5, f32[1,1024]{1,0:T(1,128)S(1)} %get-tuple-element.65.refs_2_, ...), custom_call_target="tpu_custom_call" | custom-call | tf_op jit(solution)/shard_map/pallas_call | solution.py:513
  163.4 12.6 %all_to_all.33.parts_ref = f32[32,16,128]{2,1,0:T(8,128)S(1)} all-to-all(f32[32,16,128]{2,1,0:T(8,128)S(1)} %bitcast.29), channel_id=1, replica_groups=mesh['y'=4,'z'=16,'x'=4,'c'=2] {'y','x','c'}, dimensions={0} | all-to-all | bytes 524288 | tf_op jit(solution)/shard_map/all_to_all | solution.py:401
  176.0 16.6 %all_to_all.34.parts_ref = f32[16,16,128]{2,1,0:T(8,128)S(1)} all-to-all(f32[16,16,128]{2,1,0:T(8,128)S(1)} %shard_map.134), channel_id=1, replica_groups=mesh['y'=4,'z'=16,'x'=4,'c'=2] {'z'}, dimensions={0} | all-to-all | bytes 262144 | tf_op jit(solution)/shard_map/all_to_all | solution.py:401
  192.6 15.1 %all_to_all.35 = f32[32,16,128]{2,1,0:T(8,128)S(1)} all-to-all(f32[32,16,128]{2,1,0:T(8,128)S(1)} %shard_map.135), channel_id=1, replica_groups=mesh['y'=4,'z'=16,'x'=4,'c'=2] {'y','x','c'}, dimensions={0} | all-to-all | bytes 524288 | tf_op jit(solution)/shard_map/all_to_all | solution.py:401
  207.8 5.8 %shard_map.136 = (f32[32,1024]{1,0:T(8,128)}, f32[32,512]{1,0:T(8,128)}, f32[32,256]{1,0:T(8,128)}, f32[32,32]{1,0:T(8,128)}) custom-call(f32[512,128]{1,0:T(8,128)S(1)} %bitcast.27, f32[1536,128]{1,0:T(8,128)S(1)} %bitcast.24, f32[32,128]{1,0:T(8,128)S(1)} %get-tuple-element.73.refs_2_, f32[128,1024]{1,0:T(8,128)S(1)} %get-tuple-element.74.refs_3_, ...), custom_call_target="tpu_custom_call" | custom-call | tf_op jit(solution)/shard_map/pallas_call | solution.py:518
  (19 shorter events, 0.1 us)
Async XLA Ops:
  0.6 9.3 %copy-start.6 = (s32[1,1,512]{2,1,0:T(1,128)S(1)}, s32[1,1,512]{2,1,0:T(1,128)}, u32[]{:S(2)}) copy-start(s32[1,1,512]{2,1,0:T(1,128)} %param.14) | copy-start | bytes 6148
  0.6 9.3 %copy-start.1 = (bf16[1,1,1024,1024]{3,2,1,0:T(8,128)(2,1)S(1)}, bf16[1,1,1024,1024]{3,2,1,0:T(8,128)(2,1)}, u32[]{:S(2)}) copy-start(bf16[1,1,1024,1024]{3,2,1,0:T(8,128)(2,1)} %param.10) | copy-start | bytes 6291460
  4.2 7.3 %collective-permute-start.1 = (f32[48,512]{1,0:T(8,128)}, f32[48,512]{1,0:T(8,128)S(1)}, u32[]{:S(2)}, u32[]{:S(2)}) collective-permute-start(f32[48,512]{1,0:T(8,128)} %get-tuple-element.45.refs_1_.refs_5_), channel_id=1, source_target_pairs={{0,8},{8,16},{16,24},{24,32},{32,40},{40,48},{48,56},{56,64},{64,7... | collective-permute-start | bytes 294920 | tf_op jit(solution)/shard_map/ppermute | solution.py:467
  8.6 5.8 %collective-permute-start = (f32[48,512]{1,0:T(8,128)}, f32[48,512]{1,0:T(8,128)S(1)}, u32[]{:S(2)}, u32[]{:S(2)}) collective-permute-start(f32[48,512]{1,0:T(8,128)} %get-tuple-element.42.refs_0_.refs_4_), channel_id=1, source_target_pairs={{8,0},{16,8},{24,16},{32,24},{40,32},{48,40},{56,48},{64,56},{72,6... | collective-permute-start | bytes 294920 | tf_op jit(solution)/shard_map/ppermute | solution.py:467
  10.0 4.4 %copy-start.2 = (f32[48,512]{1,0:T(8,128)S(1)}, f32[48,512]{1,0:T(8,128)}, u32[]{:S(2)}) copy-start(f32[48,512]{1,0:T(8,128)} %get-tuple-element.42.refs_0_.refs_4_) | copy-start | bytes 294916
  10.0 4.4 %copy-start.4 = (f32[48,512]{1,0:T(8,128)S(1)}, f32[48,512]{1,0:T(8,128)}, u32[]{:S(2)}) copy-start(f32[48,512]{1,0:T(8,128)} %get-tuple-element.45.refs_1_.refs_5_) | copy-start | bytes 294916
  11.5 9.2 %copy-start = (bf16[1,1,1024,1024]{3,2,1,0:T(8,128)(2,1)S(1)}, bf16[1,1,1024,1024]{3,2,1,0:T(8,128)(2,1)}, u32[]{:S(2)}) copy-start(bf16[1,1,1024,1024]{3,2,1,0:T(8,128)(2,1)} %param.9) | copy-start | bytes 6291460
  14.9 7.3 %collective-permute-start.2 = (f32[64,512]{1,0:T(8,128)S(1)}, f32[64,512]{1,0:T(8,128)S(1)}, u32[]{:S(2)}, u32[]{:S(2)}) collective-permute-start(f32[64,512]{1,0:T(8,128)S(1)} %get-tuple-element.47.refs_0_.refs_4_.refs_7_), channel_id=1, source_target_pairs={{8,0},{16,8},{24,16},{32,24},{40,32},{48,40},{56,48},{64,56},{72,6... | collective-permute-start | bytes 393224 | tf_op jit(solution)/shard_map/ppermute | solution.py:467
  16.2 6.4 %collective-permute-start.3 = (f32[64,512]{1,0:T(8,128)S(1)}, f32[64,512]{1,0:T(8,128)S(1)}, u32[]{:S(2)}, u32[]{:S(2)}) collective-permute-start(f32[64,512]{1,0:T(8,128)S(1)} %get-tuple-element.48.refs_1_.refs_5_.refs_8_), channel_id=1, source_target_pairs={{0,8},{8,16},{16,24},{24,32},{32,40},{40,48},{48,56},{56,64},{64,7... | collective-permute-start | bytes 393224 | tf_op jit(solution)/shard_map/ppermute | solution.py:467
  22.2 16.6 %copy-start.3 = (bf16[1,1,1024,256]{3,2,1,0:T(8,128)(2,1)S(1)}, bf16[1,1,1024,256]{3,2,1,0:T(8,128)(2,1)}, u32[]{:S(2)}) copy-start(bf16[1,1,1024,256]{3,2,1,0:T(8,128)(2,1)} %param.16) | copy-start | bytes 1572868
  22.2 16.6 %copy-start.8 = (f32[1,1,1024]{2,1,0:T(1,128)S(1)}, f32[1,1,1024]{2,1,0:T(1,128)}, u32[]{:S(2)}) copy-start(f32[1,1,1024]{2,1,0:T(1,128)} %param.17) | copy-start | bytes 12292
  23.1 17.8 %copy-start.7 = (f32[32,8]{1,0:T(8,128)S(1)}, f32[32,8]{1,0:T(8,128)}, u32[]{:S(2)}) copy-start(f32[32,8]{1,0:T(8,128)} %get-tuple-element.43.refs_1_) | copy-start | bytes 3076
  23.1 7.1 %collective-permute-start.4 = (f32[80,512]{1,0:T(8,128)S(1)}, f32[80,512]{1,0:T(8,128)S(1)}, u32[]{:S(2)}, u32[]{:S(2)}) collective-permute-start(f32[80,512]{1,0:T(8,128)S(1)} %get-tuple-element.50.refs_0_.refs_7_.refs_10_), channel_id=1, source_target_pairs={{8,0},{16,8},{24,16},{32,24},{40,32},{48,40},{56,48},{64,56},{72,6... | collective-permute-start | bytes 491528 | tf_op jit(solution)/shard_map/ppermute | solution.py:467
  24.4 7.3 %collective-permute-start.5 = (f32[80,512]{1,0:T(8,128)S(1)}, f32[80,512]{1,0:T(8,128)S(1)}, u32[]{:S(2)}, u32[]{:S(2)}) collective-permute-start(f32[80,512]{1,0:T(8,128)S(1)} %get-tuple-element.51.refs_1_.refs_8_.refs_11_), channel_id=1, source_target_pairs={{0,8},{8,16},{16,24},{24,32},{32,40},{40,48},{48,56},{56,64},{64,7... | collective-permute-start | bytes 491528 | tf_op jit(solution)/shard_map/ppermute | solution.py:467
  32.3 12.3 %collective-permute-start.6 = (f32[96,512]{1,0:T(8,128)S(1)}, f32[96,512]{1,0:T(8,128)S(1)}, u32[]{:S(2)}, u32[]{:S(2)}) collective-permute-start(f32[96,512]{1,0:T(8,128)S(1)} %get-tuple-element.53.refs_10_.refs_0_.refs_13_), channel_id=1, source_target_pairs={{8,0},{16,8},{24,16},{32,24},{40,32},{48,40},{56,48},{64,56},{72,6... | collective-permute-start | bytes 589832 | tf_op jit(solution)/shard_map/ppermute | solution.py:467
  33.6 11.0 %collective-permute-start.7 = (f32[96,512]{1,0:T(8,128)S(1)}, f32[96,512]{1,0:T(8,128)S(1)}, u32[]{:S(2)}, u32[]{:S(2)}) collective-permute-start(f32[96,512]{1,0:T(8,128)S(1)} %get-tuple-element.54.refs_11_.refs_1_.refs_14_), channel_id=1, source_target_pairs={{0,8},{8,16},{16,24},{24,32},{32,40},{40,48},{48,56},{56,64},{64,7... | collective-permute-start | bytes 589832 | tf_op jit(solution)/shard_map/ppermute | solution.py:467
  45.2 8.0 %collective-permute-start.8 = (f32[112,512]{1,0:T(8,128)S(1)}, f32[112,512]{1,0:T(8,128)S(1)}, u32[]{:S(2)}, u32[]{:S(2)}) collective-permute-start(f32[112,512]{1,0:T(8,128)S(1)} %get-tuple-element.58.refs_0_.refs_16_), channel_id=1, source_target_pairs={{8,0},{16,8},{24,16},{32,24},{40,32},{48,40},{56,48},{64,56},{72,6... | collective-permute-start | bytes 688136 | tf_op jit(solution)/shard_map/ppermute | solution.py:467
  46.5 8.1 %collective-permute-start.9 = (f32[112,512]{1,0:T(8,128)S(1)}, f32[112,512]{1,0:T(8,128)S(1)}, u32[]{:S(2)}, u32[]{:S(2)}) collective-permute-start(f32[112,512]{1,0:T(8,128)S(1)} %get-tuple-element.59.refs_1_.refs_17_), channel_id=1, source_target_pairs={{0,8},{8,16},{16,24},{24,32},{32,40},{40,48},{48,56},{56,64},{64,7... | collective-permute-start | bytes 688136 | tf_op jit(solution)/shard_map/ppermute | solution.py:467
  55.4 8.7 %collective-permute-start.10 = (f32[128,512]{1,0:T(8,128)S(1)}, f32[128,512]{1,0:T(8,128)S(1)}, u32[]{:S(2)}, u32[]{:S(2)}) collective-permute-start(f32[128,512]{1,0:T(8,128)S(1)} %get-tuple-element.60.refs_0_.refs_19_), channel_id=1, source_target_pairs={{8,0},{16,8},{24,16},{32,24},{40,32},{48,40},{56,48},{64,56},{72,6... | collective-permute-start | bytes 786440 | tf_op jit(solution)/shard_map/ppermute | solution.py:467
  56.7 8.9 %collective-permute-start.11 = (f32[128,512]{1,0:T(8,128)S(1)}, f32[128,512]{1,0:T(8,128)S(1)}, u32[]{:S(2)}, u32[]{:S(2)}) collective-permute-start(f32[128,512]{1,0:T(8,128)S(1)} %get-tuple-element.61.refs_1_.refs_20_), channel_id=1, source_target_pairs={{0,8},{8,16},{16,24},{24,32},{32,40},{40,48},{48,56},{56,64},{64,7... | collective-permute-start | bytes 786440 | tf_op jit(solution)/shard_map/ppermute | solution.py:467
  111.0 46.8 %copy-start.5 = (f32[256,256]{1,0:T(8,128)S(1)}, f32[256,256]{1,0:T(8,128)}, u32[]{:S(2)}) copy-start(f32[256,256]{1,0:T(8,128)} %refs_1_.1) | copy-start | bytes 786436

commit v3 on v2

--- a/solution.py
+++ b/solution.py
@@ -10,8 +10,9 @@
 F32 = jnp.float32
 BF16 = jnp.bfloat16
 RED = ("y", "x", "c")
-LEVELS = 6
+LEVELS = 3
 LANE = 128
+MOVED = 64
 
 
 def nn(a, b):
@@ -28,11 +29,11 @@
     return jnp.sum(a, axis=1, keepdims=True)
 
 
-def call(kernel, outs, scratch=()):
+def call(kernel, outs, aliases={}):
     return pl.pallas_call(
         kernel,
         out_shape=outs,
-        scratch_shapes=list(scratch),
+        input_output_aliases=aliases,
         compiler_params=pltpu.CompilerParams(vmem_limit_bytes=12 * 1024 * 1024),
     )
 
@@ -154,28 +155,29 @@
     return row, col
 
 
+def packed(matrix):
+    half = LANE
+    row, col = lower(half)
+    last = matrix[half:, half:]
+    shared = jnp.where(row >= col, matrix[:half, :half], last)
+    return shared, matrix[half:, :half], jnp.sum(jnp.where(row == col, last, 0.0), axis=0, keepdims=True)
+
+
 def pack(ref, k, matrix, diagonals):
     half = LANE
     at = 2 * half * k
-    row, col = lower(half)
-    last = matrix[half:, half:]
-    ref[at : at + half, :] = jnp.where(row >= col, matrix[:half, :half], last)
-    ref[at + half : at + 2 * half, :] = matrix[half:, :half]
-    ref[diagonals + k : diagonals + k + 1, :] = jnp.sum(
-        jnp.where(row == col, last, 0.0), axis=0, keepdims=True
-    )
-
-
-def unpack(ref, k, diagonals):
-    half = LANE
-    at = 2 * half * k
-    row, col = lower(half)
-    shared = ref[at : at + half, :]
+    shared, cross, diagonal = packed(matrix)
+    ref[at : at + half, :] = shared
+    ref[at + half : at + 2 * half, :] = cross
+    ref[diagonals + k : diagonals + k + 1, :] = diagonal
+
+
+def unpacked(shared, cross, diagonal):
+    row, col = lower(LANE)
     flipped = jnp.transpose(shared)
-    cross = ref[at + half : at + 2 * half, :]
     first = jnp.where(row >= col, shared, flipped)
     last = jnp.where(row < col, shared, flipped)
-    last = jnp.where(row == col, ref[diagonals + k : diagonals + k + 1, :], last)
+    last = jnp.where(row == col, diagonal, last)
     return jnp.concatenate(
         [
             jnp.concatenate([first, jnp.transpose(cross)], axis=1),
@@ -185,57 +187,86 @@
     )
 
 
+def unpack(ref, k, diagonals):
+    half = LANE
+    at = 2 * half * k
+    return unpacked(
+        ref[at : at + half, :],
+        ref[at + half : at + 2 * half, :],
+        ref[diagonals + k : diagonals + k + 1, :],
+    )
+
+
+def level_moments(out, refs, k, cols, count):
+    half = count // 2
+    base = 8 * half - MOVED
+    t_ref, l_ref, r_ref = refs
+    rows, double = t_ref.shape
+    face = double // 2
+    width = rows - cols
+    spot = one_hot(l_ref[rows : rows + 1, 0:width], count)
+    tl, tr = t_ref[cols:rows, :face], t_ref[cols:rows, face:]
+    inner = nt(tl, l_ref[cols:rows, :]) + nt(tr, r_ref[cols:rows, :])
+    pack(out, k, nt(nn(spot, inner), spot), base + 9 * cols)
+    cross = nt(l_ref[0:cols, :], tl) + nt(r_ref[0:cols, :], tr)
+    put(out, base + 2 * cols * (k + 1), nt(cross, spot))
+    return lane_sum(t_ref[0:cols, :face] * l_ref[0:cols, :]) + lane_sum(
+        t_ref[0:cols, face:] * r_ref[0:cols, :]
+    )
+
+
+def put(out, at, block):
+    cols, half = block.shape[0], block.shape[1] // 2
+    out[at : at + cols, :] = block[:, :half]
+    out[at + cols : at + 2 * cols, :] = block[:, half:]
+
+
+def in_lanes(items, start=0):
+    cols = items[0].shape[0]
+    lane = lax.broadcasted_iota(jnp.int32, (cols, LANE), 1)
+    block = jnp.zeros((cols, LANE), F32)
+    for k, item in enumerate(items):
+        block = jnp.where(lane == start + k, item, block)
+    return block
+
+
 def moment_kernel(sl0_ref, cl_ref, gram_ref, *refs, cols, count):
     out = refs[-1]
-    half = count // 2
-
-    def put(at, block):
-        out[at : at + cols, :] = block[:, :half]
-        out[at + cols : at + 2 * cols, :] = block[:, half:]
-
-    base = 8 * half
+    base = 4 * count - MOVED
     at = base + 8 * cols
-    diagonals = at + cols
     out[at:, :] = jnp.zeros((out.shape[0] - at, LANE), F32)
     own = sl0_ref.shape[0] - cols - 8
-    put(base, nt(cl_ref[...], one_hot(sl0_ref[cols + own : cols + own + 1, 0:own], count)))
-    sums = []
-    for k in range(3):
-        t_ref, l_ref, r_ref = refs[3 * k : 3 * k + 3]
-        rows, double = t_ref.shape
-        face = double // 2
-        width = rows - cols
-        spot = one_hot(l_ref[rows : rows + 1, 0:width], count)
-        tl, tr = t_ref[cols:rows, :face], t_ref[cols:rows, face:]
-        inner = nt(tl, l_ref[cols:rows, :]) + nt(tr, r_ref[cols:rows, :])
-        pack(out, k, nt(nn(spot, inner), spot), diagonals)
-        cross = nt(l_ref[0:cols, :], tl) + nt(r_ref[0:cols, :], tr)
-        put(base + 2 * cols * (k + 1), nt(cross, spot))
-        sums.append(
-            lane_sum(t_ref[0:cols, :face] * l_ref[0:cols, :])
-            + lane_sum(t_ref[0:cols, face:] * r_ref[0:cols, :])
+    spot = one_hot(sl0_ref[cols + own : cols + own + 1, 0:own], count)
+    put(out, base, nt(cl_ref[...], spot))
+    sums = [level_moments(out, refs[3 * k : 3 * k + 3], k, cols, count) for k in range(2)]
+    gram = gram_ref[...]
+    half = count // 2
+    shared, cross, diagonal = packed(gram)
+    out[3 * count : 3 * count + half - MOVED, :] = shared[MOVED:, :]
+    out[3 * count + half - MOVED : base, :] = cross
+    out[at + cols + 3 : at + cols + 4, :] = diagonal
+    out[at : at + cols, :] = in_lanes(sums)
+
+
+def last_moment_kernel(given_ref, *refs, cols, count):
+    out = refs[-1]
+    total = level_moments(out, refs[:3], 2, cols, count)
+    at = 4 * count - MOVED + 8 * cols
+    out[at : at + cols, :] = given_ref[at : at + cols, :] + in_lanes([total], 2)
+
+
+def coarse_kernel(sums_ref, coarse_ref, mat_ref, sl0, sr0, t1, t2, sl2, sr2, t3, sl3,
+                  ol_ref, or_ref, z0_ref, w1c_ref, r1_ref, w0_ref, field_ref, scal_ref,
+                  *, cols, count):
+    base = 4 * count - MOVED
+    face = sl0.shape[1]
+
+    def get(at):
+        return jnp.concatenate(
+            [sums_ref[at : at + cols, :], sums_ref[at + cols : at + 2 * cols, :]], axis=1
         )
-    pack(out, 3, gram_ref[...], diagonals)
-    lane = lax.broadcasted_iota(jnp.int32, (cols, LANE), 1)
-    block = jnp.zeros((cols, LANE), F32)
-    for k in range(3):
-        block = jnp.where(lane == k, sums[k], block)
-    out[at : at + cols, :] = block
-
-
-def combine_kernel(sums_ref, coarse_ref, mass_ref, prev_ref, *refs, cols, count):
-    half = count // 2
-    base = 8 * half
-    diagonals = base + 9 * cols
-    sl0, sr0 = refs[0:2]
-    level = [None] + [refs[2 + 3 * k : 5 + 3 * k] for k in range(LEVELS)]
-    out_ref, field_ref, dual_ref, scal_ref = refs[2 + 3 * LEVELS :]
-    face = sl0.shape[1]
-
-    def get(at):
-        return jnp.concatenate([sums_ref[at : at + cols, :], sums_ref[at + cols : at + 2 * cols, :]], axis=1)
-
-    m0, m1, m2 = (unpack(sums_ref, k, diagonals) for k in range(3))
+
+    m0, m1, m2 = (unpack(sums_ref, k, base + 9 * cols) for k in range(3))
     coarse = coarse_ref[...]
     c_load, w0x, w1x, w2x = (get(base + 2 * cols * k) for k in range(4))
     at = base + 8 * cols
@@ -259,75 +290,107 @@
         + be1 * m0g1
     )
     gm = nn(cm, coarse)
-    last = level[LEVELS][1]
-    spot = one_hot(last[last.shape[0] - 8 : last.shape[0] - 7, 0:LANE], count)
+    spot = one_hot(sl3[sl3.shape[0] - 8 : sl3.shape[0] - 7, 0:LANE], count)
     local = nn(jnp.concatenate([g0, g1, gz1, gm], axis=0), spot)
 
-    def coef(k, n):
+    def spread(k, ref, first, n, lanes):
         width = 8 * (2 * k + 1)
-        first = 8 * (LEVELS - k)
-        return local[: n * cols, first : first + width]
-
-    def spread(k, ref, n, lanes):
-        width = 8 * (2 * k + 1)
-        wide = nn(coef(k, n), ref[cols : cols + width, lanes])
+        lane = 8 * (LEVELS - k)
+        wide = nn(local[first * cols : (first + n) * cols, lane : lane + width],
+                  ref[cols : cols + width, lanes])
         return [wide[i * cols : (i + 1) * cols] for i in range(n)]
 
-    def fields(b2, b4, b6, lanes):
-        x2, x4, x6 = (b[0:cols, lanes] for b in (b2, b4, b6))
-        p20, p21, p2z = spread(2, b2, 3, lanes)
-        p40, p41 = spread(4, b4, 2, lanes)
-        (p60,) = spread(6, b6, 1, lanes)
-        z0 = x2 + p20
-        n0 = x4 + p40 + p21
-        z1 = z0 - al0 * n0
-        n1 = x4 + p40 - al0 * (x6 + p60 + p41) + p2z
-        return z0, z1, n1 + be1 * n0
-
-    left, right, whole = slice(0, face), slice(face, 2 * face), slice(0, face)
-    t1, t2, t3, t4, t5, t6 = (level[k][0] for k in range(1, 7))
-    z0, z1, m = fields(t2, t4, t6, right)
-    _, _, m_left = fields(t2, t4, t6, left)
-    p10, p11, p1z = spread(1, t1, 3, right)
-    p30, p31 = spread(3, t3, 2, right)
-    (p50,) = spread(5, t5, 1, right)
-    x1, x3, x5 = (ref[0:cols, right] for ref in (t1, t3, t5))
-    d = x1 + p10
-    w0 = x3 + p30 + p11
-    w1 = x3 + p30 - al0 * (x5 + p50 + p31) + p1z
-    r1 = d - al0 * w0
+    every, right = slice(0, 2 * face), slice(face, 2 * face)
+    p10, p11, p1z = spread(1, t1, 0, 3, every)
+    (p20,) = spread(2, t2, 0, 1, every)
+    (p30,) = spread(3, t3, 0, 1, every)
+    z0_ref[...] = t2[0:cols, :] + p20
+    w0 = t3[0:cols, :] + p30 + p11
+    w0_ref[...] = w0[:, right]
+    w1c_ref[...] = p1z
+    r1_ref[...] = t1[0:cols, right] + p10[:, right] - al0 * w0[:, right]
+    v = split_dot(w0, mat_ref[...]) * 0.25
+    ol_ref[...] = v[:, :face]
+    or_ref[...] = v[:, right]
+    for own, u, lanes in ((sl0, sl2, slice(0, face)), (sr0, sr2, right)):
+        corner = spread(0, own, 0, 4, slice(0, face))
+        field_ref[0:cols, lanes] = own[0:cols, :] + corner[0]
+        (u0,) = spread(2, u, 0, 1, slice(0, face))
+        field_ref[cols : 2 * cols, lanes] = u[0:cols, :] + u0 + corner[1]
+        field_ref[2 * cols : 3 * cols, lanes] = corner[2]
+        field_ref[3 * cols : 4 * cols, lanes] = corner[3]
+    scal_ref[...] = in_lanes([al0, be1, lane_sum(cm * gm)])
+
+
+def joined(own_ref, other_ref, mask_ref, left):
+    face = own_ref.shape[1]
+    lanes = slice(0, face) if left else slice(face, 2 * face)
+    return (own_ref[...] - other_ref[...]) * mask_ref[0:1, lanes]
+
+
+def field_of(sl_ref, sr_ref, nl_ref, pr_ref, mask_ref):
+    return jnp.concatenate(
+        [joined(sl_ref, pr_ref, mask_ref, True), joined(sr_ref, nl_ref, mask_ref, False)], axis=1
+    )
+
+
+def dual_kernel(sl_ref, sr_ref, nl_ref, pr_ref, mask_ref, z0_ref, scal_ref, mat_ref,
+                n0_ref, z1_ref, ol_ref, or_ref):
+    face = sl_ref.shape[1]
+    n0 = field_of(sl_ref, sr_ref, nl_ref, pr_ref, mask_ref)
+    z1 = z0_ref[...] - scal_ref[:, 0:1] * n0
+    n0_ref[...] = n0
+    z1_ref[...] = z1[:, face:]
+    u = split_dot(z1, mat_ref[...])
+    ol_ref[...] = u[:, :face]
+    or_ref[...] = u[:, face:]
+
+
+def precondition_kernel(sl_ref, sr_ref, nl_ref, pr_ref, mask_ref, w1c_ref, mat_ref,
+                        w1_ref, ol_ref, or_ref):
+    face = sl_ref.shape[1]
+    w1 = field_of(sl_ref, sr_ref, nl_ref, pr_ref, mask_ref) + w1c_ref[...]
+    w1_ref[...] = w1[:, face:]
+    v = split_dot(w1, mat_ref[...]) * 0.25
+    ol_ref[...] = v[:, :face]
+    or_ref[...] = v[:, face:]
+
+
+def combine_kernel(sl_ref, sr_ref, nl_ref, pr_ref, mask_ref, n0_ref, mat_ref, scal_ref, z0_ref,
+                   z1_ref, ul_ref, ur_ref, r1_ref, w0_ref, w1_ref, base_ref, mass_ref, prev_ref,
+                   gram_ref, out_ref, field_ref, dual_ref, *, cols, count):
+    half = count // 2
+    face = sl_ref.shape[1]
+    be1 = scal_ref[:, 1:2]
+    whole = field_of(sl_ref, sr_ref, nl_ref, pr_ref, mask_ref) + be1 * n0_ref[...]
+    u = split_dot(whole, mat_ref[...])
+    field_ref[0 : 2 * cols, :] = base_ref[0 : 2 * cols, :]
+    third, fourth = slice(2 * cols, 3 * cols), slice(3 * cols, 4 * cols)
+    field_ref[third, 0:face] = base_ref[third, 0:face] + ul_ref[...]
+    field_ref[third, face:] = base_ref[third, face:] + ur_ref[...]
+    field_ref[fourth, :] = base_ref[fourth, :] + u
+    m = whole[:, face:]
+    z0, z1, w0, w1, r1 = z0_ref[:, face:], z1_ref[...], w0_ref[...], w1_ref[...], r1_ref[...]
     q1 = w1 + be1 * w0
     p1 = z1 + be1 * z0
-    for side, (own, pos, lanes) in enumerate(((sl0, 1, left), (sr0, 2, right))):
-        u = fields(level[2][pos], level[4][pos], level[6][pos], whole)
-        corner = spread(0, own, 4, whole)
-        field_ref[0:cols, lanes] = own[0:cols, :] + corner[0]
-        for i in range(3):
-            field_ref[(i + 1) * cols : (i + 2) * cols, lanes] = u[i] + corner[i + 1]
-        mu = lane_sum((m if side else m_left) * u[2])
-        mm = mu if side == 0 else mm + mu
     for i, item in enumerate((z0, z1, m)):
         dual_ref[i * cols : (i + 1) * cols, :] = item
     moments = (
         lane_sum(r1 * z1), lane_sum(r1 * m), lane_sum(q1 * z1), lane_sum(q1 * m),
-        lane_sum(r1 * p1), lane_sum(p1 * q1), lane_sum(z1 * w1), lane_sum(m * w1), mm,
-    )
-    lane = lax.broadcasted_iota(jnp.int32, (cols, LANE), 1)
-    block = jnp.zeros((cols, LANE), F32)
-    for k, item in enumerate(moments):
-        block = jnp.where(lane == k, item, block)
+        lane_sum(r1 * p1), lane_sum(p1 * q1), lane_sum(z1 * w1), lane_sum(m * w1),
+        lane_sum(whole * u),
+    )
     field = field_ref[...]
     scaled = field * mass_ref[...]
     tq = nn(scaled, prev_ref[...].astype(F32))
     out_ref[0 : 4 * cols, :] = tq[:, :half]
     out_ref[4 * cols : 8 * cols, :] = tq[:, half:]
     out_ref[8 * cols : 12 * cols, :] = nt(scaled, field)
-    out_ref[12 * cols : 13 * cols, :] = block
-    out_ref[13 * cols :, :] = jnp.zeros((out_ref.shape[0] - 13 * cols, LANE), F32)
-    block = jnp.zeros((cols, LANE), F32)
-    for k, item in enumerate((al0, be1, lane_sum(cm * gm))):
-        block = jnp.where(lane == k, item, block)
-    scal_ref[...] = block
+    out_ref[12 * cols : 13 * cols, :] = in_lanes(moments)
+    at = 13 * cols
+    shared, _, _ = packed(gram_ref[...])
+    out_ref[at : at + MOVED, :] = shared[:MOVED, :]
+    out_ref[at + MOVED :, :] = jnp.zeros((out_ref.shape[0] - at - MOVED, LANE), F32)
 
 
 def final_kernel(sums_ref, early_ref, scal_ref, field_ref, dual_ref, prev_ref, nm_ref,
@@ -369,7 +432,16 @@
         for j in range(4):
             tile = sums_ref[(8 + i) * cols : (9 + i) * cols, j * cols : (j + 1) * cols]
             gram = gram + weights[i] * tile * across[j]
-    basis = unpack(early_ref, 3, 8 * half + 9 * cols)
+    first = 3 * count
+    base = 4 * count - MOVED
+    basis = unpacked(
+        jnp.concatenate(
+            [sums_ref[13 * cols : 13 * cols + MOVED, :], early_ref[first : first + half - MOVED, :]],
+            axis=0,
+        ),
+        early_ref[base - half : base, :],
+        early_ref[base + 9 * cols + 3 : base + 9 * cols + 4, :],
+    )
     c = 2.0 * g1 - nn(g1, basis)
     coef_ref[...] = c
     gram = gram - nt(c, g1) - nt(g1, c) + nt(nn(c, basis), c)
@@ -490,30 +562,39 @@
             lambda *refs: basis_kernel(*refs, total=total),
             (jax.ShapeDtypeStruct(earlier.shape, BF16), shape(1, rows), shape(count, count)),
         )(earlier, nm_row, weights[None, :])
+        size = up(4 * count - MOVED + 9 * cols + 8, 8 * n_red)
+        first = call(
+            lambda *refs: moment_kernel(*refs, cols=cols, count=count), shape(size, LANE)
+        )(chain[0], cl, gram, *chain[2:8])
         t, sl, sr = step(3, sl, sr, near, schur_p)
         chain += [t, sl, sr]
+        first = call(
+            lambda *refs: last_moment_kernel(*refs, cols=cols, count=count),
+            shape(size, LANE),
+            aliases={0: 0},
+        )(first, t, sl, sr)
+        first = over_all(first, n_red, n_z)
+
+        wide, part = shape(cols, 2 * face), shape(cols, face)
+        sl0, sr0, t1, _, _, t2, sl2, sr2, t3, sl3, _ = chain
+        sl, sr, z0, w1c, r1, w0, base, scal = call(
+            lambda *refs: coarse_kernel(*refs, cols=cols, count=count),
+            (part, part, wide, wide, part, part, shape(4 * cols, rows), shape(cols, LANE)),
+        )(first, coarse_inverse, schur_p, sl0, sr0, t1, t2, sl2, sr2, t3, sl3)
         near = exchange(sl, sr)
-        size = up(4 * count + 9 * cols + 8, 8 * n_red)
-        first = call(
-            lambda *refs: moment_kernel(*refs, cols=cols, count=count), shape(size, LANE)
-        )(chain[0], cl, gram, *chain[2:11])
-        t, sl, sr = step(4, sl, sr, near, inv_p)
-        chain += [t, sl, sr]
-        first, sl, sr = lax.optimization_barrier((first, sl, sr))
+        n0, z1, ul, ur = call(dual_kernel, (wide, part, part, part))(
+            sl, sr, *near, mask, z0, scal, inv_p
+        )
+        near = exchange(ul, ur)
+        w1, sl, sr = call(precondition_kernel, (part, part, part))(
+            ul, ur, *near, mask, w1c, schur_p
+        )
         near = exchange(sl, sr)
-        t, sl, sr = step(5, sl, sr, near, schur_p)
-        chain += [t, sl, sr]
-        near = exchange(sl, sr)
-        t, sl, sr = step(6, sl, sr, near, inv_p)
-        chain += [t, sl, sr]
-        first, sl, sr = lax.optimization_barrier((first, sl, sr))
-        chain[-2:] = [sl, sr]
-        first = over_all(first, n_red, n_z)
-        size = up(13 * cols, 8 * n_red)
-        second, field, dual, scal = call(
+        size = up(13 * cols + MOVED, 8 * n_red)
+        second, field, dual = call(
             lambda *refs: combine_kernel(*refs, cols=cols, count=count),
-            (shape(size, LANE), shape(4 * cols, rows), shape(3 * cols, face), shape(cols, LANE)),
-        )(first, coarse_inverse, mass_p, prev_p, *chain)
+            (shape(size, LANE), shape(4 * cols, rows), shape(3 * cols, face)),
+        )(sl, sr, *near, mask, n0, inv_p, scal, z0, z1, ul, ur, r1, w0, w1, base, mass_p, prev_p, gram)
         second = over_all(second, n_red, n_z)
         block, multi, coefficients, factor = call(
             lambda *refs: final_kernel(*refs, cols=cols, count=count),

time: 214 us -> 206 us (0.963)
  waiting for transfers between devices: 11.7 us -> 7.16 us
  starting transfers between devices: 37.7 us -> 34.6 us
    pallas_call x0 -> x4, Pallas kernels: none -> 6.42 us  [the longest x1 3.97 us: on_device(): call(lambda *refs: coarse_kernel(*refs, cols=cols, count=count), (part, p...]
    ppermute x12, waiting for transfers between devices: 11.7 us -> 7.16 us  [exchange(): return (lax.ppermute(sl, along, behind), lax.ppermute(sr, along, ahead))]
    pallas_call x1, Pallas kernels: 5.61 us -> 1.54 us  [on_device(): call(lambda *refs: combine_kernel(*refs, cols=cols, count=count), (shape(...]
    ppermute x12, starting transfers between devices: 37.7 us -> 34.6 us  [exchange(): return (lax.ppermute(sl, along, behind), lax.ppermute(sr, along, ahead))]
  transfers between devices with their start and end apart: 12 -> 12, of which waited for: 8 -> 5; matrix products, arithmetic and copies ran while one was open for 0% -> 0% of each run, Pallas kernels for 4% -> 4%
where the time goes in v3:
time: 206 us; the launch traced here: 205 us
  blocking collectives  136 us (66%)
  starting transfers between devices  34.6 us (17%)
  Pallas kernels  26.3 us (13%)
  waiting for transfers between devices  7.16 us (3%)
    all_to_all x6, blocking collectives, swap(): return lax.all_to_all(parts, axes, 0, 0, tiled=True)  136 us
    ppermute x12, starting transfers between devices, exchange(): return (lax.ppermute(sl, along, behind), lax.ppermute(sr, along, ahead))  34.6 us
    ppermute x12, waiting for transfers between devices, exchange(): return (lax.ppermute(sl, along, behind), lax.ppermute(sr, along, ahead))  7.16 us
    pallas_call x1, Pallas kernels, on_device(): call(lambda *refs: final_kernel(*refs, cols=cols, count=count), (shape(co...  5.78 us
  transfers between devices with their start and end apart: 12, of which 5 were waited for; matrix products, arithmetic and copies ran while one was open for 0% of the time, Pallas kernels for 4%

profile of v3, /device:TPU:1, one launch (start us, length us, event | category | flops | bytes accessed | tf_op | source)
XLA Modules:
  0.0 205.4 jit_solution(14605137784759976474)
XLA Ops:
  0.7 3.6 %shard_map.120 = (f32[48,512]{1,0:T(8,128)}, f32[48,512]{1,0:T(8,128)}, f32[32,8]{1,0:T(8,128)}) custom-call(bf16[1024,1024]{1,0:T(8,128)(2,1)} %bitcast.21, f32[32,1024]{1,0:T(8,128)} %bitcast.36, f32[8,1024]{1,0:T(8,128)} %bitcast.37, s32[1,512]{1,0:T(1,128)} %bitcast.30, s32[1,8]{1,0:T(1,128)} %bitcast.38), custom_call_target="tpu_custom_call" | custom-call | tf_op jit(solution)/shard_map/pallas_call | solution.py:522
  4.2 4.4 %collective-permute-start.1 = (f32[48,512]{1,0:T(8,128)}, f32[48,512]{1,0:T(8,128)S(1)}, u32[]{:S(2)}, u32[]{:S(2)}) collective-permute-start(f32[48,512]{1,0:T(8,128)} %get-tuple-element.44.refs_1_.refs_4_), channel_id=1, source_target_pairs={{0,8},{8,16},{16,24},{24,32},{32,40},{40,48},{48,56},{56,64},{64,7... | collective-permute-start | bytes 294920 | tf_op jit(solution)/shard_map/ppermute | solution.py:539
  8.6 1.3 collective-permute-start
  10.0 0.0 copy-start.2
  10.0 1.5 shard_map.122.refs_5_.refs_2_.mat_ref
  11.5 0.0 copy-start
  11.5 0.0 collective-permute-done.1.refs_3_
  11.5 2.9 %collective-permute-done.refs_2_ = f32[48,512]{1,0:T(8,128)S(1)} collective-permute-done((f32[48,512]{1,0:T(8,128)}, f32[48,512]{1,0:T(8,128)S(1)}, u32[]{:S(2)}, u32[]{:S(2)}) %collective-permute-start) | collective-permute-done | bytes 98336 | tf_op jit(solution)/shard_map/ppermute | solution.py:539
  14.4 0.5 shard_map.123
  14.9 1.3 collective-permute-start.2
  16.2 4.5 %collective-permute-start.3 = (f32[64,512]{1,0:T(8,128)S(1)}, f32[64,512]{1,0:T(8,128)S(1)}, u32[]{:S(2)}, u32[]{:S(2)}) collective-permute-start(f32[64,512]{1,0:T(8,128)S(1)} %get-tuple-element.47.refs_1_.refs_5_), channel_id=1, source_target_pairs={{0,8},{8,16},{16,24},{24,32},{32,40},{40,48},{48,56},{56,64},{64,7... | collective-permute-start | bytes 393224 | tf_op jit(solution)/shard_map/ppermute | solution.py:539
  20.6 1.5 shard_map.124.refs_5_.mat_ref.refs_6_
  22.1 0.0 copy-start.3
  22.1 0.0 copy-start.8
  22.2 0.0 copy-start.7
  22.2 0.0 collective-permute-done.2.refs_2_
  22.2 0.4 collective-permute-done.3.refs_3_
  22.6 0.5 shard_map.125
  23.1 1.3 collective-permute-start.4
  24.4 5.1 %collective-permute-start.5 = (f32[80,512]{1,0:T(8,128)S(1)}, f32[80,512]{1,0:T(8,128)S(1)}, u32[]{:S(2)}, u32[]{:S(2)}) collective-permute-start(f32[80,512]{1,0:T(8,128)S(1)} %get-tuple-element.50.refs_8_.refs_1_), channel_id=1, source_target_pairs={{0,8},{8,16},{16,24},{24,32},{32,40},{40,48},{48,56},{56,64},{64,7... | collective-permute-start | bytes 491528 | tf_op jit(solution)/shard_map/ppermute | solution.py:539
  29.5 2.1 %shard_map.121 = (bf16[1024,256]{1,0:T(8,128)(2,1)S(1)}, f32[1,1024]{1,0:T(1,128)S(1)}, f32[256,256]{1,0:T(8,128)S(1)}) custom-call(bf16[1024,256]{1,0:T(8,128)(2,1)S(1)} %bitcast.28, s32[1,512]{1,0:T(1,128)S(1)} %bitcast.33, f32[1,1024]{1,0:T(1,128)S(1)} %bitcast.35), custom_call_target="tpu_custom_call" | custom-call | tf_op jit(solution)/shard_map/pallas_call | solution.py:561
  31.6 2.3 %shard_map.126.refs_0_ = f32[1280,128]{1,0:T(8,128)S(1)} custom-call(f32[48,512]{1,0:T(8,128)S(1)} %copy-done.2, f32[32,8]{1,0:T(8,128)S(1)} %copy-done.7, f32[256,256]{1,0:T(8,128)S(1)} %get-tuple-element.43.refs_2_.refs_18_, f32[56,1024]{1,0:T(8,128)S(1)} %get-tuple-element.45.refs_3_.refs_5_, f32[64,512]{1,0:T(8,128)S(1)} %get-tuple-element.46.refs_0_.refs_4_, ...), custom_call_target="tpu_custom_call" | custom-call | tf_op jit(solution)/shard_map/pallas_call | solution.py:566
  33.9 0.0 collective-permute-done.5.refs_3_
  33.9 0.6 shard_map.127
  34.4 1.5 shard_map.128
  35.9 35.0 %all_to_all.30.parts_ref = f32[32,40,128]{2,1,0:T(8,128)S(1)} all-to-all(f32[32,40,128]{2,1,0:T(8,128)S(1)} %bitcast.25), channel_id=1, replica_groups=mesh['y'=4,'z'=16,'x'=4,'c'=2] {'y','x','c'}, dimensions={0} | all-to-all | bytes 1310720 | tf_op jit(solution)/shard_map/all_to_all | solution.py:473
  70.9 0.1 shard_map.129
  71.0 21.1 %all_to_all.31.parts_ref = f32[16,40,128]{2,1,0:T(8,128)S(1)} all-to-all(f32[16,40,128]{2,1,0:T(8,128)S(1)} %shard_map.129), channel_id=1, replica_groups=mesh['y'=4,'z'=16,'x'=4,'c'=2] {'z'}, dimensions={0} | all-to-all | bytes 655360 | tf_op jit(solution)/shard_map/all_to_all | solution.py:473
  92.0 0.1 shard_map.130
  92.1 23.2 %all_to_all.32 = f32[32,40,128]{2,1,0:T(8,128)S(1)} all-to-all(f32[32,40,128]{2,1,0:T(8,128)S(1)} %shard_map.130), channel_id=1, replica_groups=mesh['y'=4,'z'=16,'x'=4,'c'=2] {'y','x','c'}, dimensions={0} | all-to-all | bytes 1310720 | tf_op jit(solution)/shard_map/all_to_all | solution.py:473
  115.3 4.0 %shard_map.131 = (f32[32,512]{1,0:T(8,128)S(1)}, f32[32,512]{1,0:T(8,128)S(1)}, f32[32,1024]{1,0:T(8,128)S(1)}, f32[32,1024]{1,0:T(8,128)S(1)}, f32[32,512]{1,0:...) custom-call(f32[1280,128]{1,0:T(8,128)S(1)} %bitcast.23, ...), custom_call_target="tpu_custom_call" | custom-call | tf_op jit(solution)/shard_map/pallas_call | solution.py:580
  119.3 1.3 collective-permute-start.6
  120.6 4.0 %collective-permute-start.7 = (f32[32,512]{1,0:T(8,128)S(1)}, f32[32,512]{1,0:T(8,128)S(1)}, u32[]{:S(2)}, u32[]{:S(2)}) collective-permute-start(f32[32,512]{1,0:T(8,128)S(1)} %get-tuple-element.55.sr_ref), channel_id=1, source_target_pairs={{0,8},{8,16},{16,24},{24,32},{32,40},{40,48},{48,56},{56,64},{64,7... | collective-permute-start | bytes 196616 | tf_op jit(solution)/shard_map/ppermute | solution.py:539
  124.6 1.3 collective-permute-done.7.pr_ref
  125.9 0.5 shard_map.132
  126.4 1.3 collective-permute-start.8
  127.7 4.3 %collective-permute-start.9 = (f32[32,512]{1,0:T(8,128)S(1)}, f32[32,512]{1,0:T(8,128)S(1)}, u32[]{:S(2)}, u32[]{:S(2)}) collective-permute-start(f32[32,512]{1,0:T(8,128)S(1)} %get-tuple-element.59.sr_ref.refs_11_), channel_id=1, source_target_pairs={{0,8},{8,16},{16,24},{24,32},{32,40},{40,48},{48,56},{56,64},{64,7... | collective-permute-start | bytes 196616 | tf_op jit(solution)/shard_map/ppermute | solution.py:539
  132.1 0.0 collective-permute-done.8.nl_ref
  132.1 1.3 collective-permute-done.9.pr_ref
  133.4 0.5 shard_map.133
  133.9 1.3 collective-permute-start.10
  135.2 4.6 %collective-permute-start.11 = (f32[32,512]{1,0:T(8,128)S(1)}, f32[32,512]{1,0:T(8,128)S(1)}, u32[]{:S(2)}, u32[]{:S(2)}) collective-permute-start(f32[32,512]{1,0:T(8,128)S(1)} %get-tuple-element.62.refs_1_), channel_id=1, source_target_pairs={{0,8},{8,16},{16,24},{24,32},{32,40},{40,48},{48,56},{56,64},{64,7... | collective-permute-start | bytes 196616 | tf_op jit(solution)/shard_map/ppermute | solution.py:539
  139.8 1.3 collective-permute-done.11.refs_3_
  141.1 1.5 shard_map.134
  142.6 27.3 %all_to_all.33.parts_ref = f32[32,16,128]{2,1,0:T(8,128)S(1)} all-to-all(f32[32,16,128]{2,1,0:T(8,128)S(1)} %bitcast.29), channel_id=1, replica_groups=mesh['y'=4,'z'=16,'x'=4,'c'=2] {'y','x','c'}, dimensions={0} | all-to-all | bytes 524288 | tf_op jit(solution)/shard_map/all_to_all | solution.py:473
  170.0 15.0 %all_to_all.34.parts_ref = f32[16,16,128]{2,1,0:T(8,128)S(1)} all-to-all(f32[16,16,128]{2,1,0:T(8,128)S(1)} %shard_map.135), channel_id=1, replica_groups=mesh['y'=4,'z'=16,'x'=4,'c'=2] {'z'}, dimensions={0} | all-to-all | bytes 262144 | tf_op jit(solution)/shard_map/all_to_all | solution.py:473
  185.0 14.6 %all_to_all.35 = f32[32,16,128]{2,1,0:T(8,128)S(1)} all-to-all(f32[32,16,128]{2,1,0:T(8,128)S(1)} %shard_map.136), channel_id=1, replica_groups=mesh['y'=4,'z'=16,'x'=4,'c'=2] {'y','x','c'}, dimensions={0} | all-to-all | bytes 524288 | tf_op jit(solution)/shard_map/all_to_all | solution.py:473
  199.6 5.8 %shard_map.137 = (f32[32,1024]{1,0:T(8,128)}, f32[32,512]{1,0:T(8,128)}, f32[32,256]{1,0:T(8,128)}, f32[32,32]{1,0:T(8,128)}) custom-call(f32[512,128]{1,0:T(8,128)S(1)} %bitcast.27, f32[1280,128]{1,0:T(8,128)S(1)} %bitcast.24, f32[32,128]{1,0:T(8,128)S(1)} %get-tuple-element.57.scal_ref.refs_7_.refs_2_, f32[128,1024]{1,0:T(8,128)S(1)} %get-tuple-element.72.refs_3_, ...), custom_call_target="tpu_custom_call" | custom-call | tf_op jit(solution)/shard_map/pallas_call | solution.py:599
  (20 shorter events, 0.1 us)
Async XLA Ops:
  0.6 9.3 %copy-start.6 = (s32[1,1,512]{2,1,0:T(1,128)S(1)}, s32[1,1,512]{2,1,0:T(1,128)}, u32[]{:S(2)}) copy-start(s32[1,1,512]{2,1,0:T(1,128)} %param.14) | copy-start | bytes 6148
  0.6 9.3 %copy-start.1 = (bf16[1,1,1024,1024]{3,2,1,0:T(8,128)(2,1)S(1)}, bf16[1,1,1024,1024]{3,2,1,0:T(8,128)(2,1)}, u32[]{:S(2)}) copy-start(bf16[1,1,1024,1024]{3,2,1,0:T(8,128)(2,1)} %param.10) | copy-start | bytes 6291460
  4.2 7.3 %collective-permute-start.1 = (f32[48,512]{1,0:T(8,128)}, f32[48,512]{1,0:T(8,128)S(1)}, u32[]{:S(2)}, u32[]{:S(2)}) collective-permute-start(f32[48,512]{1,0:T(8,128)} %get-tuple-element.44.refs_1_.refs_4_), channel_id=1, source_target_pairs={{0,8},{8,16},{16,24},{24,32},{32,40},{40,48},{48,56},{56,64},{64,7... | collective-permute-start | bytes 294920 | tf_op jit(solution)/shard_map/ppermute | solution.py:539
  8.6 5.8 %collective-permute-start = (f32[48,512]{1,0:T(8,128)}, f32[48,512]{1,0:T(8,128)S(1)}, u32[]{:S(2)}, u32[]{:S(2)}) collective-permute-start(f32[48,512]{1,0:T(8,128)} %get-tuple-element.41.refs_0_.refs_3_), channel_id=1, source_target_pairs={{8,0},{16,8},{24,16},{32,24},{40,32},{48,40},{56,48},{64,56},{72,6... | collective-permute-start | bytes 294920 | tf_op jit(solution)/shard_map/ppermute | solution.py:539
  10.0 4.4 %copy-start.2 = (f32[48,512]{1,0:T(8,128)S(1)}, f32[48,512]{1,0:T(8,128)}, u32[]{:S(2)}) copy-start(f32[48,512]{1,0:T(8,128)} %get-tuple-element.41.refs_0_.refs_3_) | copy-start | bytes 294916
  10.0 4.4 %copy-start.4 = (f32[48,512]{1,0:T(8,128)S(1)}, f32[48,512]{1,0:T(8,128)}, u32[]{:S(2)}) copy-start(f32[48,512]{1,0:T(8,128)} %get-tuple-element.44.refs_1_.refs_4_) | copy-start | bytes 294916
  11.5 9.2 %copy-start = (bf16[1,1,1024,1024]{3,2,1,0:T(8,128)(2,1)S(1)}, bf16[1,1,1024,1024]{3,2,1,0:T(8,128)(2,1)}, u32[]{:S(2)}) copy-start(bf16[1,1,1024,1024]{3,2,1,0:T(8,128)(2,1)} %param.9) | copy-start | bytes 6291460
  14.9 7.3 %collective-permute-start.2 = (f32[64,512]{1,0:T(8,128)S(1)}, f32[64,512]{1,0:T(8,128)S(1)}, u32[]{:S(2)}, u32[]{:S(2)}) collective-permute-start(f32[64,512]{1,0:T(8,128)S(1)} %get-tuple-element.46.refs_0_.refs_4_), channel_id=1, source_target_pairs={{8,0},{16,8},{24,16},{32,24},{40,32},{48,40},{56,48},{64,56},{72,6... | collective-permute-start | bytes 393224 | tf_op jit(solution)/shard_map/ppermute | solution.py:539
  16.2 6.4 %collective-permute-start.3 = (f32[64,512]{1,0:T(8,128)S(1)}, f32[64,512]{1,0:T(8,128)S(1)}, u32[]{:S(2)}, u32[]{:S(2)}) collective-permute-start(f32[64,512]{1,0:T(8,128)S(1)} %get-tuple-element.47.refs_1_.refs_5_), channel_id=1, source_target_pairs={{0,8},{8,16},{16,24},{24,32},{32,40},{40,48},{48,56},{56,64},{64,7... | collective-permute-start | bytes 393224 | tf_op jit(solution)/shard_map/ppermute | solution.py:539
  22.1 7.3 %copy-start.3 = (bf16[1,1,1024,256]{3,2,1,0:T(8,128)(2,1)S(1)}, bf16[1,1,1024,256]{3,2,1,0:T(8,128)(2,1)}, u32[]{:S(2)}) copy-start(bf16[1,1,1024,256]{3,2,1,0:T(8,128)(2,1)} %param.16) | copy-start | bytes 1572868
  22.1 7.3 %copy-start.8 = (f32[1,1,1024]{2,1,0:T(1,128)S(1)}, f32[1,1,1024]{2,1,0:T(1,128)}, u32[]{:S(2)}) copy-start(f32[1,1,1024]{2,1,0:T(1,128)} %param.17) | copy-start | bytes 12292
  22.2 9.4 %copy-start.7 = (f32[32,8]{1,0:T(8,128)S(1)}, f32[32,8]{1,0:T(8,128)}, u32[]{:S(2)}) copy-start(f32[32,8]{1,0:T(8,128)} %get-tuple-element.42.refs_1_) | copy-start | bytes 3076
  23.1 10.8 %collective-permute-start.4 = (f32[80,512]{1,0:T(8,128)S(1)}, f32[80,512]{1,0:T(8,128)S(1)}, u32[]{:S(2)}, u32[]{:S(2)}) collective-permute-start(f32[80,512]{1,0:T(8,128)S(1)} %get-tuple-element.49.refs_7_.refs_0_), channel_id=1, source_target_pairs={{8,0},{16,8},{24,16},{32,24},{40,32},{48,40},{56,48},{64,56},{72,6... | collective-permute-start | bytes 491528 | tf_op jit(solution)/shard_map/ppermute | solution.py:539
  24.4 9.5 %collective-permute-start.5 = (f32[80,512]{1,0:T(8,128)S(1)}, f32[80,512]{1,0:T(8,128)S(1)}, u32[]{:S(2)}, u32[]{:S(2)}) collective-permute-start(f32[80,512]{1,0:T(8,128)S(1)} %get-tuple-element.50.refs_8_.refs_1_), channel_id=1, source_target_pairs={{0,8},{8,16},{16,24},{24,32},{32,40},{40,48},{48,56},{56,64},{64,7... | collective-permute-start | bytes 491528 | tf_op jit(solution)/shard_map/ppermute | solution.py:539
  70.9 44.4 %copy-start.5 = (f32[256,256]{1,0:T(8,128)S(1)}, f32[256,256]{1,0:T(8,128)}, u32[]{:S(2)}) copy-start(f32[256,256]{1,0:T(8,128)} %refs_1_.1) | copy-start | bytes 786436
  119.3 5.3 %collective-permute-start.6 = (f32[32,512]{1,0:T(8,128)S(1)}, f32[32,512]{1,0:T(8,128)S(1)}, u32[]{:S(2)}, u32[]{:S(2)}) collective-permute-start(f32[32,512]{1,0:T(8,128)S(1)} %get-tuple-element.54.sl_ref), channel_id=1, source_target_pairs={{8,0},{16,8},{24,16},{32,24},{40,32},{48,40},{56,48},{64,56},{72,6... | collective-permute-start | bytes 196616 | tf_op jit(solution)/shard_map/ppermute | solution.py:539
  120.6 5.3 %collective-permute-start.7 = (f32[32,512]{1,0:T(8,128)S(1)}, f32[32,512]{1,0:T(8,128)S(1)}, u32[]{:S(2)}, u32[]{:S(2)}) collective-permute-start(f32[32,512]{1,0:T(8,128)S(1)} %get-tuple-element.55.sr_ref), channel_id=1, source_target_pairs={{0,8},{8,16},{16,24},{24,32},{32,40},{40,48},{48,56},{56,64},{64,7... | collective-permute-start | bytes 196616 | tf_op jit(solution)/shard_map/ppermute | solution.py:539
  126.4 5.6 %collective-permute-start.8 = (f32[32,512]{1,0:T(8,128)S(1)}, f32[32,512]{1,0:T(8,128)S(1)}, u32[]{:S(2)}, u32[]{:S(2)}) collective-permute-start(f32[32,512]{1,0:T(8,128)S(1)} %get-tuple-element.58.sl_ref.refs_10_), channel_id=1, source_target_pairs={{8,0},{16,8},{24,16},{32,24},{40,32},{48,40},{56,48},{64,56},{72,6... | collective-permute-start | bytes 196616 | tf_op jit(solution)/shard_map/ppermute | solution.py:539
  127.7 5.6 %collective-permute-start.9 = (f32[32,512]{1,0:T(8,128)S(1)}, f32[32,512]{1,0:T(8,128)S(1)}, u32[]{:S(2)}, u32[]{:S(2)}) collective-permute-start(f32[32,512]{1,0:T(8,128)S(1)} %get-tuple-element.59.sr_ref.refs_11_), channel_id=1, source_target_pairs={{0,8},{8,16},{16,24},{24,32},{32,40},{40,48},{48,56},{56,64},{64,7... | collective-permute-start | bytes 196616 | tf_op jit(solution)/shard_map/ppermute | solution.py:539
  133.9 5.9 %collective-permute-start.10 = (f32[32,512]{1,0:T(8,128)S(1)}, f32[32,512]{1,0:T(8,128)S(1)}, u32[]{:S(2)}, u32[]{:S(2)}) collective-permute-start(f32[32,512]{1,0:T(8,128)S(1)} %get-tuple-element.61.refs_0_), channel_id=1, source_target_pairs={{8,0},{16,8},{24,16},{32,24},{40,32},{48,40},{56,48},{64,56},{72,6... | collective-permute-start | bytes 196616 | tf_op jit(solution)/shard_map/ppermute | solution.py:539
  135.2 5.9 %collective-permute-start.11 = (f32[32,512]{1,0:T(8,128)S(1)}, f32[32,512]{1,0:T(8,128)S(1)}, u32[]{:S(2)}, u32[]{:S(2)}) collective-permute-start(f32[32,512]{1,0:T(8,128)S(1)} %get-tuple-element.62.refs_1_), channel_id=1, source_target_pairs={{0,8},{8,16},{16,24},{24,32},{32,40},{40,48},{48,56},{56,64},{64,7... | collective-permute-start | bytes 196616 | tf_op jit(solution)/shard_map/ppermute | solution.py:539

commit v4 on v3

--- a/solution.py
+++ b/solution.py
@@ -9,10 +9,9 @@
 HI = lax.Precision.HIGHEST
 F32 = jnp.float32
 BF16 = jnp.bfloat16
-RED = ("y", "x", "c")
+RED = ("y", "zl", "x", "c")
 LEVELS = 3
 LANE = 128
-MOVED = 64
 
 
 def nn(a, b):
@@ -38,12 +37,15 @@
     )
 
 
-def split_dot(t, mat):
-    high = t.astype(BF16).astype(F32)
-    both = jnp.concatenate([high, t - high], axis=0).astype(BF16)
-    wide = jnp.dot(both, mat, preferred_element_type=F32)
+def split_dot(t, mat, parts=2):
+    pieces = []
+    for _ in range(parts - 1):
+        pieces.append(t.astype(BF16).astype(F32))
+        t = t - pieces[-1]
+    wide = jnp.concatenate(pieces + [t], axis=0).astype(BF16)
+    wide = jnp.dot(wide, mat, preferred_element_type=F32)
     rows = t.shape[0]
-    return wide[:rows] + wide[rows:]
+    return sum(wide[i * rows : (i + 1) * rows] for i in range(1, parts)) + wide[:rows]
 
 
 def to_order(nm_row, face):
@@ -72,7 +74,7 @@
     rows = cols + corners
     load = load_ref[...]
     basis = basis_ref[...]
-    order = to_order(nm_ref[...], face)
+    order = to_order(nm_ref[...], face).astype(BF16)
     cl_ref[...] = nt(load, basis)
     for ref in (sl_ref, sr_ref):
         ref[rows : rows + 8, :] = jnp.zeros((8, face), F32)
@@ -81,7 +83,9 @@
     copies[-1].wait()
     wide = split_dot(load, inv_ref[...])
     sr_ref[0:cols, :] = wide[:, face:]
-    sl_ref[0:rows, :] = nn(jnp.concatenate([wide[:, :face], basis[:, :face]], axis=0), order)
+    left = [wide[:, :face], basis[:, :face], jnp.zeros((8, face), F32)]
+    left = split_dot(jnp.concatenate(left, axis=0), order, 3)
+    sl_ref[0:rows, :] = left[0:rows]
 
 
 def matrix_kernel(src, nm_ref, dst):
@@ -93,11 +97,12 @@
     dst[:face, :] = jnp.dot(back, dst[:face, :], preferred_element_type=F32).astype(BF16)
 
 
-def basis_kernel(prev_ref, nm_ref, mass_ref, prev_out, mass_out, gram_out, *, total):
+def basis_kernel(prev_ref, nm_ref, mass_ref, prev_out, flip_out, mass_out, gram_out, *, total):
     face = nm_ref.shape[1]
     back = from_order(nm_ref[...], face).astype(BF16)
     prev_out[face:, :] = prev_ref[face:, :]
     prev_out[:face, :] = jnp.dot(back, prev_ref[:face, :], preferred_element_type=F32).astype(BF16)
+    flip_out[...] = jnp.transpose(prev_out[...].astype(F32)).astype(BF16)
     mass = mass_ref[...] / total
     mass_out[:, face:] = mass[:, face:]
     left = jnp.broadcast_to(mass[:, :face], (8, face))
@@ -155,29 +160,28 @@
     return row, col
 
 
-def packed(matrix):
-    half = LANE
-    row, col = lower(half)
-    last = matrix[half:, half:]
-    shared = jnp.where(row >= col, matrix[:half, :half], last)
-    return shared, matrix[half:, :half], jnp.sum(jnp.where(row == col, last, 0.0), axis=0, keepdims=True)
-
-
 def pack(ref, k, matrix, diagonals):
     half = LANE
     at = 2 * half * k
-    shared, cross, diagonal = packed(matrix)
-    ref[at : at + half, :] = shared
-    ref[at + half : at + 2 * half, :] = cross
-    ref[diagonals + k : diagonals + k + 1, :] = diagonal
-
-
-def unpacked(shared, cross, diagonal):
-    row, col = lower(LANE)
+    row, col = lower(half)
+    last = matrix[half:, half:]
+    ref[at : at + half, :] = jnp.where(row >= col, matrix[:half, :half], last)
+    ref[at + half : at + 2 * half, :] = matrix[half:, :half]
+    ref[diagonals + k : diagonals + k + 1, :] = jnp.sum(
+        jnp.where(row == col, last, 0.0), axis=0, keepdims=True
+    )
+
+
+def unpack(ref, k, diagonals):
+    half = LANE
+    at = 2 * half * k
+    row, col = lower(half)
+    shared = ref[at : at + half, :]
     flipped = jnp.transpose(shared)
+    cross = ref[at + half : at + 2 * half, :]
     first = jnp.where(row >= col, shared, flipped)
     last = jnp.where(row < col, shared, flipped)
-    last = jnp.where(row == col, diagonal, last)
+    last = jnp.where(row == col, ref[diagonals + k : diagonals + k + 1, :], last)
     return jnp.concatenate(
         [
             jnp.concatenate([first, jnp.transpose(cross)], axis=1),
@@ -187,19 +191,8 @@
     )
 
 
-def unpack(ref, k, diagonals):
-    half = LANE
-    at = 2 * half * k
-    return unpacked(
-        ref[at : at + half, :],
-        ref[at + half : at + 2 * half, :],
-        ref[diagonals + k : diagonals + k + 1, :],
-    )
-
-
 def level_moments(out, refs, k, cols, count):
-    half = count // 2
-    base = 8 * half - MOVED
+    base = 4 * count
     t_ref, l_ref, r_ref = refs
     rows, double = t_ref.shape
     face = double // 2
@@ -232,33 +225,28 @@
 
 def moment_kernel(sl0_ref, cl_ref, gram_ref, *refs, cols, count):
     out = refs[-1]
-    base = 4 * count - MOVED
+    base = 4 * count
     at = base + 8 * cols
     out[at:, :] = jnp.zeros((out.shape[0] - at, LANE), F32)
     own = sl0_ref.shape[0] - cols - 8
     spot = one_hot(sl0_ref[cols + own : cols + own + 1, 0:own], count)
     put(out, base, nt(cl_ref[...], spot))
     sums = [level_moments(out, refs[3 * k : 3 * k + 3], k, cols, count) for k in range(2)]
-    gram = gram_ref[...]
-    half = count // 2
-    shared, cross, diagonal = packed(gram)
-    out[3 * count : 3 * count + half - MOVED, :] = shared[MOVED:, :]
-    out[3 * count + half - MOVED : base, :] = cross
-    out[at + cols + 3 : at + cols + 4, :] = diagonal
+    pack(out, 3, gram_ref[...], at + cols)
     out[at : at + cols, :] = in_lanes(sums)
 
 
 def last_moment_kernel(given_ref, *refs, cols, count):
     out = refs[-1]
     total = level_moments(out, refs[:3], 2, cols, count)
-    at = 4 * count - MOVED + 8 * cols
+    at = 4 * count + 8 * cols
     out[at : at + cols, :] = given_ref[at : at + cols, :] + in_lanes([total], 2)
 
 
 def coarse_kernel(sums_ref, coarse_ref, mat_ref, sl0, sr0, t1, t2, sl2, sr2, t3, sl3,
                   ol_ref, or_ref, z0_ref, w1c_ref, r1_ref, w0_ref, field_ref, scal_ref,
                   *, cols, count):
-    base = 4 * count - MOVED
+    base = 4 * count
     face = sl0.shape[1]
 
     def get(at):
@@ -358,7 +346,7 @@
 
 def combine_kernel(sl_ref, sr_ref, nl_ref, pr_ref, mask_ref, n0_ref, mat_ref, scal_ref, z0_ref,
                    z1_ref, ul_ref, ur_ref, r1_ref, w0_ref, w1_ref, base_ref, mass_ref, prev_ref,
-                   gram_ref, out_ref, field_ref, dual_ref, *, cols, count):
+                   out_ref, field_ref, dual_ref, *, cols, count):
     half = count // 2
     face = sl_ref.shape[1]
     be1 = scal_ref[:, 1:2]
@@ -382,15 +370,12 @@
     )
     field = field_ref[...]
     scaled = field * mass_ref[...]
-    tq = nn(scaled, prev_ref[...].astype(F32))
+    tq = split_dot(scaled, prev_ref[...], 3)
     out_ref[0 : 4 * cols, :] = tq[:, :half]
     out_ref[4 * cols : 8 * cols, :] = tq[:, half:]
     out_ref[8 * cols : 12 * cols, :] = nt(scaled, field)
     out_ref[12 * cols : 13 * cols, :] = in_lanes(moments)
-    at = 13 * cols
-    shared, _, _ = packed(gram_ref[...])
-    out_ref[at : at + MOVED, :] = shared[:MOVED, :]
-    out_ref[at + MOVED :, :] = jnp.zeros((out_ref.shape[0] - at - MOVED, LANE), F32)
+    out_ref[13 * cols :, :] = jnp.zeros((out_ref.shape[0] - 13 * cols, LANE), F32)
 
 
 def final_kernel(sums_ref, early_ref, scal_ref, field_ref, dual_ref, prev_ref, nm_ref,
@@ -426,27 +411,17 @@
     row = lax.broadcasted_iota(jnp.int32, (cols, cols), 0)
     col = lax.broadcasted_iota(jnp.int32, (cols, cols), 1)
     eye = (row == col).astype(F32)
-    across = [jnp.sum(y * eye, axis=0, keepdims=True) for y in weights]
-    gram = jnp.zeros((cols, cols), F32)
-    for i in range(4):
-        for j in range(4):
-            tile = sums_ref[(8 + i) * cols : (9 + i) * cols, j * cols : (j + 1) * cols]
-            gram = gram + weights[i] * tile * across[j]
-    first = 3 * count
-    base = 4 * count - MOVED
-    basis = unpacked(
-        jnp.concatenate(
-            [sums_ref[13 * cols : 13 * cols + MOVED, :], early_ref[first : first + half - MOVED, :]],
-            axis=0,
-        ),
-        early_ref[base - half : base, :],
-        early_ref[base + 9 * cols + 3 : base + 9 * cols + 4, :],
-    )
+    stacked = jnp.concatenate(weights, axis=0)
+    across = jnp.concatenate([jnp.sum(y * eye, axis=0, keepdims=True) for y in weights], axis=1)
+    tiles = stacked * sums_ref[8 * cols : 12 * cols, :] * across
+    tiles = sum(tiles[i * cols : (i + 1) * cols] for i in range(4))
+    gram = sum(tiles[:, j * cols : (j + 1) * cols] for j in range(4))
+    basis = unpack(early_ref, 3, 4 * count + 9 * cols)
     c = 2.0 * g1 - nn(g1, basis)
     coef_ref[...] = c
-    gram = gram - nt(c, g1) - nt(g1, c) + nt(nn(c, basis), c)
+    gram = gram + nt(c, nn(c, basis) - 2.0 * g1)
     gram = 0.5 * (gram + jnp.transpose(gram))
-    final = primal - nt(c, prev_ref[...].astype(F32))
+    final = primal - split_dot(c, prev_ref[...], 3)
     work = jnp.concatenate([gram, eye], axis=1)
     index = lax.broadcasted_iota(jnp.int32, (cols, 1), 0)
     pivots = jnp.zeros((cols, 1), F32)
@@ -458,7 +433,7 @@
     work = work / jnp.sqrt(pivots)
     factor_ref[...] = jnp.transpose(jnp.where(row <= col, work[:, :cols], 0.0))
     solved = nn(work[:, cols:], final)
-    left = nn(solved[:, :face], from_order(nm_ref[...], face))
+    left = split_dot(solved[:, :face], from_order(nm_ref[...], face).astype(BF16), 3)
     block_ref[:, :face] = left
     block_ref[:, face:] = solved[:, face:]
 
@@ -479,7 +454,7 @@
 
 def over_all(rows, n_red, n_z):
     parts = swap(rows.reshape(n_red, rows.shape[0] // n_red, LANE), RED)
-    parts = swap(summed(parts, n_z), "z")
+    parts = swap(summed(parts, n_z), "zh")
     return swap(summed(parts, n_red), RED).reshape(rows.shape)
 
 
@@ -490,12 +465,13 @@
 def solution(mesh):
     n_sub, n_grp = mesh.shape["sub"], mesh.shape["grp"]
     n_y = min(4, n_sub)
-    n_z = n_sub // n_y
-    n_c = 2
+    n_zl, n_c = 2, 2
+    n_z = n_sub // n_y // n_zl
     n_x = n_grp // n_c
-    fine = Mesh(np.asarray(mesh.devices).reshape(n_y, n_z, n_x, n_c), ("y", "z", "x", "c"))
-    n_red = n_y * n_x * n_c
-    along = ("y", "z")
+    devices = np.asarray(mesh.devices).reshape(n_y, n_z, n_zl, n_x, n_c)
+    fine = Mesh(devices, ("y", "zh", "zl", "x", "c"))
+    n_red = n_y * n_zl * n_x * n_c
+    along = ("y", "zh", "zl")
     ahead = [(i, i + 1) for i in range(n_sub - 1)]
     behind = [(i + 1, i) for i in range(n_sub - 1)]
 
@@ -555,14 +531,20 @@
         chain += [t, sl, sr]
         near = exchange(sl, sr)
         inv_p = call(matrix_kernel, square)(inverse_block, nm_row)
+        prev_p, prev_t, mass_p, gram = call(
+            lambda *refs: basis_kernel(*refs, total=total),
+            (
+                jax.ShapeDtypeStruct(earlier.shape, BF16),
+                jax.ShapeDtypeStruct(earlier.shape[::-1], BF16),
+                shape(1, rows),
+                shape(count, count),
+            ),
+        )(earlier, nm_row, weights[None, :])
+        near, gram = lax.optimization_barrier((near, gram))
         t, sl, sr = step(2, sl, sr, near, inv_p)
         chain += [t, sl, sr]
         near = exchange(sl, sr)
-        prev_p, mass_p, gram = call(
-            lambda *refs: basis_kernel(*refs, total=total),
-            (jax.ShapeDtypeStruct(earlier.shape, BF16), shape(1, rows), shape(count, count)),
-        )(earlier, nm_row, weights[None, :])
-        size = up(4 * count - MOVED + 9 * cols + 8, 8 * n_red)
+        size = up(4 * count + 9 * cols + 8, 8 * n_red)
         first = call(
             lambda *refs: moment_kernel(*refs, cols=cols, count=count), shape(size, LANE)
         )(chain[0], cl, gram, *chain[2:8])
@@ -590,16 +572,16 @@
             ul, ur, *near, mask, w1c, schur_p
         )
         near = exchange(sl, sr)
-        size = up(13 * cols + MOVED, 8 * n_red)
+        size = up(13 * cols, 8 * n_red)
         second, field, dual = call(
             lambda *refs: combine_kernel(*refs, cols=cols, count=count),
             (shape(size, LANE), shape(4 * cols, rows), shape(3 * cols, face)),
-        )(sl, sr, *near, mask, n0, inv_p, scal, z0, z1, ul, ur, r1, w0, w1, base, mass_p, prev_p, gram)
+        )(sl, sr, *near, mask, n0, inv_p, scal, z0, z1, ul, ur, r1, w0, w1, base, mass_p, prev_p)
         second = over_all(second, n_red, n_z)
         block, multi, coefficients, factor = call(
             lambda *refs: final_kernel(*refs, cols=cols, count=count),
             (shape(cols, rows), shape(cols, face), shape(cols, count), shape(cols, cols)),
-        )(second, first, scal, field, dual, prev_p, nm_row)
+        )(second, first, scal, field, dual, prev_t, nm_row)
         return block.T[None, None], multi.T[None, None], coefficients.T, factor
 
     split = (along, ("x", "c"))

time: 206 us -> 201 us (0.976)
  blocking collectives: 136 us -> 133 us
    all_to_all x6, blocking collectives: 136 us -> 133 us  [swap(): return lax.all_to_all(parts, axes, 0, 0, tiled=True)]
  transfers between devices with their start and end apart: 12 -> 12, of which waited for: 5 -> 4; matrix products, arithmetic and copies ran while one was open for 0% -> 0% of each run, Pallas kernels for 4% -> 4%
where the time goes in v4:
time: 201 us; the launch traced here: 200 us
  blocking collectives  133 us (66%)
  starting transfers between devices  34.8 us (17%)
  Pallas kernels  25.3 us (13%)
  waiting for transfers between devices  6.8 us (3%)
    all_to_all x6, blocking collectives, swap(): return lax.all_to_all(parts, axes, 0, 0, tiled=True)  133 us
    ppermute x12, starting transfers between devices, exchange(): return (lax.ppermute(sl, along, behind), lax.ppermute(sr, along, ahead))  34.8 us
    ppermute x12, waiting for transfers between devices, exchange(): return (lax.ppermute(sl, along, behind), lax.ppermute(sr, along, ahead))  6.8 us
    pallas_call x1, Pallas kernels, on_device(): call(lambda *refs: final_kernel(*refs, cols=cols, count=count), (shape(co...  5.24 us
  transfers between devices with their start and end apart: 12, of which 4 were waited for; matrix products, arithmetic and copies ran while one was open for 0% of the time, Pallas kernels for 4%

profile of v4, /device:TPU:1, one launch (start us, length us, event | category | flops | bytes accessed | tf_op | source)
XLA Modules:
  0.0 200.4 jit_solution(9208279548439932456)
XLA Ops:
  0.7 3.2 %shard_map.120 = (f32[48,512]{1,0:T(8,128)}, f32[48,512]{1,0:T(8,128)}, f32[32,8]{1,0:T(8,128)}) custom-call(bf16[1024,1024]{1,0:T(8,128)(2,1)} %bitcast.21, f32[32,1024]{1,0:T(8,128)} %bitcast.36, f32[8,1024]{1,0:T(8,128)} %bitcast.37, s32[1,512]{1,0:T(1,128)} %bitcast.30, s32[1,8]{1,0:T(1,128)} %bitcast.38), custom_call_target="tpu_custom_call" | custom-call | tf_op jit(solution)/shard_map/pallas_call | solution.py:498
  3.8 4.4 %collective-permute-start.1 = (f32[48,512]{1,0:T(8,128)}, f32[48,512]{1,0:T(8,128)S(1)}, u32[]{:S(2)}, u32[]{:S(2)}) collective-permute-start(f32[48,512]{1,0:T(8,128)} %get-tuple-element.47.refs_1_.refs_4_), channel_id=1, source_target_pairs={{0,8},{8,16},{16,24},{24,32},{32,40},{40,48},{48,56},{56,64},{64,7... | collective-permute-start | bytes 294920 | tf_op jit(solution)/shard_map/ppermute | solution.py:515
  8.2 1.3 collective-permute-start
  9.5 0.0 copy-start.2
  9.6 1.5 shard_map.121.refs_5_.refs_2_.mat_ref
  11.1 0.0 copy-start
  11.1 2.9 %collective-permute-done.refs_2_ = f32[48,512]{1,0:T(8,128)S(1)} collective-permute-done((f32[48,512]{1,0:T(8,128)}, f32[48,512]{1,0:T(8,128)S(1)}, u32[]{:S(2)}, u32[]{:S(2)}) %collective-permute-start) | collective-permute-done | bytes 98336 | tf_op jit(solution)/shard_map/ppermute | solution.py:515
  14.0 0.5 shard_map.122
  14.4 1.3 collective-permute-start.2
  15.7 0.0 copy-start.3
  15.7 0.0 copy-start.8
  15.8 4.6 %collective-permute-start.3 = (f32[64,512]{1,0:T(8,128)S(1)}, f32[64,512]{1,0:T(8,128)S(1)}, u32[]{:S(2)}, u32[]{:S(2)}) collective-permute-start(f32[64,512]{1,0:T(8,128)S(1)} %get-tuple-element.49.refs_1_.refs_5_), channel_id=1, source_target_pairs={{0,8},{8,16},{16,24},{24,32},{32,40},{40,48},{48,56},{56,64},{64,7... | collective-permute-start | bytes 393224 | tf_op jit(solution)/shard_map/ppermute | solution.py:515
  20.4 1.5 shard_map.124.refs_5_.mat_ref.refs_6_
  21.9 0.0 copy-start.7
  21.9 2.1 %shard_map.123 = (bf16[1024,256]{1,0:T(8,128)(2,1)S(1)}, bf16[256,1024]{1,0:T(8,128)(2,1)S(1)}, f32[1,1024]{1,0:T(1,128)S(1)}, f32[256,256]{1,0:T(8,128)S(1)}) custom-call(bf16[1024,256]{1,0:T(8,128)(2,1)S(1)} %bitcast.28, s32[1,512]{1,0:T(1,128)S(1)} %bitcast.33, f32[1,1024]{1,0:T(1,128)S(1)} %bitcast.35), custom_call_target="tpu_custom_call" | custom-call | tf_op jit(solution)/shard_map/pallas_call | solution.py:534
  24.0 0.0 collective-permute-done.2.refs_2_
  24.0 0.5 shard_map.125
  24.5 1.3 collective-permute-start.4
  25.8 5.1 %collective-permute-start.5 = (f32[80,512]{1,0:T(8,128)S(1)}, f32[80,512]{1,0:T(8,128)S(1)}, u32[]{:S(2)}, u32[]{:S(2)}) collective-permute-start(f32[80,512]{1,0:T(8,128)S(1)} %get-tuple-element.57.refs_8_.refs_1_), channel_id=1, source_target_pairs={{0,8},{8,16},{16,24},{24,32},{32,40},{40,48},{48,56},{56,64},{64,7... | collective-permute-start | bytes 491528 | tf_op jit(solution)/shard_map/ppermute | solution.py:515
  30.9 2.3 %shard_map.126.refs_0_ = f32[1536,128]{1,0:T(8,128)S(1)} custom-call(f32[48,512]{1,0:T(8,128)S(1)} %copy-done.2, f32[32,8]{1,0:T(8,128)S(1)} %copy-done.7, f32[256,256]{1,0:T(8,128)S(1)} %get-tuple-element.51.refs_2_, f32[56,1024]{1,0:T(8,128)S(1)} %get-tuple-element.52.refs_3_.refs_5_, f32[64,512]{1,0:T(8,128)S(1)} %get-tuple-element.48.refs_0_.refs_4_, ...), custom_call_target="tpu_custom_call" | custom-call | tf_op jit(solution)/shard_map/pallas_call | solution.py:548
  33.2 0.0 collective-permute-done.4.refs_2_
  33.2 0.0 collective-permute-done.5.refs_3_
  33.2 0.6 shard_map.127
  33.8 1.5 shard_map.128
  35.3 38.8 %all_to_all.30.parts_ref = f32[64,24,128]{2,1,0:T(8,128)S(1)} all-to-all(f32[64,24,128]{2,1,0:T(8,128)S(1)} %bitcast.25), channel_id=1, replica_groups=mesh['y'=4,'zh'=8,'zl'=2,'x'=4,'c'=2] {'y','zl','x','c'}, dimensions={0} | all-to-all | bytes 1572864 | tf_op jit(solution)/shard_map/all_to_all | solution.py:448
  74.1 0.1 shard_map.129
  74.1 18.1 %all_to_all.31.parts_ref = f32[8,24,128]{2,1,0:T(8,128)S(1)} all-to-all(f32[8,24,128]{2,1,0:T(8,128)S(1)} %shard_map.129), channel_id=1, replica_groups=mesh['y'=4,'zh'=8,'zl'=2,'x'=4,'c'=2] {'zh'}, dimensions={0} | all-to-all | bytes 196608 | tf_op jit(solution)/shard_map/all_to_all | solution.py:448
  92.2 0.1 shard_map.130
  92.3 22.1 %all_to_all.32 = f32[64,24,128]{2,1,0:T(8,128)S(1)} all-to-all(f32[64,24,128]{2,1,0:T(8,128)S(1)} %shard_map.130), channel_id=1, replica_groups=mesh['y'=4,'zh'=8,'zl'=2,'x'=4,'c'=2] {'y','zl','x','c'}, dimensions={0} | all-to-all | bytes 1572864 | tf_op jit(solution)/shard_map/all_to_all | solution.py:448
  114.4 4.0 %shard_map.131 = (f32[32,512]{1,0:T(8,128)S(1)}, f32[32,512]{1,0:T(8,128)S(1)}, f32[32,1024]{1,0:T(8,128)S(1)}, f32[32,1024]{1,0:T(8,128)S(1)}, f32[32,512]{1,0:...) custom-call(f32[1536,128]{1,0:T(8,128)S(1)} %bitcast.23, ...), custom_call_target="tpu_custom_call" | custom-call | tf_op jit(solution)/shard_map/pallas_call | solution.py:562
  118.4 1.3 collective-permute-start.6
  119.7 4.0 %collective-permute-start.7 = (f32[32,512]{1,0:T(8,128)S(1)}, f32[32,512]{1,0:T(8,128)S(1)}, u32[]{:S(2)}, u32[]{:S(2)}) collective-permute-start(f32[32,512]{1,0:T(8,128)S(1)} %get-tuple-element.62.sr_ref), channel_id=1, source_target_pairs={{0,8},{8,16},{16,24},{24,32},{32,40},{40,48},{48,56},{56,64},{64,7... | collective-permute-start | bytes 196616 | tf_op jit(solution)/shard_map/ppermute | solution.py:515
  123.7 0.0 collective-permute-done.6.nl_ref
  123.7 1.3 collective-permute-done.7.pr_ref
  125.0 0.5 shard_map.132
  125.5 1.3 collective-permute-start.8
  126.8 4.3 %collective-permute-start.9 = (f32[32,512]{1,0:T(8,128)S(1)}, f32[32,512]{1,0:T(8,128)S(1)}, u32[]{:S(2)}, u32[]{:S(2)}) collective-permute-start(f32[32,512]{1,0:T(8,128)S(1)} %get-tuple-element.66.sr_ref.refs_11_), channel_id=1, source_target_pairs={{0,8},{8,16},{16,24},{24,32},{32,40},{40,48},{48,56},{56,64},{64,7... | collective-permute-start | bytes 196616 | tf_op jit(solution)/shard_map/ppermute | solution.py:515
  131.1 1.3 collective-permute-done.9.pr_ref
  132.4 0.5 shard_map.133
  132.9 1.3 collective-permute-start.10
  134.2 4.6 %collective-permute-start.11 = (f32[32,512]{1,0:T(8,128)S(1)}, f32[32,512]{1,0:T(8,128)S(1)}, u32[]{:S(2)}, u32[]{:S(2)}) collective-permute-start(f32[32,512]{1,0:T(8,128)S(1)} %get-tuple-element.69.refs_1_), channel_id=1, source_target_pairs={{0,8},{8,16},{16,24},{24,32},{32,40},{40,48},{48,56},{56,64},{64,7... | collective-permute-start | bytes 196616 | tf_op jit(solution)/shard_map/ppermute | solution.py:515
  138.8 1.3 collective-permute-done.11.refs_3_
  140.1 1.4 shard_map.134
  141.5 24.2 %all_to_all.33.parts_ref = f32[64,8,128]{2,1,0:T(8,128)S(1)} all-to-all(f32[64,8,128]{2,1,0:T(8,128)S(1)} %bitcast.29), channel_id=1, replica_groups=mesh['y'=4,'zh'=8,'zl'=2,'x'=4,'c'=2] {'y','zl','x','c'}, dimensions={0} | all-to-all | bytes 524288 | tf_op jit(solution)/shard_map/all_to_all | solution.py:448
  165.7 0.1 shard_map.135
  165.8 14.4 %all_to_all.34.parts_ref = f32[8,8,128]{2,1,0:T(8,128)S(1)} all-to-all(f32[8,8,128]{2,1,0:T(8,128)S(1)} %shard_map.135), channel_id=1, replica_groups=mesh['y'=4,'zh'=8,'zl'=2,'x'=4,'c'=2] {'zh'}, dimensions={0} | all-to-all | bytes 65536 | tf_op jit(solution)/shard_map/all_to_all | solution.py:448
  180.2 15.0 %all_to_all.35 = f32[64,8,128]{2,1,0:T(8,128)S(1)} all-to-all(f32[64,8,128]{2,1,0:T(8,128)S(1)} %shard_map.136), channel_id=1, replica_groups=mesh['y'=4,'zh'=8,'zl'=2,'x'=4,'c'=2] {'y','zl','x','c'}, dimensions={0} | all-to-all | bytes 524288 | tf_op jit(solution)/shard_map/all_to_all | solution.py:448
  195.2 5.2 %shard_map.137 = (f32[32,1024]{1,0:T(8,128)}, f32[32,512]{1,0:T(8,128)}, f32[32,256]{1,0:T(8,128)}, f32[32,32]{1,0:T(8,128)}) custom-call(f32[512,128]{1,0:T(8,128)S(1)} %bitcast.27, f32[1536,128]{1,0:T(8,128)S(1)} %bitcast.24, f32[32,128]{1,0:T(8,128)S(1)} %get-tuple-element.64.scal_ref.refs_7_.refs_2_, f32[128,1024]{1,0:T(8,128)S(1)} %get-tuple-element.79.refs_3_, ...), custom_call_target="tpu_custom_call" | custom-call | tf_op jit(solution)/shard_map/pallas_call | solution.py:581
  (20 shorter events, 0.1 us)
Async XLA Ops:
  0.6 8.9 %copy-start.6 = (s32[1,1,512]{2,1,0:T(1,128)S(1)}, s32[1,1,512]{2,1,0:T(1,128)}, u32[]{:S(2)}) copy-start(s32[1,1,512]{2,1,0:T(1,128)} %param.14) | copy-start | bytes 6148
  0.6 8.9 %copy-start.1 = (bf16[1,1,1024,1024]{3,2,1,0:T(8,128)(2,1)S(1)}, bf16[1,1,1024,1024]{3,2,1,0:T(8,128)(2,1)}, u32[]{:S(2)}) copy-start(bf16[1,1,1024,1024]{3,2,1,0:T(8,128)(2,1)} %param.10) | copy-start | bytes 6291460
  3.8 7.3 %collective-permute-start.1 = (f32[48,512]{1,0:T(8,128)}, f32[48,512]{1,0:T(8,128)S(1)}, u32[]{:S(2)}, u32[]{:S(2)}) collective-permute-start(f32[48,512]{1,0:T(8,128)} %get-tuple-element.47.refs_1_.refs_4_), channel_id=1, source_target_pairs={{0,8},{8,16},{16,24},{24,32},{32,40},{40,48},{48,56},{56,64},{64,7... | collective-permute-start | bytes 294920 | tf_op jit(solution)/shard_map/ppermute | solution.py:515
  8.2 5.8 %collective-permute-start = (f32[48,512]{1,0:T(8,128)}, f32[48,512]{1,0:T(8,128)S(1)}, u32[]{:S(2)}, u32[]{:S(2)}) collective-permute-start(f32[48,512]{1,0:T(8,128)} %get-tuple-element.45.refs_0_.refs_3_), channel_id=1, source_target_pairs={{8,0},{16,8},{24,16},{32,24},{40,32},{48,40},{56,48},{64,56},{72,6... | collective-permute-start | bytes 294920 | tf_op jit(solution)/shard_map/ppermute | solution.py:515
  9.5 4.4 %copy-start.2 = (f32[48,512]{1,0:T(8,128)S(1)}, f32[48,512]{1,0:T(8,128)}, u32[]{:S(2)}) copy-start(f32[48,512]{1,0:T(8,128)} %get-tuple-element.45.refs_0_.refs_3_) | copy-start | bytes 294916
  9.6 4.4 %copy-start.4 = (f32[48,512]{1,0:T(8,128)S(1)}, f32[48,512]{1,0:T(8,128)}, u32[]{:S(2)}) copy-start(f32[48,512]{1,0:T(8,128)} %get-tuple-element.47.refs_1_.refs_4_) | copy-start | bytes 294916
  11.1 9.3 %copy-start = (bf16[1,1,1024,1024]{3,2,1,0:T(8,128)(2,1)S(1)}, bf16[1,1,1024,1024]{3,2,1,0:T(8,128)(2,1)}, u32[]{:S(2)}) copy-start(bf16[1,1,1024,1024]{3,2,1,0:T(8,128)(2,1)} %param.9) | copy-start | bytes 6291460
  14.4 9.6 %collective-permute-start.2 = (f32[64,512]{1,0:T(8,128)S(1)}, f32[64,512]{1,0:T(8,128)S(1)}, u32[]{:S(2)}, u32[]{:S(2)}) collective-permute-start(f32[64,512]{1,0:T(8,128)S(1)} %get-tuple-element.48.refs_0_.refs_4_), channel_id=1, source_target_pairs={{8,0},{16,8},{24,16},{32,24},{40,32},{48,40},{56,48},{64,56},{72,6... | collective-permute-start | bytes 393224 | tf_op jit(solution)/shard_map/ppermute | solution.py:515
  15.7 6.1 %copy-start.3 = (bf16[1,1,1024,256]{3,2,1,0:T(8,128)(2,1)S(1)}, bf16[1,1,1024,256]{3,2,1,0:T(8,128)(2,1)}, u32[]{:S(2)}) copy-start(bf16[1,1,1024,256]{3,2,1,0:T(8,128)(2,1)} %param.16) | copy-start | bytes 1572868
  15.7 6.1 %copy-start.8 = (f32[1,1,1024]{2,1,0:T(1,128)S(1)}, f32[1,1,1024]{2,1,0:T(1,128)}, u32[]{:S(2)}) copy-start(f32[1,1,1024]{2,1,0:T(1,128)} %param.17) | copy-start | bytes 12292
  15.8 8.3 %collective-permute-start.3 = (f32[64,512]{1,0:T(8,128)S(1)}, f32[64,512]{1,0:T(8,128)S(1)}, u32[]{:S(2)}, u32[]{:S(2)}) collective-permute-start(f32[64,512]{1,0:T(8,128)S(1)} %get-tuple-element.49.refs_1_.refs_5_), channel_id=1, source_target_pairs={{0,8},{8,16},{16,24},{24,32},{32,40},{40,48},{48,56},{56,64},{64,7... | collective-permute-start | bytes 393224 | tf_op jit(solution)/shard_map/ppermute | solution.py:515
  21.9 9.1 %copy-start.7 = (f32[32,8]{1,0:T(8,128)S(1)}, f32[32,8]{1,0:T(8,128)}, u32[]{:S(2)}) copy-start(f32[32,8]{1,0:T(8,128)} %get-tuple-element.46.refs_1_) | copy-start | bytes 3076
  24.5 8.7 %collective-permute-start.4 = (f32[80,512]{1,0:T(8,128)S(1)}, f32[80,512]{1,0:T(8,128)S(1)}, u32[]{:S(2)}, u32[]{:S(2)}) collective-permute-start(f32[80,512]{1,0:T(8,128)S(1)} %get-tuple-element.56.refs_7_.refs_0_), channel_id=1, source_target_pairs={{8,0},{16,8},{24,16},{32,24},{40,32},{48,40},{56,48},{64,56},{72,6... | collective-permute-start | bytes 491528 | tf_op jit(solution)/shard_map/ppermute | solution.py:515
  25.8 7.4 %collective-permute-start.5 = (f32[80,512]{1,0:T(8,128)S(1)}, f32[80,512]{1,0:T(8,128)S(1)}, u32[]{:S(2)}, u32[]{:S(2)}) collective-permute-start(f32[80,512]{1,0:T(8,128)S(1)} %get-tuple-element.57.refs_8_.refs_1_), channel_id=1, source_target_pairs={{0,8},{8,16},{16,24},{24,32},{32,40},{40,48},{48,56},{56,64},{64,7... | collective-permute-start | bytes 491528 | tf_op jit(solution)/shard_map/ppermute | solution.py:515
  74.1 40.3 %copy-start.5 = (f32[256,256]{1,0:T(8,128)S(1)}, f32[256,256]{1,0:T(8,128)}, u32[]{:S(2)}) copy-start(f32[256,256]{1,0:T(8,128)} %refs_1_.1) | copy-start | bytes 786436
  118.4 5.3 %collective-permute-start.6 = (f32[32,512]{1,0:T(8,128)S(1)}, f32[32,512]{1,0:T(8,128)S(1)}, u32[]{:S(2)}, u32[]{:S(2)}) collective-permute-start(f32[32,512]{1,0:T(8,128)S(1)} %get-tuple-element.61.sl_ref), channel_id=1, source_target_pairs={{8,0},{16,8},{24,16},{32,24},{40,32},{48,40},{56,48},{64,56},{72,6... | collective-permute-start | bytes 196616 | tf_op jit(solution)/shard_map/ppermute | solution.py:515
  119.7 5.3 %collective-permute-start.7 = (f32[32,512]{1,0:T(8,128)S(1)}, f32[32,512]{1,0:T(8,128)S(1)}, u32[]{:S(2)}, u32[]{:S(2)}) collective-permute-start(f32[32,512]{1,0:T(8,128)S(1)} %get-tuple-element.62.sr_ref), channel_id=1, source_target_pairs={{0,8},{8,16},{16,24},{24,32},{32,40},{40,48},{48,56},{56,64},{64,7... | collective-permute-start | bytes 196616 | tf_op jit(solution)/shard_map/ppermute | solution.py:515
  125.5 5.6 %collective-permute-start.8 = (f32[32,512]{1,0:T(8,128)S(1)}, f32[32,512]{1,0:T(8,128)S(1)}, u32[]{:S(2)}, u32[]{:S(2)}) collective-permute-start(f32[32,512]{1,0:T(8,128)S(1)} %get-tuple-element.65.sl_ref.refs_10_), channel_id=1, source_target_pairs={{8,0},{16,8},{24,16},{32,24},{40,32},{48,40},{56,48},{64,56},{72,6... | collective-permute-start | bytes 196616 | tf_op jit(solution)/shard_map/ppermute | solution.py:515
  126.8 5.6 %collective-permute-start.9 = (f32[32,512]{1,0:T(8,128)S(1)}, f32[32,512]{1,0:T(8,128)S(1)}, u32[]{:S(2)}, u32[]{:S(2)}) collective-permute-start(f32[32,512]{1,0:T(8,128)S(1)} %get-tuple-element.66.sr_ref.refs_11_), channel_id=1, source_target_pairs={{0,8},{8,16},{16,24},{24,32},{32,40},{40,48},{48,56},{56,64},{64,7... | collective-permute-start | bytes 196616 | tf_op jit(solution)/shard_map/ppermute | solution.py:515
  132.9 5.9 %collective-permute-start.10 = (f32[32,512]{1,0:T(8,128)S(1)}, f32[32,512]{1,0:T(8,128)S(1)}, u32[]{:S(2)}, u32[]{:S(2)}) collective-permute-start(f32[32,512]{1,0:T(8,128)S(1)} %get-tuple-element.68.refs_0_), channel_id=1, source_target_pairs={{8,0},{16,8},{24,16},{32,24},{40,32},{48,40},{56,48},{64,56},{72,6... | collective-permute-start | bytes 196616 | tf_op jit(solution)/shard_map/ppermute | solution.py:515
  134.2 5.9 %collective-permute-start.11 = (f32[32,512]{1,0:T(8,128)S(1)}, f32[32,512]{1,0:T(8,128)S(1)}, u32[]{:S(2)}, u32[]{:S(2)}) collective-permute-start(f32[32,512]{1,0:T(8,128)S(1)} %get-tuple-element.69.refs_1_), channel_id=1, source_target_pairs={{0,8},{8,16},{16,24},{24,32},{32,40},{40,48},{48,56},{56,64},{64,7... | collective-permute-start | bytes 196616 | tf_op jit(solution)/shard_map/ppermute | solution.py:515

commit v5 on v4

--- a/solution.py
+++ b/solution.py
@@ -199,10 +199,9 @@
     width = rows - cols
     spot = one_hot(l_ref[rows : rows + 1, 0:width], count)
     tl, tr = t_ref[cols:rows, :face], t_ref[cols:rows, face:]
-    inner = nt(tl, l_ref[cols:rows, :]) + nt(tr, r_ref[cols:rows, :])
-    pack(out, k, nt(nn(spot, inner), spot), base + 9 * cols)
-    cross = nt(l_ref[0:cols, :], tl) + nt(r_ref[0:cols, :], tr)
-    put(out, base + 2 * cols * (k + 1), nt(cross, spot))
+    inner = nt(nt(l_ref[0:rows, :], tl) + nt(r_ref[0:rows, :], tr), spot)
+    put(out, base + 2 * cols * (k + 1), inner[0:cols])
+    pack(out, k, nn(spot, inner[cols:rows]), base + 9 * cols)
     return lane_sum(t_ref[0:cols, :face] * l_ref[0:cols, :]) + lane_sum(
         t_ref[0:cols, face:] * r_ref[0:cols, :]
     )
@@ -243,21 +242,50 @@
     out[at : at + cols, :] = given_ref[at : at + cols, :] + in_lanes([total], 2)
 
 
-def coarse_kernel(sums_ref, coarse_ref, mat_ref, sl0, sr0, t1, t2, sl2, sr2, t3, sl3,
-                  ol_ref, or_ref, z0_ref, w1c_ref, r1_ref, w0_ref, field_ref, scal_ref,
+def vector(sums_ref, k, cols, count):
+    at = 4 * count + 2 * cols * k
+    return jnp.concatenate([sums_ref[at : at + cols, :], sums_ref[at + cols : at + 2 * cols, :]], axis=1)
+
+
+def at_corners(values, ids_ref):
+    rows = ids_ref.shape[0]
+    spot = one_hot(ids_ref[rows - 8 : rows - 7, 0:LANE], values.shape[1])
+    return nn(values, spot)
+
+
+def spread(local, k, ref, lanes, cols):
+    width = 8 * (2 * k + 1)
+    lane = 8 * (LEVELS - k)
+    wide = nn(local[:, lane : lane + width], ref[cols : cols + width, lanes])
+    return [wide[i : i + cols] for i in range(0, wide.shape[0], cols)]
+
+
+def coarse_kernel(sums_ref, coarse_ref, mat_ref, t1, t3, sl3, ol_ref, or_ref, w0_ref,
                   *, cols, count):
-    base = 4 * count
+    diagonals = 4 * count + 9 * cols
+    face = ol_ref.shape[1]
+    every = slice(0, 2 * face)
+    g0 = nn(vector(sums_ref, 0, cols, count), coarse_ref[...])
+    g1 = nn(vector(sums_ref, 1, cols, count) + nn(g0, unpack(sums_ref, 0, diagonals)), coarse_ref[...])
+    local = at_corners(jnp.concatenate([g0, g1], axis=0), sl3)
+    (p30,) = spread(local[0:cols], 3, t3, every, cols)
+    (p11,) = spread(local[cols:], 1, t1, every, cols)
+    w0 = t3[0:cols, :] + p30 + p11
+    w0_ref[...] = w0
+    v = split_dot(w0, mat_ref[...]) * 0.25
+    ol_ref[...] = v[:, :face]
+    or_ref[...] = v[:, face:]
+
+
+def values_kernel(sums_ref, coarse_ref, nm_ref, sl0, sr0, t1, t2, sl2, sr2, sl3, w0_ref,
+                  z0_ref, w1c_ref, r1_ref, field_ref, scal_ref, gram_ref, back_ref,
+                  *, cols, count):
+    diagonals = 4 * count + 9 * cols
     face = sl0.shape[1]
-
-    def get(at):
-        return jnp.concatenate(
-            [sums_ref[at : at + cols, :], sums_ref[at + cols : at + 2 * cols, :]], axis=1
-        )
-
-    m0, m1, m2 = (unpack(sums_ref, k, base + 9 * cols) for k in range(3))
+    m0, m1, m2 = (unpack(sums_ref, k, diagonals) for k in range(3))
     coarse = coarse_ref[...]
-    c_load, w0x, w1x, w2x = (get(base + 2 * cols * k) for k in range(4))
-    at = base + 8 * cols
+    c_load, w0x, w1x, w2x = (vector(sums_ref, k, cols, count) for k in range(4))
+    at = 4 * count + 8 * cols
     s0, s1, s2 = (sums_ref[at : at + cols, k : k + 1] for k in range(3))
     g0 = nn(c_load, coarse)
     m0g0, m1g0, m2g0 = nn(g0, m0), nn(g0, m1), nn(g0, m2)
@@ -278,36 +306,23 @@
         + be1 * m0g1
     )
     gm = nn(cm, coarse)
-    spot = one_hot(sl3[sl3.shape[0] - 8 : sl3.shape[0] - 7, 0:LANE], count)
-    local = nn(jnp.concatenate([g0, g1, gz1, gm], axis=0), spot)
-
-    def spread(k, ref, first, n, lanes):
-        width = 8 * (2 * k + 1)
-        lane = 8 * (LEVELS - k)
-        wide = nn(local[first * cols : (first + n) * cols, lane : lane + width],
-                  ref[cols : cols + width, lanes])
-        return [wide[i * cols : (i + 1) * cols] for i in range(n)]
-
-    every, right = slice(0, 2 * face), slice(face, 2 * face)
-    p10, p11, p1z = spread(1, t1, 0, 3, every)
-    (p20,) = spread(2, t2, 0, 1, every)
-    (p30,) = spread(3, t3, 0, 1, every)
+    local = at_corners(jnp.concatenate([g0, g1, gz1, gm], axis=0), sl3)
+    every, right, whole = slice(0, 2 * face), slice(face, 2 * face), slice(0, face)
+    (p20,) = spread(local[0:cols], 2, t2, every, cols)
+    (p10,) = spread(local[0:cols], 1, t1, right, cols)
+    (w1c_ref[...],) = spread(local[2 * cols : 3 * cols], 1, t1, every, cols)
     z0_ref[...] = t2[0:cols, :] + p20
-    w0 = t3[0:cols, :] + p30 + p11
-    w0_ref[...] = w0[:, right]
-    w1c_ref[...] = p1z
-    r1_ref[...] = t1[0:cols, right] + p10[:, right] - al0 * w0[:, right]
-    v = split_dot(w0, mat_ref[...]) * 0.25
-    ol_ref[...] = v[:, :face]
-    or_ref[...] = v[:, right]
+    r1_ref[...] = t1[0:cols, right] + p10 - al0 * w0_ref[:, right]
     for own, u, lanes in ((sl0, sl2, slice(0, face)), (sr0, sr2, right)):
-        corner = spread(0, own, 0, 4, slice(0, face))
+        corner = spread(local, 0, own, whole, cols)
+        (u0,) = spread(local[0:cols], 2, u, whole, cols)
         field_ref[0:cols, lanes] = own[0:cols, :] + corner[0]
-        (u0,) = spread(2, u, 0, 1, slice(0, face))
         field_ref[cols : 2 * cols, lanes] = u[0:cols, :] + u0 + corner[1]
         field_ref[2 * cols : 3 * cols, lanes] = corner[2]
         field_ref[3 * cols : 4 * cols, lanes] = corner[3]
     scal_ref[...] = in_lanes([al0, be1, lane_sum(cm * gm)])
+    gram_ref[...] = unpack(sums_ref, 3, diagonals)
+    back_ref[...] = from_order(nm_ref[...], face).astype(BF16)
 
 
 def joined(own_ref, other_ref, mask_ref, left):
@@ -358,7 +373,8 @@
     field_ref[third, face:] = base_ref[third, face:] + ur_ref[...]
     field_ref[fourth, :] = base_ref[fourth, :] + u
     m = whole[:, face:]
-    z0, z1, w0, w1, r1 = z0_ref[:, face:], z1_ref[...], w0_ref[...], w1_ref[...], r1_ref[...]
+    z0, w0 = z0_ref[:, face:], w0_ref[:, face:]
+    z1, w1, r1 = z1_ref[...], w1_ref[...], r1_ref[...]
     q1 = w1 + be1 * w0
     p1 = z1 + be1 * z0
     for i, item in enumerate((z0, z1, m)):
@@ -378,7 +394,7 @@
     out_ref[13 * cols :, :] = jnp.zeros((out_ref.shape[0] - 13 * cols, LANE), F32)
 
 
-def final_kernel(sums_ref, early_ref, scal_ref, field_ref, dual_ref, prev_ref, nm_ref,
+def final_kernel(sums_ref, basis_ref, scal_ref, field_ref, dual_ref, prev_ref, back_ref,
                  block_ref, multi_ref, coef_ref, factor_ref, *, cols, count):
     half = count // 2
     face = dual_ref.shape[1]
@@ -416,7 +432,7 @@
     tiles = stacked * sums_ref[8 * cols : 12 * cols, :] * across
     tiles = sum(tiles[i * cols : (i + 1) * cols] for i in range(4))
     gram = sum(tiles[:, j * cols : (j + 1) * cols] for j in range(4))
-    basis = unpack(early_ref, 3, 4 * count + 9 * cols)
+    basis = basis_ref[...]
     c = 2.0 * g1 - nn(g1, basis)
     coef_ref[...] = c
     gram = gram + nt(c, nn(c, basis) - 2.0 * g1)
@@ -425,15 +441,24 @@
     work = jnp.concatenate([gram, eye], axis=1)
     index = lax.broadcasted_iota(jnp.int32, (cols, 1), 0)
     pivots = jnp.zeros((cols, 1), F32)
-    for k in range(cols):
-        pivot = work[k : k + 1, k : k + 1]
-        pivots = jnp.where(index == k, pivot, pivots)
-        times = jnp.where(index > k, work[:, k : k + 1], 0.0) / pivot
-        work = work - times * work[k : k + 1, :]
+    for k in range(0, cols, 2):
+        first = work[k : k + 1, :]
+        pivot = first[:, k : k + 1]
+        column = work[:, k : k + 1]
+        ratio = first[:, k + 1 : k + 2] / pivot
+        second = work[k + 1 : k + 2, :] - ratio * first
+        follow = second[:, k + 1 : k + 2]
+        other = work[:, k + 1 : k + 2] - ratio * column
+        pivots = jnp.where(index == k, pivot, jnp.where(index == k + 1, follow, pivots))
+        work = (
+            work
+            - (jnp.where(index > k, column, 0.0) / pivot) * first
+            - (jnp.where(index > k + 1, other, 0.0) / follow) * second
+        )
     work = work / jnp.sqrt(pivots)
     factor_ref[...] = jnp.transpose(jnp.where(row <= col, work[:, :cols], 0.0))
     solved = nn(work[:, cols:], final)
-    left = split_dot(solved[:, :face], from_order(nm_ref[...], face).astype(BF16), 3)
+    left = split_dot(solved[:, :face], back_ref[...], 3)
     block_ref[:, :face] = left
     block_ref[:, face:] = solved[:, face:]
 
@@ -559,10 +584,14 @@
 
         wide, part = shape(cols, 2 * face), shape(cols, face)
         sl0, sr0, t1, _, _, t2, sl2, sr2, t3, sl3, _ = chain
-        sl, sr, z0, w1c, r1, w0, base, scal = call(
-            lambda *refs: coarse_kernel(*refs, cols=cols, count=count),
-            (part, part, wide, wide, part, part, shape(4 * cols, rows), shape(cols, LANE)),
-        )(first, coarse_inverse, schur_p, sl0, sr0, t1, t2, sl2, sr2, t3, sl3)
+        sl, sr, w0 = call(
+            lambda *refs: coarse_kernel(*refs, cols=cols, count=count), (part, part, wide)
+        )(first, coarse_inverse, schur_p, t1, t3, sl3)
+        z0, w1c, r1, base, scal, gram, back = call(
+            lambda *refs: values_kernel(*refs, cols=cols, count=count),
+            (wide, wide, part, shape(4 * cols, rows), shape(cols, LANE), shape(count, count),
+             jax.ShapeDtypeStruct((face, face), BF16)),
+        )(first, coarse_inverse, nm_row, sl0, sr0, t1, t2, sl2, sr2, sl3, w0)
         near = exchange(sl, sr)
         n0, z1, ul, ur = call(dual_kernel, (wide, part, part, part))(
             sl, sr, *near, mask, z0, scal, inv_p
@@ -581,7 +610,7 @@
         block, multi, coefficients, factor = call(
             lambda *refs: final_kernel(*refs, cols=cols, count=count),
             (shape(cols, rows), shape(cols, face), shape(cols, count), shape(cols, cols)),
-        )(second, first, scal, field, dual, prev_t, nm_row)
+        )(second, gram, scal, field, dual, prev_t, back)
         return block.T[None, None], multi.T[None, None], coefficients.T, factor
 
     split = (along, ("x", "c"))

time: 201 us -> 201 us (level)
    pallas_call x0 -> x1, Pallas kernels: none -> 3.38 us  [on_device(): call(lambda *refs: values_kernel(*refs, cols=cols, count=count), (wide, w...]
    pallas_call x1, Pallas kernels: 3.97 us -> 1.86 us  [on_device(): call(lambda *refs: coarse_kernel(*refs, cols=cols, count=count), (part, p...]
  transfers between devices with their start and end apart: 12 -> 12, of which waited for: 4 -> 4; matrix products, arithmetic and copies ran while one was open for 0% -> 0% of each run, Pallas kernels for 4% -> 5%
where the time goes in v5:
time: 201 us
  blocking collectives  132 us (66%)
  starting transfers between devices  34.1 us (17%)
  Pallas kernels  27.3 us (14%)
  waiting for transfers between devices  5.8 us (3%)
    all_to_all x6, blocking collectives, swap(): return lax.all_to_all(parts, axes, 0, 0, tiled=True)  132 us
    ppermute x12, starting transfers between devices, exchange(): return (lax.ppermute(sl, along, behind), lax.ppermute(sr, along, ahead))  34.1 us
    pallas_call x1, Pallas kernels, on_device(): call(lambda *refs: final_kernel(*refs, cols=cols, count=count), (shape(co...  6.29 us
    ppermute x12, waiting for transfers between devices, exchange(): return (lax.ppermute(sl, along, behind), lax.ppermute(sr, along, ahead))  5.8 us
  transfers between devices with their start and end apart: 12, of which 4 were waited for; matrix products, arithmetic and copies ran while one was open for 0% of the time, Pallas kernels for 5%

profile of v5, /device:TPU:1, one launch (start us, length us, event | category | flops | bytes accessed | tf_op | source)
XLA Modules:
  0.0 200.7 jit_solution(624896631577265773)
XLA Ops:
  0.7 3.2 %shard_map.120 = (f32[48,512]{1,0:T(8,128)}, f32[48,512]{1,0:T(8,128)}, f32[32,8]{1,0:T(8,128)}) custom-call(bf16[1024,1024]{1,0:T(8,128)(2,1)} %bitcast.21, f32[32,1024]{1,0:T(8,128)} %bitcast.36, f32[8,1024]{1,0:T(8,128)} %bitcast.37, s32[1,512]{1,0:T(1,128)} %bitcast.30, s32[1,8]{1,0:T(1,128)} %bitcast.38), custom_call_target="tpu_custom_call" | custom-call | tf_op jit(solution)/shard_map/pallas_call | solution.py:523
  3.8 4.4 %collective-permute-start.1 = (f32[48,512]{1,0:T(8,128)}, f32[48,512]{1,0:T(8,128)S(1)}, u32[]{:S(2)}, u32[]{:S(2)}) collective-permute-start(f32[48,512]{1,0:T(8,128)} %get-tuple-element.49.refs_1_.refs_4_), channel_id=1, source_target_pairs={{0,8},{8,16},{16,24},{24,32},{32,40},{40,48},{48,56},{56,64},{64,7... | collective-permute-start | bytes 294920 | tf_op jit(solution)/shard_map/ppermute | solution.py:540
  8.2 1.3 collective-permute-start
  9.5 0.0 copy-start.3
  9.6 1.5 shard_map.121.refs_5_.refs_2_.mat_ref
  11.1 0.0 copy-start
  11.1 2.9 %collective-permute-done.refs_2_ = f32[48,512]{1,0:T(8,128)S(1)} collective-permute-done((f32[48,512]{1,0:T(8,128)}, f32[48,512]{1,0:T(8,128)S(1)}, u32[]{:S(2)}, u32[]{:S(2)}) %collective-permute-start) | collective-permute-done | bytes 98336 | tf_op jit(solution)/shard_map/ppermute | solution.py:540
  14.0 0.5 shard_map.122
  14.5 1.3 collective-permute-start.2
  15.8 0.0 copy-start.4
  15.8 0.0 copy-start.8
  15.8 4.6 %collective-permute-start.3 = (f32[64,512]{1,0:T(8,128)S(1)}, f32[64,512]{1,0:T(8,128)S(1)}, u32[]{:S(2)}, u32[]{:S(2)}) collective-permute-start(f32[64,512]{1,0:T(8,128)S(1)} %get-tuple-element.51.refs_1_.refs_5_), channel_id=1, source_target_pairs={{0,8},{8,16},{16,24},{24,32},{32,40},{40,48},{48,56},{56,64},{64,7... | collective-permute-start | bytes 393224 | tf_op jit(solution)/shard_map/ppermute | solution.py:540
  20.4 1.5 shard_map.124.refs_5_.mat_ref.refs_6_
  21.9 0.0 copy-start.7
  21.9 2.1 %shard_map.123 = (bf16[1024,256]{1,0:T(8,128)(2,1)S(1)}, bf16[256,1024]{1,0:T(8,128)(2,1)S(1)}, f32[1,1024]{1,0:T(1,128)S(1)}, f32[256,256]{1,0:T(8,128)S(1)}) custom-call(bf16[1024,256]{1,0:T(8,128)(2,1)S(1)} %bitcast.28, s32[1,512]{1,0:T(1,128)S(1)} %bitcast.33, f32[1,1024]{1,0:T(1,128)S(1)} %bitcast.35), custom_call_target="tpu_custom_call" | custom-call | tf_op jit(solution)/shard_map/pallas_call | solution.py:559
  24.0 0.0 collective-permute-done.2.refs_2_
  24.1 0.0 collective-permute-done.3.refs_3_
  24.1 0.5 shard_map.125
  24.6 1.3 collective-permute-start.4
  25.9 5.1 %collective-permute-start.5 = (f32[80,512]{1,0:T(8,128)S(1)}, f32[80,512]{1,0:T(8,128)S(1)}, u32[]{:S(2)}, u32[]{:S(2)}) collective-permute-start(f32[80,512]{1,0:T(8,128)S(1)} %get-tuple-element.59.refs_8_.refs_1_), channel_id=1, source_target_pairs={{0,8},{8,16},{16,24},{24,32},{32,40},{40,48},{48,56},{56,64},{64,7... | collective-permute-start | bytes 491528 | tf_op jit(solution)/shard_map/ppermute | solution.py:540
  31.0 1.9 shard_map.126.refs_0_
  32.9 0.3 collective-permute-done.5.refs_3_
  33.2 0.6 shard_map.127
  33.8 1.5 shard_map.128
  35.3 38.9 %all_to_all.30.parts_ref = f32[64,24,128]{2,1,0:T(8,128)S(1)} all-to-all(f32[64,24,128]{2,1,0:T(8,128)S(1)} %bitcast.23), channel_id=1, replica_groups=mesh['y'=4,'zh'=8,'zl'=2,'x'=4,'c'=2] {'y','zl','x','c'}, dimensions={0} | all-to-all | bytes 1572864 | tf_op jit(solution)/shard_map/all_to_all | solution.py:473
  74.1 0.1 shard_map.129
  74.2 18.1 %all_to_all.31.parts_ref = f32[8,24,128]{2,1,0:T(8,128)S(1)} all-to-all(f32[8,24,128]{2,1,0:T(8,128)S(1)} %shard_map.129), channel_id=1, replica_groups=mesh['y'=4,'zh'=8,'zl'=2,'x'=4,'c'=2] {'zh'}, dimensions={0} | all-to-all | bytes 196608 | tf_op jit(solution)/shard_map/all_to_all | solution.py:473
  92.3 0.1 shard_map.130
  92.4 22.1 %all_to_all.32 = f32[64,24,128]{2,1,0:T(8,128)S(1)} all-to-all(f32[64,24,128]{2,1,0:T(8,128)S(1)} %shard_map.130), channel_id=1, replica_groups=mesh['y'=4,'zh'=8,'zl'=2,'x'=4,'c'=2] {'y','zl','x','c'}, dimensions={0} | all-to-all | bytes 1572864 | tf_op jit(solution)/shard_map/all_to_all | solution.py:473
  114.5 1.9 shard_map.131
  116.3 1.3 collective-permute-start.6
  117.6 4.0 %collective-permute-start.7 = (f32[32,512]{1,0:T(8,128)S(1)}, f32[32,512]{1,0:T(8,128)S(1)}, u32[]{:S(2)}, u32[]{:S(2)}) collective-permute-start(f32[32,512]{1,0:T(8,128)S(1)} %get-tuple-element.64.sr_ref), channel_id=1, source_target_pairs={{0,8},{8,16},{16,24},{24,32},{32,40},{40,48},{48,56},{56,64},{64,7... | collective-permute-start | bytes 196616 | tf_op jit(solution)/shard_map/ppermute | solution.py:540
  121.6 3.4 %shard_map.132 = (f32[32,1024]{1,0:T(8,128)S(1)}, f32[32,1024]{1,0:T(8,128)S(1)}, f32[32,512]{1,0:T(8,128)S(1)}, f32[128,1024]{1,0:T(8,128)S(1)}, f32[32,128]{1,...) custom-call(f32[1536,128]{1,0:T(8,128)S(1)} %bitcast.25, f32[256,256]{1,0:T(8,128)S(1)} %copy-done.2, ...), custom_call_target="tpu_custom_call" | custom-call | tf_op jit(solution)/shard_map/pallas_call | solution.py:590
  125.0 0.0 collective-permute-done.6.nl_ref
  125.0 0.5 shard_map.133
  125.5 1.3 collective-permute-start.8
  126.9 4.0 %collective-permute-start.9 = (f32[32,512]{1,0:T(8,128)S(1)}, f32[32,512]{1,0:T(8,128)S(1)}, u32[]{:S(2)}, u32[]{:S(2)}) collective-permute-start(f32[32,512]{1,0:T(8,128)S(1)} %get-tuple-element.69.sr_ref.refs_11_), channel_id=1, source_target_pairs={{0,8},{8,16},{16,24},{24,32},{32,40},{40,48},{48,56},{56,64},{64,7... | collective-permute-start | bytes 196616 | tf_op jit(solution)/shard_map/ppermute | solution.py:540
  130.9 1.3 collective-permute-done.9.pr_ref
  132.2 0.5 shard_map.134
  132.6 1.3 collective-permute-start.10
  133.9 4.3 %collective-permute-start.11 = (f32[32,512]{1,0:T(8,128)S(1)}, f32[32,512]{1,0:T(8,128)S(1)}, u32[]{:S(2)}, u32[]{:S(2)}) collective-permute-start(f32[32,512]{1,0:T(8,128)S(1)} %get-tuple-element.72.refs_1_), channel_id=1, source_target_pairs={{0,8},{8,16},{16,24},{24,32},{32,40},{40,48},{48,56},{56,64},{64,7... | collective-permute-start | bytes 196616 | tf_op jit(solution)/shard_map/ppermute | solution.py:540
  138.3 1.3 collective-permute-done.11.refs_3_
  139.6 1.4 shard_map.135
  141.0 23.9 %all_to_all.33.parts_ref = f32[64,8,128]{2,1,0:T(8,128)S(1)} all-to-all(f32[64,8,128]{2,1,0:T(8,128)S(1)} %bitcast.29), channel_id=1, replica_groups=mesh['y'=4,'zh'=8,'zl'=2,'x'=4,'c'=2] {'y','zl','x','c'}, dimensions={0} | all-to-all | bytes 524288 | tf_op jit(solution)/shard_map/all_to_all | solution.py:473
  164.9 0.1 shard_map.136
  164.9 14.4 %all_to_all.34.parts_ref = f32[8,8,128]{2,1,0:T(8,128)S(1)} all-to-all(f32[8,8,128]{2,1,0:T(8,128)S(1)} %shard_map.136), channel_id=1, replica_groups=mesh['y'=4,'zh'=8,'zl'=2,'x'=4,'c'=2] {'zh'}, dimensions={0} | all-to-all | bytes 65536 | tf_op jit(solution)/shard_map/all_to_all | solution.py:473
  179.4 15.0 %all_to_all.35 = f32[64,8,128]{2,1,0:T(8,128)S(1)} all-to-all(f32[64,8,128]{2,1,0:T(8,128)S(1)} %shard_map.137), channel_id=1, replica_groups=mesh['y'=4,'zh'=8,'zl'=2,'x'=4,'c'=2] {'y','zl','x','c'}, dimensions={0} | all-to-all | bytes 524288 | tf_op jit(solution)/shard_map/all_to_all | solution.py:473
  194.4 6.3 %shard_map.138 = (f32[32,1024]{1,0:T(8,128)}, f32[32,512]{1,0:T(8,128)}, f32[32,256]{1,0:T(8,128)}, f32[32,32]{1,0:T(8,128)}) custom-call(f32[512,128]{1,0:T(8,128)S(1)} %bitcast.27, f32[256,256]{1,0:T(8,128)S(1)} %get-tuple-element.81.refs_1_, f32[32,128]{1,0:T(8,128)S(1)} %get-tuple-element.67.scal_ref.refs_7_.refs_2_, ...), custom_call_target="tpu_custom_call" | custom-call | tf_op jit(solution)/shard_map/pallas_call | solution.py:610
  (21 shorter events, 0.1 us)
Async XLA Ops:
  0.6 8.9 %copy-start.6 = (s32[1,1,512]{2,1,0:T(1,128)S(1)}, s32[1,1,512]{2,1,0:T(1,128)}, u32[]{:S(2)}) copy-start(s32[1,1,512]{2,1,0:T(1,128)} %param.14) | copy-start | bytes 6148
  0.6 8.9 %copy-start.1 = (bf16[1,1,1024,1024]{3,2,1,0:T(8,128)(2,1)S(1)}, bf16[1,1,1024,1024]{3,2,1,0:T(8,128)(2,1)}, u32[]{:S(2)}) copy-start(bf16[1,1,1024,1024]{3,2,1,0:T(8,128)(2,1)} %param.10) | copy-start | bytes 6291460
  3.8 7.3 %collective-permute-start.1 = (f32[48,512]{1,0:T(8,128)}, f32[48,512]{1,0:T(8,128)S(1)}, u32[]{:S(2)}, u32[]{:S(2)}) collective-permute-start(f32[48,512]{1,0:T(8,128)} %get-tuple-element.49.refs_1_.refs_4_), channel_id=1, source_target_pairs={{0,8},{8,16},{16,24},{24,32},{32,40},{40,48},{48,56},{56,64},{64,7... | collective-permute-start | bytes 294920 | tf_op jit(solution)/shard_map/ppermute | solution.py:540
  8.2 5.8 %collective-permute-start = (f32[48,512]{1,0:T(8,128)}, f32[48,512]{1,0:T(8,128)S(1)}, u32[]{:S(2)}, u32[]{:S(2)}) collective-permute-start(f32[48,512]{1,0:T(8,128)} %get-tuple-element.47.refs_0_.refs_3_), channel_id=1, source_target_pairs={{8,0},{16,8},{24,16},{32,24},{40,32},{48,40},{56,48},{64,56},{72,6... | collective-permute-start | bytes 294920 | tf_op jit(solution)/shard_map/ppermute | solution.py:540
  9.5 4.4 %copy-start.3 = (f32[48,512]{1,0:T(8,128)S(1)}, f32[48,512]{1,0:T(8,128)}, u32[]{:S(2)}) copy-start(f32[48,512]{1,0:T(8,128)} %get-tuple-element.47.refs_0_.refs_3_) | copy-start | bytes 294916
  9.6 4.4 %copy-start.5 = (f32[48,512]{1,0:T(8,128)S(1)}, f32[48,512]{1,0:T(8,128)}, u32[]{:S(2)}) copy-start(f32[48,512]{1,0:T(8,128)} %get-tuple-element.49.refs_1_.refs_4_) | copy-start | bytes 294916
  11.1 9.4 %copy-start = (bf16[1,1,1024,1024]{3,2,1,0:T(8,128)(2,1)S(1)}, bf16[1,1,1024,1024]{3,2,1,0:T(8,128)(2,1)}, u32[]{:S(2)}) copy-start(bf16[1,1,1024,1024]{3,2,1,0:T(8,128)(2,1)} %param.9) | copy-start | bytes 6291460
  14.5 9.6 %collective-permute-start.2 = (f32[64,512]{1,0:T(8,128)S(1)}, f32[64,512]{1,0:T(8,128)S(1)}, u32[]{:S(2)}, u32[]{:S(2)}) collective-permute-start(f32[64,512]{1,0:T(8,128)S(1)} %get-tuple-element.50.refs_0_.refs_4_), channel_id=1, source_target_pairs={{8,0},{16,8},{24,16},{32,24},{40,32},{48,40},{56,48},{64,56},{72,6... | collective-permute-start | bytes 393224 | tf_op jit(solution)/shard_map/ppermute | solution.py:540
  15.8 6.1 %copy-start.4 = (bf16[1,1,1024,256]{3,2,1,0:T(8,128)(2,1)S(1)}, bf16[1,1,1024,256]{3,2,1,0:T(8,128)(2,1)}, u32[]{:S(2)}) copy-start(bf16[1,1,1024,256]{3,2,1,0:T(8,128)(2,1)} %param.16) | copy-start | bytes 1572868
  15.8 6.1 %copy-start.8 = (f32[1,1,1024]{2,1,0:T(1,128)S(1)}, f32[1,1,1024]{2,1,0:T(1,128)}, u32[]{:S(2)}) copy-start(f32[1,1,1024]{2,1,0:T(1,128)} %param.17) | copy-start | bytes 12292
  15.8 8.3 %collective-permute-start.3 = (f32[64,512]{1,0:T(8,128)S(1)}, f32[64,512]{1,0:T(8,128)S(1)}, u32[]{:S(2)}, u32[]{:S(2)}) collective-permute-start(f32[64,512]{1,0:T(8,128)S(1)} %get-tuple-element.51.refs_1_.refs_5_), channel_id=1, source_target_pairs={{0,8},{8,16},{16,24},{24,32},{32,40},{40,48},{48,56},{56,64},{64,7... | collective-permute-start | bytes 393224 | tf_op jit(solution)/shard_map/ppermute | solution.py:540
  21.9 9.1 %copy-start.7 = (f32[32,8]{1,0:T(8,128)S(1)}, f32[32,8]{1,0:T(8,128)}, u32[]{:S(2)}) copy-start(f32[32,8]{1,0:T(8,128)} %get-tuple-element.48.refs_1_) | copy-start | bytes 3076
  24.6 8.3 %collective-permute-start.4 = (f32[80,512]{1,0:T(8,128)S(1)}, f32[80,512]{1,0:T(8,128)S(1)}, u32[]{:S(2)}, u32[]{:S(2)}) collective-permute-start(f32[80,512]{1,0:T(8,128)S(1)} %get-tuple-element.58.refs_7_.refs_0_), channel_id=1, source_target_pairs={{8,0},{16,8},{24,16},{32,24},{40,32},{48,40},{56,48},{64,56},{72,6... | collective-permute-start | bytes 491528 | tf_op jit(solution)/shard_map/ppermute | solution.py:540
  25.9 7.3 %collective-permute-start.5 = (f32[80,512]{1,0:T(8,128)S(1)}, f32[80,512]{1,0:T(8,128)S(1)}, u32[]{:S(2)}, u32[]{:S(2)}) collective-permute-start(f32[80,512]{1,0:T(8,128)S(1)} %get-tuple-element.59.refs_8_.refs_1_), channel_id=1, source_target_pairs={{0,8},{8,16},{16,24},{24,32},{32,40},{40,48},{48,56},{56,64},{64,7... | collective-permute-start | bytes 491528 | tf_op jit(solution)/shard_map/ppermute | solution.py:540
  74.1 40.3 %copy-start.2 = (f32[256,256]{1,0:T(8,128)S(1)}, f32[256,256]{1,0:T(8,128)}, u32[]{:S(2)}) copy-start(f32[256,256]{1,0:T(8,128)} %refs_1_.3) | copy-start | bytes 786436
  116.3 8.7 %collective-permute-start.6 = (f32[32,512]{1,0:T(8,128)S(1)}, f32[32,512]{1,0:T(8,128)S(1)}, u32[]{:S(2)}, u32[]{:S(2)}) collective-permute-start(f32[32,512]{1,0:T(8,128)S(1)} %get-tuple-element.63.sl_ref), channel_id=1, source_target_pairs={{8,0},{16,8},{24,16},{32,24},{40,32},{48,40},{56,48},{64,56},{72,6... | collective-permute-start | bytes 196616 | tf_op jit(solution)/shard_map/ppermute | solution.py:540
  117.6 7.4 %collective-permute-start.7 = (f32[32,512]{1,0:T(8,128)S(1)}, f32[32,512]{1,0:T(8,128)S(1)}, u32[]{:S(2)}, u32[]{:S(2)}) collective-permute-start(f32[32,512]{1,0:T(8,128)S(1)} %get-tuple-element.64.sr_ref), channel_id=1, source_target_pairs={{0,8},{8,16},{16,24},{24,32},{32,40},{40,48},{48,56},{56,64},{64,7... | collective-permute-start | bytes 196616 | tf_op jit(solution)/shard_map/ppermute | solution.py:540
  125.5 5.3 %collective-permute-start.8 = (f32[32,512]{1,0:T(8,128)S(1)}, f32[32,512]{1,0:T(8,128)S(1)}, u32[]{:S(2)}, u32[]{:S(2)}) collective-permute-start(f32[32,512]{1,0:T(8,128)S(1)} %get-tuple-element.68.sl_ref.refs_10_), channel_id=1, source_target_pairs={{8,0},{16,8},{24,16},{32,24},{40,32},{48,40},{56,48},{64,56},{72,6... | collective-permute-start | bytes 196616 | tf_op jit(solution)/shard_map/ppermute | solution.py:540
  126.9 5.3 %collective-permute-start.9 = (f32[32,512]{1,0:T(8,128)S(1)}, f32[32,512]{1,0:T(8,128)S(1)}, u32[]{:S(2)}, u32[]{:S(2)}) collective-permute-start(f32[32,512]{1,0:T(8,128)S(1)} %get-tuple-element.69.sr_ref.refs_11_), channel_id=1, source_target_pairs={{0,8},{8,16},{16,24},{24,32},{32,40},{40,48},{48,56},{56,64},{64,7... | collective-permute-start | bytes 196616 | tf_op jit(solution)/shard_map/ppermute | solution.py:540
  132.6 5.6 %collective-permute-start.10 = (f32[32,512]{1,0:T(8,128)S(1)}, f32[32,512]{1,0:T(8,128)S(1)}, u32[]{:S(2)}, u32[]{:S(2)}) collective-permute-start(f32[32,512]{1,0:T(8,128)S(1)} %get-tuple-element.71.refs_0_), channel_id=1, source_target_pairs={{8,0},{16,8},{24,16},{32,24},{40,32},{48,40},{56,48},{64,56},{72,6... | collective-permute-start | bytes 196616 | tf_op jit(solution)/shard_map/ppermute | solution.py:540
  133.9 5.6 %collective-permute-start.11 = (f32[32,512]{1,0:T(8,128)S(1)}, f32[32,512]{1,0:T(8,128)S(1)}, u32[]{:S(2)}, u32[]{:S(2)}) collective-permute-start(f32[32,512]{1,0:T(8,128)S(1)} %get-tuple-element.72.refs_1_), channel_id=1, source_target_pairs={{0,8},{8,16},{16,24},{24,32},{32,40},{40,48},{48,56},{56,64},{64,7... | collective-permute-start | bytes 196616 | tf_op jit(solution)/shard_map/ppermute | solution.py:540

commit v6 on v5

--- a/solution.py
+++ b/solution.py
@@ -37,15 +37,32 @@
     )
 
 
-def split_dot(t, mat, parts=2):
+def pieces_of(t, parts, axis):
     pieces = []
     for _ in range(parts - 1):
         pieces.append(t.astype(BF16).astype(F32))
         t = t - pieces[-1]
-    wide = jnp.concatenate(pieces + [t], axis=0).astype(BF16)
-    wide = jnp.dot(wide, mat, preferred_element_type=F32)
+    return jnp.concatenate(pieces + [t], axis=axis).astype(BF16)
+
+
+def split_dot(t, mat, parts=2):
+    wide = jnp.dot(pieces_of(t, parts, 0), mat, preferred_element_type=F32)
     rows = t.shape[0]
     return sum(wide[i * rows : (i + 1) * rows] for i in range(1, parts)) + wide[:rows]
+
+
+def split_nt(t, mat):
+    rows = t.shape[0]
+    wide = lax.dot_general(
+        pieces_of(t, 3, 0), mat, (((1,), (1,)), ((), ())), preferred_element_type=F32
+    )
+    return wide[2 * rows :] + wide[rows : 2 * rows] + wide[:rows]
+
+
+def split_right(mat, t):
+    cols = t.shape[1]
+    wide = jnp.dot(mat, pieces_of(t, 3, 1), preferred_element_type=F32)
+    return wide[:, 2 * cols :] + wide[:, cols : 2 * cols] + wide[:, :cols]
 
 
 def to_order(nm_row, face):
@@ -151,7 +168,7 @@
 
 def one_hot(ids, count):
     dof = lax.broadcasted_iota(jnp.int32, (count, ids.shape[1]), 0).astype(F32)
-    return (ids == dof).astype(F32)
+    return (ids == dof).astype(F32).astype(BF16)
 
 
 def lower(half):
@@ -199,9 +216,9 @@
     width = rows - cols
     spot = one_hot(l_ref[rows : rows + 1, 0:width], count)
     tl, tr = t_ref[cols:rows, :face], t_ref[cols:rows, face:]
-    inner = nt(nt(l_ref[0:rows, :], tl) + nt(r_ref[0:rows, :], tr), spot)
+    inner = split_nt(nt(l_ref[0:rows, :], tl) + nt(r_ref[0:rows, :], tr), spot)
     put(out, base + 2 * cols * (k + 1), inner[0:cols])
-    pack(out, k, nn(spot, inner[cols:rows]), base + 9 * cols)
+    pack(out, k, split_right(spot, inner[cols:rows]), base + 9 * cols)
     return lane_sum(t_ref[0:cols, :face] * l_ref[0:cols, :]) + lane_sum(
         t_ref[0:cols, face:] * r_ref[0:cols, :]
     )
@@ -229,7 +246,7 @@
     out[at:, :] = jnp.zeros((out.shape[0] - at, LANE), F32)
     own = sl0_ref.shape[0] - cols - 8
     spot = one_hot(sl0_ref[cols + own : cols + own + 1, 0:own], count)
-    put(out, base, nt(cl_ref[...], spot))
+    put(out, base, split_nt(cl_ref[...], spot))
     sums = [level_moments(out, refs[3 * k : 3 * k + 3], k, cols, count) for k in range(2)]
     pack(out, 3, gram_ref[...], at + cols)
     out[at : at + cols, :] = in_lanes(sums)
@@ -250,7 +267,7 @@
 def at_corners(values, ids_ref):
     rows = ids_ref.shape[0]
     spot = one_hot(ids_ref[rows - 8 : rows - 7, 0:LANE], values.shape[1])
-    return nn(values, spot)
+    return split_dot(values, spot, 3)
 
 
 def spread(local, k, ref, lanes, cols):
@@ -440,21 +457,17 @@
     final = primal - split_dot(c, prev_ref[...], 3)
     work = jnp.concatenate([gram, eye], axis=1)
     index = lax.broadcasted_iota(jnp.int32, (cols, 1), 0)
-    pivots = jnp.zeros((cols, 1), F32)
-    for k in range(0, cols, 2):
-        first = work[k : k + 1, :]
-        pivot = first[:, k : k + 1]
-        column = work[:, k : k + 1]
-        ratio = first[:, k + 1 : k + 2] / pivot
-        second = work[k + 1 : k + 2, :] - ratio * first
-        follow = second[:, k + 1 : k + 2]
-        other = work[:, k + 1 : k + 2] - ratio * column
-        pivots = jnp.where(index == k, pivot, jnp.where(index == k + 1, follow, pivots))
-        work = (
-            work
-            - (jnp.where(index > k, column, 0.0) / pivot) * first
-            - (jnp.where(index > k + 1, other, 0.0) / follow) * second
-        )
+    pivots = jnp.zeros(work.shape, F32)
+    for start in range(0, cols, 8):
+        wide = [jnp.broadcast_to(work[:, start + j : start + j + 1], work.shape) for j in range(8)]
+        for j in range(8):
+            k = start + j
+            pivot = wide[j][k : k + 1, :]
+            pivots = jnp.where(index == k, pivot, pivots)
+            times = jnp.where(index > k, wide[j], 0.0) * (1.0 / pivot)
+            for i in range(j + 1, 8):
+                wide[i] = wide[i] - times * wide[i][k : k + 1, :]
+            work = work - times * work[k : k + 1, :]
     work = work / jnp.sqrt(pivots)
     factor_ref[...] = jnp.transpose(jnp.where(row <= col, work[:, :cols], 0.0))
     solved = nn(work[:, cols:], final)

time: 201 us -> 198 us (0.985)
  Pallas kernels: 27.3 us -> 23.7 us
    pallas_call x1, Pallas kernels: 6.29 us -> 3.21 us  [on_device(): call(lambda *refs: final_kernel(*refs, cols=cols, count=count), (shape(co...]
where the time goes in v6:
time: 198 us; the launch traced here: 197 us
  blocking collectives  132 us (67%)
  starting transfers between devices  34.3 us (17%)
  Pallas kernels  23.7 us (12%)
  waiting for transfers between devices  5.87 us (3%)
    all_to_all x6, blocking collectives, swap(): return lax.all_to_all(parts, axes, 0, 0, tiled=True)  132 us
    ppermute x12, starting transfers between devices, exchange(): return (lax.ppermute(sl, along, behind), lax.ppermute(sr, along, ahead))  34.3 us
    ppermute x12, waiting for transfers between devices, exchange(): return (lax.ppermute(sl, along, behind), lax.ppermute(sr, along, ahead))  5.87 us
  transfers between devices with their start and end apart: 12, of which 4 were waited for; matrix products, arithmetic and copies ran while one was open for 0% of the time, Pallas kernels for 5%

profile of v6, /device:TPU:1, one launch (start us, length us, event | category | flops | bytes accessed | tf_op | source)
XLA Modules:
  0.0 197.3 jit_solution(6776030928552760795)
XLA Ops:
  0.7 3.2 %shard_map.120 = (f32[48,512]{1,0:T(8,128)}, f32[48,512]{1,0:T(8,128)}, f32[32,8]{1,0:T(8,128)}) custom-call(bf16[1024,1024]{1,0:T(8,128)(2,1)} %bitcast.21, f32[32,1024]{1,0:T(8,128)} %bitcast.36, f32[8,1024]{1,0:T(8,128)} %bitcast.37, s32[1,512]{1,0:T(1,128)} %bitcast.30, s32[1,8]{1,0:T(1,128)} %bitcast.38), custom_call_target="tpu_custom_call" | custom-call | tf_op jit(solution)/shard_map/pallas_call | solution.py:536
  3.8 4.4 %collective-permute-start.1 = (f32[48,512]{1,0:T(8,128)}, f32[48,512]{1,0:T(8,128)S(1)}, u32[]{:S(2)}, u32[]{:S(2)}) collective-permute-start(f32[48,512]{1,0:T(8,128)} %get-tuple-element.49.refs_1_.refs_4_), channel_id=1, source_target_pairs={{0,8},{8,16},{16,24},{24,32},{32,40},{40,48},{48,56},{56,64},{64,7... | collective-permute-start | bytes 294920 | tf_op jit(solution)/shard_map/ppermute | solution.py:553
  8.2 1.3 collective-permute-start
  9.5 0.0 copy-start.3
  9.6 1.5 shard_map.121.refs_5_.refs_2_.mat_ref
  11.1 0.0 copy-start
  11.1 2.9 %collective-permute-done.refs_2_ = f32[48,512]{1,0:T(8,128)S(1)} collective-permute-done((f32[48,512]{1,0:T(8,128)}, f32[48,512]{1,0:T(8,128)S(1)}, u32[]{:S(2)}, u32[]{:S(2)}) %collective-permute-start) | collective-permute-done | bytes 98336 | tf_op jit(solution)/shard_map/ppermute | solution.py:553
  14.0 0.5 shard_map.122
  14.5 1.3 collective-permute-start.2
  15.8 0.0 copy-start.4
  15.8 0.0 copy-start.8
  15.8 4.6 %collective-permute-start.3 = (f32[64,512]{1,0:T(8,128)S(1)}, f32[64,512]{1,0:T(8,128)S(1)}, u32[]{:S(2)}, u32[]{:S(2)}) collective-permute-start(f32[64,512]{1,0:T(8,128)S(1)} %get-tuple-element.51.refs_1_.refs_5_), channel_id=1, source_target_pairs={{0,8},{8,16},{16,24},{24,32},{32,40},{40,48},{48,56},{56,64},{64,7... | collective-permute-start | bytes 393224 | tf_op jit(solution)/shard_map/ppermute | solution.py:553
  20.4 1.5 shard_map.124.refs_5_.mat_ref.refs_6_
  21.9 0.0 copy-start.7
  21.9 2.1 %shard_map.123 = (bf16[1024,256]{1,0:T(8,128)(2,1)S(1)}, bf16[256,1024]{1,0:T(8,128)(2,1)S(1)}, f32[1,1024]{1,0:T(1,128)S(1)}, f32[256,256]{1,0:T(8,128)S(1)}) custom-call(bf16[1024,256]{1,0:T(8,128)(2,1)S(1)} %bitcast.28, s32[1,512]{1,0:T(1,128)S(1)} %bitcast.33, f32[1,1024]{1,0:T(1,128)S(1)} %bitcast.35), custom_call_target="tpu_custom_call" | custom-call | tf_op jit(solution)/shard_map/pallas_call | solution.py:572
  24.0 0.0 collective-permute-done.2.refs_2_
  24.1 0.0 collective-permute-done.3.refs_3_
  24.1 0.5 shard_map.125
  24.6 1.3 collective-permute-start.4
  25.9 5.1 %collective-permute-start.5 = (f32[80,512]{1,0:T(8,128)S(1)}, f32[80,512]{1,0:T(8,128)S(1)}, u32[]{:S(2)}, u32[]{:S(2)}) collective-permute-start(f32[80,512]{1,0:T(8,128)S(1)} %get-tuple-element.59.refs_8_.refs_1_), channel_id=1, source_target_pairs={{0,8},{8,16},{16,24},{24,32},{32,40},{40,48},{48,56},{56,64},{64,7... | collective-permute-start | bytes 491528 | tf_op jit(solution)/shard_map/ppermute | solution.py:553
  31.0 1.8 shard_map.126.refs_0_
  32.8 0.0 collective-permute-done.4.refs_2_
  32.8 0.4 collective-permute-done.5.refs_3_
  33.2 0.6 shard_map.127
  33.8 1.0 shard_map.128
  34.8 38.9 %all_to_all.30.parts_ref = f32[64,24,128]{2,1,0:T(8,128)S(1)} all-to-all(f32[64,24,128]{2,1,0:T(8,128)S(1)} %bitcast.23), channel_id=1, replica_groups=mesh['y'=4,'zh'=8,'zl'=2,'x'=4,'c'=2] {'y','zl','x','c'}, dimensions={0} | all-to-all | bytes 1572864 | tf_op jit(solution)/shard_map/all_to_all | solution.py:486
  73.7 0.1 shard_map.129
  73.8 18.1 %all_to_all.31.parts_ref = f32[8,24,128]{2,1,0:T(8,128)S(1)} all-to-all(f32[8,24,128]{2,1,0:T(8,128)S(1)} %shard_map.129), channel_id=1, replica_groups=mesh['y'=4,'zh'=8,'zl'=2,'x'=4,'c'=2] {'zh'}, dimensions={0} | all-to-all | bytes 196608 | tf_op jit(solution)/shard_map/all_to_all | solution.py:486
  91.9 0.1 shard_map.130
  91.9 22.1 %all_to_all.32 = f32[64,24,128]{2,1,0:T(8,128)S(1)} all-to-all(f32[64,24,128]{2,1,0:T(8,128)S(1)} %shard_map.130), channel_id=1, replica_groups=mesh['y'=4,'zh'=8,'zl'=2,'x'=4,'c'=2] {'y','zl','x','c'}, dimensions={0} | all-to-all | bytes 1572864 | tf_op jit(solution)/shard_map/all_to_all | solution.py:486
  114.0 1.8 shard_map.131
  115.8 1.3 collective-permute-start.6
  117.1 4.2 %collective-permute-start.7 = (f32[32,512]{1,0:T(8,128)S(1)}, f32[32,512]{1,0:T(8,128)S(1)}, u32[]{:S(2)}, u32[]{:S(2)}) collective-permute-start(f32[32,512]{1,0:T(8,128)S(1)} %get-tuple-element.64.sr_ref), channel_id=1, source_target_pairs={{0,8},{8,16},{16,24},{24,32},{32,40},{40,48},{48,56},{56,64},{64,7... | collective-permute-start | bytes 196616 | tf_op jit(solution)/shard_map/ppermute | solution.py:553
  121.3 3.4 %shard_map.132 = (f32[32,1024]{1,0:T(8,128)S(1)}, f32[32,1024]{1,0:T(8,128)S(1)}, f32[32,512]{1,0:T(8,128)S(1)}, f32[128,1024]{1,0:T(8,128)S(1)}, f32[32,128]{1,...) custom-call(f32[1536,128]{1,0:T(8,128)S(1)} %bitcast.25, f32[256,256]{1,0:T(8,128)S(1)} %copy-done.2, ...), custom_call_target="tpu_custom_call" | custom-call | tf_op jit(solution)/shard_map/pallas_call | solution.py:603
  124.8 0.5 shard_map.133
  125.3 1.3 collective-permute-start.8
  126.6 4.0 %collective-permute-start.9 = (f32[32,512]{1,0:T(8,128)S(1)}, f32[32,512]{1,0:T(8,128)S(1)}, u32[]{:S(2)}, u32[]{:S(2)}) collective-permute-start(f32[32,512]{1,0:T(8,128)S(1)} %get-tuple-element.69.sr_ref.refs_11_), channel_id=1, source_target_pairs={{0,8},{8,16},{16,24},{24,32},{32,40},{40,48},{48,56},{56,64},{64,7... | collective-permute-start | bytes 196616 | tf_op jit(solution)/shard_map/ppermute | solution.py:553
  130.6 1.3 collective-permute-done.9.pr_ref
  131.9 0.5 shard_map.134
  132.4 1.3 collective-permute-start.10
  133.7 4.3 %collective-permute-start.11 = (f32[32,512]{1,0:T(8,128)S(1)}, f32[32,512]{1,0:T(8,128)S(1)}, u32[]{:S(2)}, u32[]{:S(2)}) collective-permute-start(f32[32,512]{1,0:T(8,128)S(1)} %get-tuple-element.72.refs_1_), channel_id=1, source_target_pairs={{0,8},{8,16},{16,24},{24,32},{32,40},{40,48},{48,56},{56,64},{64,7... | collective-permute-start | bytes 196616 | tf_op jit(solution)/shard_map/ppermute | solution.py:553
  138.0 1.3 collective-permute-done.11.refs_3_
  139.3 1.4 shard_map.135
  140.7 23.9 %all_to_all.33.parts_ref = f32[64,8,128]{2,1,0:T(8,128)S(1)} all-to-all(f32[64,8,128]{2,1,0:T(8,128)S(1)} %bitcast.29), channel_id=1, replica_groups=mesh['y'=4,'zh'=8,'zl'=2,'x'=4,'c'=2] {'y','zl','x','c'}, dimensions={0} | all-to-all | bytes 524288 | tf_op jit(solution)/shard_map/all_to_all | solution.py:486
  164.6 0.1 shard_map.136
  164.7 14.4 %all_to_all.34.parts_ref = f32[8,8,128]{2,1,0:T(8,128)S(1)} all-to-all(f32[8,8,128]{2,1,0:T(8,128)S(1)} %shard_map.136), channel_id=1, replica_groups=mesh['y'=4,'zh'=8,'zl'=2,'x'=4,'c'=2] {'zh'}, dimensions={0} | all-to-all | bytes 65536 | tf_op jit(solution)/shard_map/all_to_all | solution.py:486
  179.1 15.0 %all_to_all.35 = f32[64,8,128]{2,1,0:T(8,128)S(1)} all-to-all(f32[64,8,128]{2,1,0:T(8,128)S(1)} %shard_map.137), channel_id=1, replica_groups=mesh['y'=4,'zh'=8,'zl'=2,'x'=4,'c'=2] {'y','zl','x','c'}, dimensions={0} | all-to-all | bytes 524288 | tf_op jit(solution)/shard_map/all_to_all | solution.py:486
  194.1 3.2 %shard_map.138 = (f32[32,1024]{1,0:T(8,128)}, f32[32,512]{1,0:T(8,128)}, f32[32,256]{1,0:T(8,128)}, f32[32,32]{1,0:T(8,128)}) custom-call(f32[512,128]{1,0:T(8,128)S(1)} %bitcast.27, f32[256,256]{1,0:T(8,128)S(1)} %get-tuple-element.81.refs_1_, f32[32,128]{1,0:T(8,128)S(1)} %get-tuple-element.67.scal_ref.refs_7_.refs_2_, ...), custom_call_target="tpu_custom_call" | custom-call | tf_op jit(solution)/shard_map/pallas_call | solution.py:623
  (21 shorter events, 0.1 us)
Async XLA Ops:
  0.6 8.9 %copy-start.6 = (s32[1,1,512]{2,1,0:T(1,128)S(1)}, s32[1,1,512]{2,1,0:T(1,128)}, u32[]{:S(2)}) copy-start(s32[1,1,512]{2,1,0:T(1,128)} %param.14) | copy-start | bytes 6148
  0.6 8.9 %copy-start.1 = (bf16[1,1,1024,1024]{3,2,1,0:T(8,128)(2,1)S(1)}, bf16[1,1,1024,1024]{3,2,1,0:T(8,128)(2,1)}, u32[]{:S(2)}) copy-start(bf16[1,1,1024,1024]{3,2,1,0:T(8,128)(2,1)} %param.10) | copy-start | bytes 6291460
  3.8 7.3 %collective-permute-start.1 = (f32[48,512]{1,0:T(8,128)}, f32[48,512]{1,0:T(8,128)S(1)}, u32[]{:S(2)}, u32[]{:S(2)}) collective-permute-start(f32[48,512]{1,0:T(8,128)} %get-tuple-element.49.refs_1_.refs_4_), channel_id=1, source_target_pairs={{0,8},{8,16},{16,24},{24,32},{32,40},{40,48},{48,56},{56,64},{64,7... | collective-permute-start | bytes 294920 | tf_op jit(solution)/shard_map/ppermute | solution.py:553
  8.2 5.8 %collective-permute-start = (f32[48,512]{1,0:T(8,128)}, f32[48,512]{1,0:T(8,128)S(1)}, u32[]{:S(2)}, u32[]{:S(2)}) collective-permute-start(f32[48,512]{1,0:T(8,128)} %get-tuple-element.47.refs_0_.refs_3_), channel_id=1, source_target_pairs={{8,0},{16,8},{24,16},{32,24},{40,32},{48,40},{56,48},{64,56},{72,6... | collective-permute-start | bytes 294920 | tf_op jit(solution)/shard_map/ppermute | solution.py:553
  9.5 4.4 %copy-start.3 = (f32[48,512]{1,0:T(8,128)S(1)}, f32[48,512]{1,0:T(8,128)}, u32[]{:S(2)}) copy-start(f32[48,512]{1,0:T(8,128)} %get-tuple-element.47.refs_0_.refs_3_) | copy-start | bytes 294916
  9.6 4.4 %copy-start.5 = (f32[48,512]{1,0:T(8,128)S(1)}, f32[48,512]{1,0:T(8,128)}, u32[]{:S(2)}) copy-start(f32[48,512]{1,0:T(8,128)} %get-tuple-element.49.refs_1_.refs_4_) | copy-start | bytes 294916
  11.1 9.4 %copy-start = (bf16[1,1,1024,1024]{3,2,1,0:T(8,128)(2,1)S(1)}, bf16[1,1,1024,1024]{3,2,1,0:T(8,128)(2,1)}, u32[]{:S(2)}) copy-start(bf16[1,1,1024,1024]{3,2,1,0:T(8,128)(2,1)} %param.9) | copy-start | bytes 6291460
  14.5 9.6 %collective-permute-start.2 = (f32[64,512]{1,0:T(8,128)S(1)}, f32[64,512]{1,0:T(8,128)S(1)}, u32[]{:S(2)}, u32[]{:S(2)}) collective-permute-start(f32[64,512]{1,0:T(8,128)S(1)} %get-tuple-element.50.refs_0_.refs_4_), channel_id=1, source_target_pairs={{8,0},{16,8},{24,16},{32,24},{40,32},{48,40},{56,48},{64,56},{72,6... | collective-permute-start | bytes 393224 | tf_op jit(solution)/shard_map/ppermute | solution.py:553
  15.8 6.1 %copy-start.4 = (bf16[1,1,1024,256]{3,2,1,0:T(8,128)(2,1)S(1)}, bf16[1,1,1024,256]{3,2,1,0:T(8,128)(2,1)}, u32[]{:S(2)}) copy-start(bf16[1,1,1024,256]{3,2,1,0:T(8,128)(2,1)} %param.16) | copy-start | bytes 1572868
  15.8 6.1 %copy-start.8 = (f32[1,1,1024]{2,1,0:T(1,128)S(1)}, f32[1,1,1024]{2,1,0:T(1,128)}, u32[]{:S(2)}) copy-start(f32[1,1,1024]{2,1,0:T(1,128)} %param.17) | copy-start | bytes 12292
  15.8 8.3 %collective-permute-start.3 = (f32[64,512]{1,0:T(8,128)S(1)}, f32[64,512]{1,0:T(8,128)S(1)}, u32[]{:S(2)}, u32[]{:S(2)}) collective-permute-start(f32[64,512]{1,0:T(8,128)S(1)} %get-tuple-element.51.refs_1_.refs_5_), channel_id=1, source_target_pairs={{0,8},{8,16},{16,24},{24,32},{32,40},{40,48},{48,56},{56,64},{64,7... | collective-permute-start | bytes 393224 | tf_op jit(solution)/shard_map/ppermute | solution.py:553
  21.9 9.1 %copy-start.7 = (f32[32,8]{1,0:T(8,128)S(1)}, f32[32,8]{1,0:T(8,128)}, u32[]{:S(2)}) copy-start(f32[32,8]{1,0:T(8,128)} %get-tuple-element.48.refs_1_) | copy-start | bytes 3076
  24.6 8.3 %collective-permute-start.4 = (f32[80,512]{1,0:T(8,128)S(1)}, f32[80,512]{1,0:T(8,128)S(1)}, u32[]{:S(2)}, u32[]{:S(2)}) collective-permute-start(f32[80,512]{1,0:T(8,128)S(1)} %get-tuple-element.58.refs_7_.refs_0_), channel_id=1, source_target_pairs={{8,0},{16,8},{24,16},{32,24},{40,32},{48,40},{56,48},{64,56},{72,6... | collective-permute-start | bytes 491528 | tf_op jit(solution)/shard_map/ppermute | solution.py:553
  25.9 7.3 %collective-permute-start.5 = (f32[80,512]{1,0:T(8,128)S(1)}, f32[80,512]{1,0:T(8,128)S(1)}, u32[]{:S(2)}, u32[]{:S(2)}) collective-permute-start(f32[80,512]{1,0:T(8,128)S(1)} %get-tuple-element.59.refs_8_.refs_1_), channel_id=1, source_target_pairs={{0,8},{8,16},{16,24},{24,32},{32,40},{40,48},{48,56},{56,64},{64,7... | collective-permute-start | bytes 491528 | tf_op jit(solution)/shard_map/ppermute | solution.py:553
  73.7 40.3 %copy-start.2 = (f32[256,256]{1,0:T(8,128)S(1)}, f32[256,256]{1,0:T(8,128)}, u32[]{:S(2)}) copy-start(f32[256,256]{1,0:T(8,128)} %refs_1_.3) | copy-start | bytes 786436
  115.8 8.9 %collective-permute-start.6 = (f32[32,512]{1,0:T(8,128)S(1)}, f32[32,512]{1,0:T(8,128)S(1)}, u32[]{:S(2)}, u32[]{:S(2)}) collective-permute-start(f32[32,512]{1,0:T(8,128)S(1)} %get-tuple-element.63.sl_ref), channel_id=1, source_target_pairs={{8,0},{16,8},{24,16},{32,24},{40,32},{48,40},{56,48},{64,56},{72,6... | collective-permute-start | bytes 196616 | tf_op jit(solution)/shard_map/ppermute | solution.py:553
  117.1 7.6 %collective-permute-start.7 = (f32[32,512]{1,0:T(8,128)S(1)}, f32[32,512]{1,0:T(8,128)S(1)}, u32[]{:S(2)}, u32[]{:S(2)}) collective-permute-start(f32[32,512]{1,0:T(8,128)S(1)} %get-tuple-element.64.sr_ref), channel_id=1, source_target_pairs={{0,8},{8,16},{16,24},{24,32},{32,40},{40,48},{48,56},{56,64},{64,7... | collective-permute-start | bytes 196616 | tf_op jit(solution)/shard_map/ppermute | solution.py:553
  125.3 5.3 %collective-permute-start.8 = (f32[32,512]{1,0:T(8,128)S(1)}, f32[32,512]{1,0:T(8,128)S(1)}, u32[]{:S(2)}, u32[]{:S(2)}) collective-permute-start(f32[32,512]{1,0:T(8,128)S(1)} %get-tuple-element.68.sl_ref.refs_10_), channel_id=1, source_target_pairs={{8,0},{16,8},{24,16},{32,24},{40,32},{48,40},{56,48},{64,56},{72,6... | collective-permute-start | bytes 196616 | tf_op jit(solution)/shard_map/ppermute | solution.py:553
  126.6 5.3 %collective-permute-start.9 = (f32[32,512]{1,0:T(8,128)S(1)}, f32[32,512]{1,0:T(8,128)S(1)}, u32[]{:S(2)}, u32[]{:S(2)}) collective-permute-start(f32[32,512]{1,0:T(8,128)S(1)} %get-tuple-element.69.sr_ref.refs_11_), channel_id=1, source_target_pairs={{0,8},{8,16},{16,24},{24,32},{32,40},{40,48},{48,56},{56,64},{64,7... | collective-permute-start | bytes 196616 | tf_op jit(solution)/shard_map/ppermute | solution.py:553
  132.4 5.6 %collective-permute-start.10 = (f32[32,512]{1,0:T(8,128)S(1)}, f32[32,512]{1,0:T(8,128)S(1)}, u32[]{:S(2)}, u32[]{:S(2)}) collective-permute-start(f32[32,512]{1,0:T(8,128)S(1)} %get-tuple-element.71.refs_0_), channel_id=1, source_target_pairs={{8,0},{16,8},{24,16},{32,24},{40,32},{48,40},{56,48},{64,56},{72,6... | collective-permute-start | bytes 196616 | tf_op jit(solution)/shard_map/ppermute | solution.py:553
  133.7 5.6 %collective-permute-start.11 = (f32[32,512]{1,0:T(8,128)S(1)}, f32[32,512]{1,0:T(8,128)S(1)}, u32[]{:S(2)}, u32[]{:S(2)}) collective-permute-start(f32[32,512]{1,0:T(8,128)S(1)} %get-tuple-element.72.refs_1_), channel_id=1, source_target_pairs={{0,8},{8,16},{16,24},{24,32},{32,40},{40,48},{48,56},{56,64},{64,7... | collective-permute-start | bytes 196616 | tf_op jit(solution)/shard_map/ppermute | solution.py:553

commit v7 on v6

--- a/solution.py
+++ b/solution.py
@@ -28,11 +28,10 @@
     return jnp.sum(a, axis=1, keepdims=True)
 
 
-def call(kernel, outs, aliases={}):
+def call(kernel, outs):
     return pl.pallas_call(
         kernel,
         out_shape=outs,
-        input_output_aliases=aliases,
         compiler_params=pltpu.CompilerParams(vmem_limit_bytes=12 * 1024 * 1024),
     )
 
@@ -254,6 +253,7 @@
 
 def last_moment_kernel(given_ref, *refs, cols, count):
     out = refs[-1]
+    out[...] = given_ref[...]
     total = level_moments(out, refs[:3], 2, cols, count)
     at = 4 * count + 8 * cols
     out[at : at + cols, :] = given_ref[at : at + cols, :] + in_lanes([total], 2)
@@ -376,47 +376,65 @@
     or_ref[...] = v[:, face:]
 
 
-def combine_kernel(sl_ref, sr_ref, nl_ref, pr_ref, mask_ref, n0_ref, mat_ref, scal_ref, z0_ref,
-                   z1_ref, ul_ref, ur_ref, r1_ref, w0_ref, w1_ref, base_ref, mass_ref, prev_ref,
-                   out_ref, field_ref, dual_ref, *, cols, count):
+def early_kernel(scal_ref, z0_ref, z1_ref, ul_ref, ur_ref, r1_ref, w0_ref, w1_ref, base_ref,
+                 mass_ref, prev_ref, out_ref, field_ref, *, cols, count):
+    half = count // 2
+    face = ul_ref.shape[1]
+    third = slice(2 * cols, 3 * cols)
+    field_ref[0 : 2 * cols, :] = base_ref[0 : 2 * cols, :]
+    field_ref[third, 0:face] = base_ref[third, 0:face] + ul_ref[...]
+    field_ref[third, face:] = base_ref[third, face:] + ur_ref[...]
+    field_ref[3 * cols :, :] = base_ref[3 * cols :, :]
+    be1 = scal_ref[:, 1:2]
+    z0, w0 = z0_ref[:, face:], w0_ref[:, face:]
+    z1, w1, r1 = z1_ref[...], w1_ref[...], r1_ref[...]
+    q1 = w1 + be1 * w0
+    out_ref[...] = jnp.zeros(out_ref.shape, F32)
+    out_ref[12 * cols : 13 * cols, :] = in_lanes([
+        lane_sum(r1 * z1), lane_sum(q1 * z1), lane_sum(r1 * (z1 + be1 * z0)),
+        lane_sum((z1 + be1 * z0) * q1), lane_sum(z1 * w1),
+    ])
+    known = field_ref[0 : 3 * cols, :]
+    scaled = known * mass_ref[...]
+    tq = split_dot(scaled, prev_ref[...], 3)
+    out_ref[0 : 3 * cols, :] = tq[:, :half]
+    out_ref[4 * cols : 7 * cols, :] = tq[:, half:]
+    out_ref[8 * cols : 11 * cols, 0 : 3 * cols] = nt(scaled, known)
+
+
+def combine_kernel(given_ref, known_ref, sl_ref, sr_ref, nl_ref, pr_ref, mask_ref, n0_ref, mat_ref,
+                   scal_ref, r1_ref, w0_ref, w1_ref, mass_ref, prev_ref,
+                   out_ref, field_ref, m_ref, *, cols, count):
     half = count // 2
     face = sl_ref.shape[1]
     be1 = scal_ref[:, 1:2]
+    out_ref[...] = given_ref[...]
+    field_ref[0 : 3 * cols, :] = known_ref[0 : 3 * cols, :]
     whole = field_of(sl_ref, sr_ref, nl_ref, pr_ref, mask_ref) + be1 * n0_ref[...]
     u = split_dot(whole, mat_ref[...])
-    field_ref[0 : 2 * cols, :] = base_ref[0 : 2 * cols, :]
-    third, fourth = slice(2 * cols, 3 * cols), slice(3 * cols, 4 * cols)
-    field_ref[third, 0:face] = base_ref[third, 0:face] + ul_ref[...]
-    field_ref[third, face:] = base_ref[third, face:] + ur_ref[...]
-    field_ref[fourth, :] = base_ref[fourth, :] + u
+    last = known_ref[3 * cols :, :] + u
+    field_ref[3 * cols :, :] = last
     m = whole[:, face:]
-    z0, w0 = z0_ref[:, face:], w0_ref[:, face:]
-    z1, w1, r1 = z1_ref[...], w1_ref[...], r1_ref[...]
-    q1 = w1 + be1 * w0
-    p1 = z1 + be1 * z0
-    for i, item in enumerate((z0, z1, m)):
-        dual_ref[i * cols : (i + 1) * cols, :] = item
-    moments = (
-        lane_sum(r1 * z1), lane_sum(r1 * m), lane_sum(q1 * z1), lane_sum(q1 * m),
-        lane_sum(r1 * p1), lane_sum(p1 * q1), lane_sum(z1 * w1), lane_sum(m * w1),
+    m_ref[...] = m
+    w0, w1 = w0_ref[:, face:], w1_ref[...]
+    scaled = last * mass_ref[...]
+    tq = split_dot(scaled, prev_ref[...], 3)
+    out_ref[3 * cols : 4 * cols, :] = tq[:, :half]
+    out_ref[7 * cols : 8 * cols, :] = tq[:, half:]
+    out_ref[11 * cols : 12 * cols, :] = nt(scaled, field_ref[...])
+    at = 12 * cols
+    out_ref[at : at + cols, :] = given_ref[at : at + cols, :] + in_lanes([
+        lane_sum(r1_ref[...] * m), lane_sum((w1 + be1 * w0) * m), lane_sum(m * w1),
         lane_sum(whole * u),
-    )
-    field = field_ref[...]
-    scaled = field * mass_ref[...]
-    tq = split_dot(scaled, prev_ref[...], 3)
-    out_ref[0 : 4 * cols, :] = tq[:, :half]
-    out_ref[4 * cols : 8 * cols, :] = tq[:, half:]
-    out_ref[8 * cols : 12 * cols, :] = nt(scaled, field)
-    out_ref[12 * cols : 13 * cols, :] = in_lanes(moments)
-    out_ref[13 * cols :, :] = jnp.zeros((out_ref.shape[0] - 13 * cols, LANE), F32)
-
-
-def final_kernel(sums_ref, basis_ref, scal_ref, field_ref, dual_ref, prev_ref, back_ref,
+    ], 5)
+
+
+def final_kernel(sums_ref, basis_ref, scal_ref, field_ref, z0_ref, z1_ref, m_ref, prev_ref, back_ref,
                  block_ref, multi_ref, coef_ref, factor_ref, *, cols, count):
     half = count // 2
-    face = dual_ref.shape[1]
+    face = m_ref.shape[1]
     at = 12 * cols
-    r1z1, r1m, q1z1, q1m, r1p1, p1q1, z1w1, mw1, mm = (
+    r1z1, q1z1, r1p1, p1q1, z1w1, r1m, q1m, mw1, mm = (
         sums_ref[at : at + cols, k : k + 1] for k in range(9)
     )
     al0, be1, extra = (scal_ref[:, k : k + 1] for k in range(3))
@@ -429,8 +447,8 @@
     al2 = rz2 / (z2fz2 + 2.0 * be2 * z2q1 + be2 * be2 * p1q1)
     along = al1 + al2 * be2
     parts = (al0 + along * be1, along + al2, -al1 * al2)
-    multi = sum(y * dual_ref[i * cols : (i + 1) * cols, :] for i, y in enumerate(parts))
-    multi_ref[...] = multi
+    duals = (z0_ref[:, face:], z1_ref[...], m_ref[...])
+    multi_ref[...] = sum(y * dual for y, dual in zip(parts, duals))
     weights = [jnp.ones((cols, 1), F32)] + [-y for y in parts]
     primal = sum(y * field_ref[i * cols : (i + 1) * cols, :] for i, y in enumerate(weights))
     g1 = sum(
@@ -447,8 +465,11 @@
     stacked = jnp.concatenate(weights, axis=0)
     across = jnp.concatenate([jnp.sum(y * eye, axis=0, keepdims=True) for y in weights], axis=1)
     tiles = stacked * sums_ref[8 * cols : 12 * cols, :] * across
+    cross = tiles[3 * cols :]
+    cross = sum(cross[:, j * cols : (j + 1) * cols] for j in range(3))
     tiles = sum(tiles[i * cols : (i + 1) * cols] for i in range(4))
     gram = sum(tiles[:, j * cols : (j + 1) * cols] for j in range(4))
+    gram = gram + jnp.transpose(cross)
     basis = basis_ref[...]
     c = 2.0 * g1 - nn(g1, basis)
     coef_ref[...] = c
@@ -591,7 +612,6 @@
         first = call(
             lambda *refs: last_moment_kernel(*refs, cols=cols, count=count),
             shape(size, LANE),
-            aliases={0: 0},
         )(first, t, sl, sr)
         first = over_all(first, n_red, n_z)
 
@@ -615,15 +635,19 @@
         )
         near = exchange(sl, sr)
         size = up(13 * cols, 8 * n_red)
-        second, field, dual = call(
+        second, field = call(
+            lambda *refs: early_kernel(*refs, cols=cols, count=count),
+            (shape(size, LANE), shape(4 * cols, rows)),
+        )(scal, z0, z1, ul, ur, r1, w0, w1, base, mass_p, prev_p)
+        second, field, m = call(
             lambda *refs: combine_kernel(*refs, cols=cols, count=count),
-            (shape(size, LANE), shape(4 * cols, rows), shape(3 * cols, face)),
-        )(sl, sr, *near, mask, n0, inv_p, scal, z0, z1, ul, ur, r1, w0, w1, base, mass_p, prev_p)
+            (shape(size, LANE), shape(4 * cols, rows), part),
+        )(second, field, sl, sr, *near, mask, n0, inv_p, scal, r1, w0, w1, mass_p, prev_p)
         second = over_all(second, n_red, n_z)
         block, multi, coefficients, factor = call(
             lambda *refs: final_kernel(*refs, cols=cols, count=count),
             (shape(cols, rows), shape(cols, face), shape(cols, count), shape(cols, cols)),
-        )(second, gram, scal, field, dual, prev_t, back)
+        )(second, gram, scal, field, z0, z1, m, prev_t, back)
         return block.T[None, None], multi.T[None, None], coefficients.T, factor
 
     split = (along, ("x", "c"))

time: 198 us -> 198 us (level)
  transfers between devices with their start and end apart: 12 -> 12, of which waited for: 4 -> 4; matrix products, arithmetic and copies ran while one was open for 0% -> 0% of each run, Pallas kernels for 5% -> 6%
where the time goes in v7:
time: 198 us; the launch traced here: 197 us
  blocking collectives  132 us (67%)
  starting transfers between devices  34.3 us (17%)
  Pallas kernels  24.3 us (12%)
  waiting for transfers between devices  5.15 us (3%)
    all_to_all x6, blocking collectives, swap(): return lax.all_to_all(parts, axes, 0, 0, tiled=True)  132 us
    ppermute x12, starting transfers between devices, exchange(): return (lax.ppermute(sl, along, behind), lax.ppermute(sr, along, ahead))  34.3 us
    ppermute x12, waiting for transfers between devices, exchange(): return (lax.ppermute(sl, along, behind), lax.ppermute(sr, along, ahead))  5.15 us
  transfers between devices with their start and end apart: 12, of which 4 were waited for; matrix products, arithmetic and copies ran while one was open for 0% of the time, Pallas kernels for 6%

profile of v7, /device:TPU:1, one launch (start us, length us, event | category | flops | bytes accessed | tf_op | source)
XLA Modules:
  0.0 197.2 jit_solution(7317459842975553698)
XLA Ops:
  0.7 3.2 %shard_map.120 = (f32[48,512]{1,0:T(8,128)}, f32[48,512]{1,0:T(8,128)}, f32[32,8]{1,0:T(8,128)}) custom-call(bf16[1024,1024]{1,0:T(8,128)(2,1)} %bitcast.21, f32[32,1024]{1,0:T(8,128)} %bitcast.36, f32[8,1024]{1,0:T(8,128)} %bitcast.37, s32[1,512]{1,0:T(1,128)} %bitcast.30, s32[1,8]{1,0:T(1,128)} %bitcast.38), custom_call_target="tpu_custom_call" | custom-call | tf_op jit(solution)/shard_map/pallas_call | solution.py:557
  3.8 4.4 %collective-permute-start.1 = (f32[48,512]{1,0:T(8,128)}, f32[48,512]{1,0:T(8,128)S(1)}, u32[]{:S(2)}, u32[]{:S(2)}) collective-permute-start(f32[48,512]{1,0:T(8,128)} %get-tuple-element.51.refs_1_.refs_4_), channel_id=1, source_target_pairs={{0,8},{8,16},{16,24},{24,32},{32,40},{40,48},{48,56},{56,64},{64,7... | collective-permute-start | bytes 294920 | tf_op jit(solution)/shard_map/ppermute | solution.py:574
  8.2 1.3 collective-permute-start
  9.5 0.0 copy-start.3
  9.6 1.5 shard_map.121.refs_5_.refs_2_.mat_ref
  11.1 0.0 copy-start
  11.1 2.9 %collective-permute-done.refs_2_ = f32[48,512]{1,0:T(8,128)S(1)} collective-permute-done((f32[48,512]{1,0:T(8,128)}, f32[48,512]{1,0:T(8,128)S(1)}, u32[]{:S(2)}, u32[]{:S(2)}) %collective-permute-start) | collective-permute-done | bytes 98336 | tf_op jit(solution)/shard_map/ppermute | solution.py:574
  14.0 0.5 shard_map.122
  14.5 1.3 collective-permute-start.2
  15.8 0.0 copy-start.4
  15.8 0.0 copy-start.8
  15.8 4.6 %collective-permute-start.3 = (f32[64,512]{1,0:T(8,128)S(1)}, f32[64,512]{1,0:T(8,128)S(1)}, u32[]{:S(2)}, u32[]{:S(2)}) collective-permute-start(f32[64,512]{1,0:T(8,128)S(1)} %get-tuple-element.53.refs_1_.refs_5_), channel_id=1, source_target_pairs={{0,8},{8,16},{16,24},{24,32},{32,40},{40,48},{48,56},{56,64},{64,7... | collective-permute-start | bytes 393224 | tf_op jit(solution)/shard_map/ppermute | solution.py:574
  20.4 1.5 shard_map.124.refs_5_.mat_ref.refs_8_
  21.9 0.0 copy-start.7
  21.9 2.1 %shard_map.123 = (bf16[1024,256]{1,0:T(8,128)(2,1)S(1)}, bf16[256,1024]{1,0:T(8,128)(2,1)S(1)}, f32[1,1024]{1,0:T(1,128)S(1)}, f32[256,256]{1,0:T(8,128)S(1)}) custom-call(bf16[1024,256]{1,0:T(8,128)(2,1)S(1)} %bitcast.28, s32[1,512]{1,0:T(1,128)S(1)} %bitcast.33, f32[1,1024]{1,0:T(1,128)S(1)} %bitcast.35), custom_call_target="tpu_custom_call" | custom-call | tf_op jit(solution)/shard_map/pallas_call | solution.py:593
  24.0 0.0 collective-permute-done.2.refs_2_
  24.1 0.0 collective-permute-done.3.refs_3_
  24.1 0.5 shard_map.125
  24.6 1.3 collective-permute-start.4
  25.9 5.1 %collective-permute-start.5 = (f32[80,512]{1,0:T(8,128)S(1)}, f32[80,512]{1,0:T(8,128)S(1)}, u32[]{:S(2)}, u32[]{:S(2)}) collective-permute-start(f32[80,512]{1,0:T(8,128)S(1)} %get-tuple-element.61.refs_8_.refs_1_), channel_id=1, source_target_pairs={{0,8},{8,16},{16,24},{24,32},{32,40},{40,48},{48,56},{56,64},{64,7... | collective-permute-start | bytes 491528 | tf_op jit(solution)/shard_map/ppermute | solution.py:574
  31.0 1.8 shard_map.126.refs_0_
  32.8 0.4 collective-permute-done.5.refs_3_
  33.2 0.6 shard_map.127
  33.8 1.0 shard_map.128
  34.8 38.9 %all_to_all.30.parts_ref = f32[64,24,128]{2,1,0:T(8,128)S(1)} all-to-all(f32[64,24,128]{2,1,0:T(8,128)S(1)} %bitcast.25), channel_id=1, replica_groups=mesh['y'=4,'zh'=8,'zl'=2,'x'=4,'c'=2] {'y','zl','x','c'}, dimensions={0} | all-to-all | bytes 1572864 | tf_op jit(solution)/shard_map/all_to_all | solution.py:507
  73.7 0.1 shard_map.129
  73.8 18.1 %all_to_all.31.parts_ref = f32[8,24,128]{2,1,0:T(8,128)S(1)} all-to-all(f32[8,24,128]{2,1,0:T(8,128)S(1)} %shard_map.129), channel_id=1, replica_groups=mesh['y'=4,'zh'=8,'zl'=2,'x'=4,'c'=2] {'zh'}, dimensions={0} | all-to-all | bytes 196608 | tf_op jit(solution)/shard_map/all_to_all | solution.py:507
  91.9 0.1 shard_map.130
  91.9 22.1 %all_to_all.32 = f32[64,24,128]{2,1,0:T(8,128)S(1)} all-to-all(f32[64,24,128]{2,1,0:T(8,128)S(1)} %shard_map.130), channel_id=1, replica_groups=mesh['y'=4,'zh'=8,'zl'=2,'x'=4,'c'=2] {'y','zl','x','c'}, dimensions={0} | all-to-all | bytes 1572864 | tf_op jit(solution)/shard_map/all_to_all | solution.py:507
  114.0 1.8 shard_map.131
  115.8 1.3 collective-permute-start.6
  117.1 4.2 %collective-permute-start.7 = (f32[32,512]{1,0:T(8,128)S(1)}, f32[32,512]{1,0:T(8,128)S(1)}, u32[]{:S(2)}, u32[]{:S(2)}) collective-permute-start(f32[32,512]{1,0:T(8,128)S(1)} %get-tuple-element.69.sr_ref), channel_id=1, source_target_pairs={{0,8},{8,16},{16,24},{24,32},{32,40},{40,48},{48,56},{56,64},{64,7... | collective-permute-start | bytes 196616 | tf_op jit(solution)/shard_map/ppermute | solution.py:574
  121.3 3.4 %shard_map.132 = (f32[32,1024]{1,0:T(8,128)S(1)}, f32[32,1024]{1,0:T(8,128)S(1)}, f32[32,512]{1,0:T(8,128)S(1)}, f32[128,1024]{1,0:T(8,128)S(1)}, f32[32,128]{1,...) custom-call(f32[1536,128]{1,0:T(8,128)S(1)} %bitcast.24, f32[256,256]{1,0:T(8,128)S(1)} %copy-done.2, ...), custom_call_target="tpu_custom_call" | custom-call | tf_op jit(solution)/shard_map/pallas_call | solution.py:623
  124.8 0.5 shard_map.133
  125.3 1.3 collective-permute-start.8
  126.6 4.0 %collective-permute-start.9 = (f32[32,512]{1,0:T(8,128)S(1)}, f32[32,512]{1,0:T(8,128)S(1)}, u32[]{:S(2)}, u32[]{:S(2)}) collective-permute-start(f32[32,512]{1,0:T(8,128)S(1)} %get-tuple-element.72.sr_ref.refs_4_), channel_id=1, source_target_pairs={{0,8},{8,16},{16,24},{24,32},{32,40},{40,48},{48,56},{56,64},{64,7... | collective-permute-start | bytes 196616 | tf_op jit(solution)/shard_map/ppermute | solution.py:574
  130.6 1.3 collective-permute-done.9.pr_ref
  131.9 0.5 shard_map.134
  132.4 1.3 collective-permute-start.10
  133.7 4.3 %collective-permute-start.11 = (f32[32,512]{1,0:T(8,128)S(1)}, f32[32,512]{1,0:T(8,128)S(1)}, u32[]{:S(2)}, u32[]{:S(2)}) collective-permute-start(f32[32,512]{1,0:T(8,128)S(1)} %get-tuple-element.82.refs_3_), channel_id=1, source_target_pairs={{0,8},{8,16},{16,24},{24,32},{32,40},{40,48},{48,56},{56,64},{64,7... | collective-permute-start | bytes 196616 | tf_op jit(solution)/shard_map/ppermute | solution.py:574
  138.0 0.7 shard_map.135
  138.7 0.6 collective-permute-done.11.refs_5_
  139.3 1.3 shard_map.136
  140.6 23.9 %all_to_all.33.parts_ref = f32[64,8,128]{2,1,0:T(8,128)S(1)} all-to-all(f32[64,8,128]{2,1,0:T(8,128)S(1)} %bitcast.29), channel_id=1, replica_groups=mesh['y'=4,'zh'=8,'zl'=2,'x'=4,'c'=2] {'y','zl','x','c'}, dimensions={0} | all-to-all | bytes 524288 | tf_op jit(solution)/shard_map/all_to_all | solution.py:507
  164.5 0.1 shard_map.137
  164.6 14.4 %all_to_all.34.parts_ref = f32[8,8,128]{2,1,0:T(8,128)S(1)} all-to-all(f32[8,8,128]{2,1,0:T(8,128)S(1)} %shard_map.137), channel_id=1, replica_groups=mesh['y'=4,'zh'=8,'zl'=2,'x'=4,'c'=2] {'zh'}, dimensions={0} | all-to-all | bytes 65536 | tf_op jit(solution)/shard_map/all_to_all | solution.py:507
  179.0 15.0 %all_to_all.35 = f32[64,8,128]{2,1,0:T(8,128)S(1)} all-to-all(f32[64,8,128]{2,1,0:T(8,128)S(1)} %shard_map.138), channel_id=1, replica_groups=mesh['y'=4,'zh'=8,'zl'=2,'x'=4,'c'=2] {'y','zl','x','c'}, dimensions={0} | all-to-all | bytes 524288 | tf_op jit(solution)/shard_map/all_to_all | solution.py:507
  194.0 3.2 %shard_map.139 = (f32[32,1024]{1,0:T(8,128)}, f32[32,512]{1,0:T(8,128)}, f32[32,256]{1,0:T(8,128)}, f32[32,32]{1,0:T(8,128)}) custom-call(f32[512,128]{1,0:T(8,128)S(1)} %bitcast.27, f32[256,256]{1,0:T(8,128)S(1)} %get-tuple-element.85.refs_1_, f32[32,128]{1,0:T(8,128)S(1)} %get-tuple-element.66.scal_ref.refs_0_.refs_9_.refs_2_, ...), custom_call_target="tpu_custom_call" | custom-call | tf_op jit(solution)/shard_map/pallas_call | solution.py:647
  (22 shorter events, 0.1 us)
Async XLA Ops:
  0.6 8.9 %copy-start.6 = (s32[1,1,512]{2,1,0:T(1,128)S(1)}, s32[1,1,512]{2,1,0:T(1,128)}, u32[]{:S(2)}) copy-start(s32[1,1,512]{2,1,0:T(1,128)} %param.14) | copy-start | bytes 6148
  0.6 8.9 %copy-start.1 = (bf16[1,1,1024,1024]{3,2,1,0:T(8,128)(2,1)S(1)}, bf16[1,1,1024,1024]{3,2,1,0:T(8,128)(2,1)}, u32[]{:S(2)}) copy-start(bf16[1,1,1024,1024]{3,2,1,0:T(8,128)(2,1)} %param.10) | copy-start | bytes 6291460
  3.8 7.3 %collective-permute-start.1 = (f32[48,512]{1,0:T(8,128)}, f32[48,512]{1,0:T(8,128)S(1)}, u32[]{:S(2)}, u32[]{:S(2)}) collective-permute-start(f32[48,512]{1,0:T(8,128)} %get-tuple-element.51.refs_1_.refs_4_), channel_id=1, source_target_pairs={{0,8},{8,16},{16,24},{24,32},{32,40},{40,48},{48,56},{56,64},{64,7... | collective-permute-start | bytes 294920 | tf_op jit(solution)/shard_map/ppermute | solution.py:574
  8.2 5.8 %collective-permute-start = (f32[48,512]{1,0:T(8,128)}, f32[48,512]{1,0:T(8,128)S(1)}, u32[]{:S(2)}, u32[]{:S(2)}) collective-permute-start(f32[48,512]{1,0:T(8,128)} %get-tuple-element.49.refs_0_.refs_3_), channel_id=1, source_target_pairs={{8,0},{16,8},{24,16},{32,24},{40,32},{48,40},{56,48},{64,56},{72,6... | collective-permute-start | bytes 294920 | tf_op jit(solution)/shard_map/ppermute | solution.py:574
  9.5 4.4 %copy-start.3 = (f32[48,512]{1,0:T(8,128)S(1)}, f32[48,512]{1,0:T(8,128)}, u32[]{:S(2)}) copy-start(f32[48,512]{1,0:T(8,128)} %get-tuple-element.49.refs_0_.refs_3_) | copy-start | bytes 294916
  9.6 4.4 %copy-start.5 = (f32[48,512]{1,0:T(8,128)S(1)}, f32[48,512]{1,0:T(8,128)}, u32[]{:S(2)}) copy-start(f32[48,512]{1,0:T(8,128)} %get-tuple-element.51.refs_1_.refs_4_) | copy-start | bytes 294916
  11.1 9.4 %copy-start = (bf16[1,1,1024,1024]{3,2,1,0:T(8,128)(2,1)S(1)}, bf16[1,1,1024,1024]{3,2,1,0:T(8,128)(2,1)}, u32[]{:S(2)}) copy-start(bf16[1,1,1024,1024]{3,2,1,0:T(8,128)(2,1)} %param.9) | copy-start | bytes 6291460
  14.5 9.6 %collective-permute-start.2 = (f32[64,512]{1,0:T(8,128)S(1)}, f32[64,512]{1,0:T(8,128)S(1)}, u32[]{:S(2)}, u32[]{:S(2)}) collective-permute-start(f32[64,512]{1,0:T(8,128)S(1)} %get-tuple-element.52.refs_0_.refs_4_), channel_id=1, source_target_pairs={{8,0},{16,8},{24,16},{32,24},{40,32},{48,40},{56,48},{64,56},{72,6... | collective-permute-start | bytes 393224 | tf_op jit(solution)/shard_map/ppermute | solution.py:574
  15.8 6.2 %copy-start.4 = (bf16[1,1,1024,256]{3,2,1,0:T(8,128)(2,1)S(1)}, bf16[1,1,1024,256]{3,2,1,0:T(8,128)(2,1)}, u32[]{:S(2)}) copy-start(bf16[1,1,1024,256]{3,2,1,0:T(8,128)(2,1)} %param.16) | copy-start | bytes 1572868
  15.8 6.1 %copy-start.8 = (f32[1,1,1024]{2,1,0:T(1,128)S(1)}, f32[1,1,1024]{2,1,0:T(1,128)}, u32[]{:S(2)}) copy-start(f32[1,1,1024]{2,1,0:T(1,128)} %param.17) | copy-start | bytes 12292
  15.8 8.3 %collective-permute-start.3 = (f32[64,512]{1,0:T(8,128)S(1)}, f32[64,512]{1,0:T(8,128)S(1)}, u32[]{:S(2)}, u32[]{:S(2)}) collective-permute-start(f32[64,512]{1,0:T(8,128)S(1)} %get-tuple-element.53.refs_1_.refs_5_), channel_id=1, source_target_pairs={{0,8},{8,16},{16,24},{24,32},{32,40},{40,48},{48,56},{56,64},{64,7... | collective-permute-start | bytes 393224 | tf_op jit(solution)/shard_map/ppermute | solution.py:574
  21.9 9.1 %copy-start.7 = (f32[32,8]{1,0:T(8,128)S(1)}, f32[32,8]{1,0:T(8,128)}, u32[]{:S(2)}) copy-start(f32[32,8]{1,0:T(8,128)} %get-tuple-element.50.refs_1_) | copy-start | bytes 3076
  24.6 8.3 %collective-permute-start.4 = (f32[80,512]{1,0:T(8,128)S(1)}, f32[80,512]{1,0:T(8,128)S(1)}, u32[]{:S(2)}, u32[]{:S(2)}) collective-permute-start(f32[80,512]{1,0:T(8,128)S(1)} %get-tuple-element.60.refs_7_.refs_0_), channel_id=1, source_target_pairs={{8,0},{16,8},{24,16},{32,24},{40,32},{48,40},{56,48},{64,56},{72,6... | collective-permute-start | bytes 491528 | tf_op jit(solution)/shard_map/ppermute | solution.py:574
  25.9 7.3 %collective-permute-start.5 = (f32[80,512]{1,0:T(8,128)S(1)}, f32[80,512]{1,0:T(8,128)S(1)}, u32[]{:S(2)}, u32[]{:S(2)}) collective-permute-start(f32[80,512]{1,0:T(8,128)S(1)} %get-tuple-element.61.refs_8_.refs_1_), channel_id=1, source_target_pairs={{0,8},{8,16},{16,24},{24,32},{32,40},{40,48},{48,56},{56,64},{64,7... | collective-permute-start | bytes 491528 | tf_op jit(solution)/shard_map/ppermute | solution.py:574
  73.7 40.3 %copy-start.2 = (f32[256,256]{1,0:T(8,128)S(1)}, f32[256,256]{1,0:T(8,128)}, u32[]{:S(2)}) copy-start(f32[256,256]{1,0:T(8,128)} %refs_1_.3) | copy-start | bytes 786436
  115.8 8.9 %collective-permute-start.6 = (f32[32,512]{1,0:T(8,128)S(1)}, f32[32,512]{1,0:T(8,128)S(1)}, u32[]{:S(2)}, u32[]{:S(2)}) collective-permute-start(f32[32,512]{1,0:T(8,128)S(1)} %get-tuple-element.68.sl_ref), channel_id=1, source_target_pairs={{8,0},{16,8},{24,16},{32,24},{40,32},{48,40},{56,48},{64,56},{72,6... | collective-permute-start | bytes 196616 | tf_op jit(solution)/shard_map/ppermute | solution.py:574
  117.1 7.6 %collective-permute-start.7 = (f32[32,512]{1,0:T(8,128)S(1)}, f32[32,512]{1,0:T(8,128)S(1)}, u32[]{:S(2)}, u32[]{:S(2)}) collective-permute-start(f32[32,512]{1,0:T(8,128)S(1)} %get-tuple-element.69.sr_ref), channel_id=1, source_target_pairs={{0,8},{8,16},{16,24},{24,32},{32,40},{40,48},{48,56},{56,64},{64,7... | collective-permute-start | bytes 196616 | tf_op jit(solution)/shard_map/ppermute | solution.py:574
  125.3 5.3 %collective-permute-start.8 = (f32[32,512]{1,0:T(8,128)S(1)}, f32[32,512]{1,0:T(8,128)S(1)}, u32[]{:S(2)}, u32[]{:S(2)}) collective-permute-start(f32[32,512]{1,0:T(8,128)S(1)} %get-tuple-element.71.sl_ref.refs_3_), channel_id=1, source_target_pairs={{8,0},{16,8},{24,16},{32,24},{40,32},{48,40},{56,48},{64,56},{72,6... | collective-permute-start | bytes 196616 | tf_op jit(solution)/shard_map/ppermute | solution.py:574
  126.6 5.3 %collective-permute-start.9 = (f32[32,512]{1,0:T(8,128)S(1)}, f32[32,512]{1,0:T(8,128)S(1)}, u32[]{:S(2)}, u32[]{:S(2)}) collective-permute-start(f32[32,512]{1,0:T(8,128)S(1)} %get-tuple-element.72.sr_ref.refs_4_), channel_id=1, source_target_pairs={{0,8},{8,16},{16,24},{24,32},{32,40},{40,48},{48,56},{56,64},{64,7... | collective-permute-start | bytes 196616 | tf_op jit(solution)/shard_map/ppermute | solution.py:574
  132.4 6.4 %collective-permute-start.10 = (f32[32,512]{1,0:T(8,128)S(1)}, f32[32,512]{1,0:T(8,128)S(1)}, u32[]{:S(2)}, u32[]{:S(2)}) collective-permute-start(f32[32,512]{1,0:T(8,128)S(1)} %get-tuple-element.81.refs_2_), channel_id=1, source_target_pairs={{8,0},{16,8},{24,16},{32,24},{40,32},{48,40},{56,48},{64,56},{72,6... | collective-permute-start | bytes 196616 | tf_op jit(solution)/shard_map/ppermute | solution.py:574
  133.7 5.6 %collective-permute-start.11 = (f32[32,512]{1,0:T(8,128)S(1)}, f32[32,512]{1,0:T(8,128)S(1)}, u32[]{:S(2)}, u32[]{:S(2)}) collective-permute-start(f32[32,512]{1,0:T(8,128)S(1)} %get-tuple-element.82.refs_3_), channel_id=1, source_target_pairs={{0,8},{8,16},{16,24},{24,32},{32,40},{40,48},{48,56},{56,64},{64,7... | collective-permute-start | bytes 196616 | tf_op jit(solution)/shard_map/ppermute | solution.py:574

commit v8 on v7

--- a/solution.py
+++ b/solution.py
@@ -294,11 +294,8 @@
     or_ref[...] = v[:, face:]
 
 
-def values_kernel(sums_ref, coarse_ref, nm_ref, sl0, sr0, t1, t2, sl2, sr2, sl3, w0_ref,
-                  z0_ref, w1c_ref, r1_ref, field_ref, scal_ref, gram_ref, back_ref,
-                  *, cols, count):
+def values_kernel(sums_ref, coarse_ref, t2, sl3, z0_ref, local_ref, scal_ref, *, cols, count):
     diagonals = 4 * count + 9 * cols
-    face = sl0.shape[1]
     m0, m1, m2 = (unpack(sums_ref, k, diagonals) for k in range(3))
     coarse = coarse_ref[...]
     c_load, w0x, w1x, w2x = (vector(sums_ref, k, cols, count) for k in range(4))
@@ -324,11 +321,21 @@
     )
     gm = nn(cm, coarse)
     local = at_corners(jnp.concatenate([g0, g1, gz1, gm], axis=0), sl3)
+    local_ref[...] = local
+    (p20,) = spread(local[0:cols], 2, t2, slice(0, t2.shape[1]), cols)
+    z0_ref[...] = t2[0:cols, :] + p20
+    scal_ref[...] = in_lanes([al0, be1, lane_sum(cm * gm)])
+
+
+def base_kernel(sums_ref, local_ref, scal_ref, nm_ref, sl0, sr0, t1, sl2, sr2, w0_ref,
+                w1c_ref, r1_ref, field_ref, gram_ref, back_ref, *, cols, count):
+    diagonals = 4 * count + 9 * cols
+    face = sl0.shape[1]
+    local = local_ref[...]
+    al0 = scal_ref[:, 0:1]
     every, right, whole = slice(0, 2 * face), slice(face, 2 * face), slice(0, face)
-    (p20,) = spread(local[0:cols], 2, t2, every, cols)
     (p10,) = spread(local[0:cols], 1, t1, right, cols)
     (w1c_ref[...],) = spread(local[2 * cols : 3 * cols], 1, t1, every, cols)
-    z0_ref[...] = t2[0:cols, :] + p20
     r1_ref[...] = t1[0:cols, right] + p10 - al0 * w0_ref[:, right]
     for own, u, lanes in ((sl0, sl2, slice(0, face)), (sr0, sr2, right)):
         corner = spread(local, 0, own, whole, cols)
@@ -337,7 +344,6 @@
         field_ref[cols : 2 * cols, lanes] = u[0:cols, :] + u0 + corner[1]
         field_ref[2 * cols : 3 * cols, lanes] = corner[2]
         field_ref[3 * cols : 4 * cols, lanes] = corner[3]
-    scal_ref[...] = in_lanes([al0, be1, lane_sum(cm * gm)])
     gram_ref[...] = unpack(sums_ref, 3, diagonals)
     back_ref[...] = from_order(nm_ref[...], face).astype(BF16)
 
@@ -620,16 +626,20 @@
         sl, sr, w0 = call(
             lambda *refs: coarse_kernel(*refs, cols=cols, count=count), (part, part, wide)
         )(first, coarse_inverse, schur_p, t1, t3, sl3)
-        z0, w1c, r1, base, scal, gram, back = call(
+        z0, local, scal = call(
             lambda *refs: values_kernel(*refs, cols=cols, count=count),
-            (wide, wide, part, shape(4 * cols, rows), shape(cols, LANE), shape(count, count),
-             jax.ShapeDtypeStruct((face, face), BF16)),
-        )(first, coarse_inverse, nm_row, sl0, sr0, t1, t2, sl2, sr2, sl3, w0)
+            (wide, shape(4 * cols, LANE), shape(cols, LANE)),
+        )(first, coarse_inverse, t2, sl3)
         near = exchange(sl, sr)
         n0, z1, ul, ur = call(dual_kernel, (wide, part, part, part))(
             sl, sr, *near, mask, z0, scal, inv_p
         )
         near = exchange(ul, ur)
+        w1c, r1, base, gram, back = call(
+            lambda *refs: base_kernel(*refs, cols=cols, count=count),
+            (wide, part, shape(4 * cols, rows), shape(count, count),
+             jax.ShapeDtypeStruct((face, face), BF16)),
+        )(first, local, scal, nm_row, sl0, sr0, t1, sl2, sr2, w0)
         w1, sl, sr = call(precondition_kernel, (part, part, part))(
             ul, ur, *near, mask, w1c, schur_p
         )

time: 198 us -> 197 us (level)
  no operation moved by 1% of the time
where the time goes in v8:
time: 197 us; the launch traced here: 196 us
  blocking collectives  132 us (67%)
  starting transfers between devices  34.3 us (17%)
  Pallas kernels  24.6 us (12%)
  waiting for transfers between devices  4.15 us (2%)
    all_to_all x6, blocking collectives, swap(): return lax.all_to_all(parts, axes, 0, 0, tiled=True)  132 us
    ppermute x12, starting transfers between devices, exchange(): return (lax.ppermute(sl, along, behind), lax.ppermute(sr, along, ahead))  34.3 us
    ppermute x12, waiting for transfers between devices, exchange(): return (lax.ppermute(sl, along, behind), lax.ppermute(sr, along, ahead))  4.15 us
  transfers between devices with their start and end apart: 12, of which 4 were waited for; matrix products, arithmetic and copies ran while one was open for 0% of the time, Pallas kernels for 6%

profile of v8, /device:TPU:1, one launch (start us, length us, event | category | flops | bytes accessed | tf_op | source)
XLA Modules:
  0.0 196.5 jit_solution(411690356251410440)
XLA Ops:
  0.7 3.2 %shard_map.120 = (f32[48,512]{1,0:T(8,128)}, f32[48,512]{1,0:T(8,128)}, f32[32,8]{1,0:T(8,128)}) custom-call(bf16[1024,1024]{1,0:T(8,128)(2,1)} %bitcast.24, f32[32,1024]{1,0:T(8,128)} %bitcast.37, f32[8,1024]{1,0:T(8,128)} %bitcast.38, s32[1,512]{1,0:T(1,128)} %bitcast.31, s32[1,8]{1,0:T(1,128)} %bitcast.39), custom_call_target="tpu_custom_call" | custom-call | tf_op jit(solution)/shard_map/pallas_call | solution.py:563
  3.8 4.4 %collective-permute-start.1 = (f32[48,512]{1,0:T(8,128)}, f32[48,512]{1,0:T(8,128)S(1)}, u32[]{:S(2)}, u32[]{:S(2)}) collective-permute-start(f32[48,512]{1,0:T(8,128)} %get-tuple-element.52.refs_1_.refs_5_), channel_id=1, source_target_pairs={{0,8},{8,16},{16,24},{24,32},{32,40},{40,48},{48,56},{56,64},{64,7... | collective-permute-start | bytes 294920 | tf_op jit(solution)/shard_map/ppermute | solution.py:580
  8.2 1.3 collective-permute-start
  9.5 0.0 copy-start.3
  9.6 1.5 shard_map.121.refs_5_.refs_2_.mat_ref
  11.1 0.0 copy-start
  11.1 2.9 %collective-permute-done.refs_2_ = f32[48,512]{1,0:T(8,128)S(1)} collective-permute-done((f32[48,512]{1,0:T(8,128)}, f32[48,512]{1,0:T(8,128)S(1)}, u32[]{:S(2)}, u32[]{:S(2)}) %collective-permute-start) | collective-permute-done | bytes 98336 | tf_op jit(solution)/shard_map/ppermute | solution.py:580
  14.0 0.5 shard_map.122
  14.4 1.3 collective-permute-start.2
  15.7 0.0 copy-start.4
  15.8 0.0 copy-start.8
  15.8 4.6 %collective-permute-start.3 = (f32[64,512]{1,0:T(8,128)S(1)}, f32[64,512]{1,0:T(8,128)S(1)}, u32[]{:S(2)}, u32[]{:S(2)}) collective-permute-start(f32[64,512]{1,0:T(8,128)S(1)} %get-tuple-element.54.refs_1_.refs_5_), channel_id=1, source_target_pairs={{0,8},{8,16},{16,24},{24,32},{32,40},{40,48},{48,56},{56,64},{64,7... | collective-permute-start | bytes 393224 | tf_op jit(solution)/shard_map/ppermute | solution.py:580
  20.4 1.5 shard_map.124.refs_5_.mat_ref.refs_8_
  21.9 0.0 copy-start.7
  21.9 2.1 %shard_map.123 = (bf16[1024,256]{1,0:T(8,128)(2,1)S(1)}, bf16[256,1024]{1,0:T(8,128)(2,1)S(1)}, f32[1,1024]{1,0:T(1,128)S(1)}, f32[256,256]{1,0:T(8,128)S(1)}) custom-call(bf16[1024,256]{1,0:T(8,128)(2,1)S(1)} %bitcast.29, s32[1,512]{1,0:T(1,128)S(1)} %bitcast.34, f32[1,1024]{1,0:T(1,128)S(1)} %bitcast.36), custom_call_target="tpu_custom_call" | custom-call | tf_op jit(solution)/shard_map/pallas_call | solution.py:599
  24.0 0.0 collective-permute-done.2.refs_2_
  24.1 0.5 shard_map.125
  24.6 1.3 collective-permute-start.4
  25.9 5.1 %collective-permute-start.5 = (f32[80,512]{1,0:T(8,128)S(1)}, f32[80,512]{1,0:T(8,128)S(1)}, u32[]{:S(2)}, u32[]{:S(2)}) collective-permute-start(f32[80,512]{1,0:T(8,128)S(1)} %get-tuple-element.62.refs_8_.refs_1_), channel_id=1, source_target_pairs={{0,8},{8,16},{16,24},{24,32},{32,40},{40,48},{48,56},{56,64},{64,7... | collective-permute-start | bytes 491528 | tf_op jit(solution)/shard_map/ppermute | solution.py:580
  31.0 1.8 shard_map.126.refs_0_
  32.8 0.4 collective-permute-done.5.refs_3_
  33.2 0.6 shard_map.127
  33.8 1.0 shard_map.128
  34.8 38.9 %all_to_all.30.parts_ref = f32[64,24,128]{2,1,0:T(8,128)S(1)} all-to-all(f32[64,24,128]{2,1,0:T(8,128)S(1)} %bitcast.26), channel_id=1, replica_groups=mesh['y'=4,'zh'=8,'zl'=2,'x'=4,'c'=2] {'y','zl','x','c'}, dimensions={0} | all-to-all | bytes 1572864 | tf_op jit(solution)/shard_map/all_to_all | solution.py:513
  73.7 0.1 shard_map.129
  73.8 18.1 %all_to_all.31.parts_ref = f32[8,24,128]{2,1,0:T(8,128)S(1)} all-to-all(f32[8,24,128]{2,1,0:T(8,128)S(1)} %shard_map.129), channel_id=1, replica_groups=mesh['y'=4,'zh'=8,'zl'=2,'x'=4,'c'=2] {'zh'}, dimensions={0} | all-to-all | bytes 196608 | tf_op jit(solution)/shard_map/all_to_all | solution.py:513
  91.8 0.1 shard_map.130
  91.9 22.1 %all_to_all.32 = f32[64,24,128]{2,1,0:T(8,128)S(1)} all-to-all(f32[64,24,128]{2,1,0:T(8,128)S(1)} %shard_map.130), channel_id=1, replica_groups=mesh['y'=4,'zh'=8,'zl'=2,'x'=4,'c'=2] {'y','zl','x','c'}, dimensions={0} | all-to-all | bytes 1572864 | tf_op jit(solution)/shard_map/all_to_all | solution.py:513
  114.0 1.8 shard_map.132
  115.8 1.3 collective-permute-start.6
  117.1 4.2 %collective-permute-start.7 = (f32[32,512]{1,0:T(8,128)S(1)}, f32[32,512]{1,0:T(8,128)S(1)}, u32[]{:S(2)}, u32[]{:S(2)}) collective-permute-start(f32[32,512]{1,0:T(8,128)S(1)} %get-tuple-element.69.sr_ref), channel_id=1, source_target_pairs={{0,8},{8,16},{16,24},{24,32},{32,40},{40,48},{48,56},{56,64},{64,7... | collective-permute-start | bytes 196616 | tf_op jit(solution)/shard_map/ppermute | solution.py:580
  121.3 2.7 %shard_map.131 = (f32[32,1024]{1,0:T(8,128)S(1)}, f32[128,128]{1,0:T(8,128)S(1)}, f32[32,128]{1,0:T(8,128)S(1)}) custom-call(f32[1536,128]{1,0:T(8,128)S(1)} %bitcast.22, f32[256,256]{1,0:T(8,128)S(1)} %copy-done.2, f32[72,1024]{1,0:T(8,128)S(1)} %get-tuple-element.60.refs_6_.refs_2_, f32[96,512]{1,0:T(8,128)S(1)} %get-tuple-element.64.refs_2_.refs_3_.refs_5_), custom_call_target="tpu_custom_call" | custom-call | tf_op jit(solution)/shard_map/pallas_call | solution.py:629
  124.0 0.5 shard_map.133
  124.5 1.3 collective-permute-start.8
  125.8 4.0 %collective-permute-start.9 = (f32[32,512]{1,0:T(8,128)S(1)}, f32[32,512]{1,0:T(8,128)S(1)}, u32[]{:S(2)}, u32[]{:S(2)}) collective-permute-start(f32[32,512]{1,0:T(8,128)S(1)} %get-tuple-element.72.sr_ref.refs_4_), channel_id=1, source_target_pairs={{0,8},{8,16},{16,24},{24,32},{32,40},{40,48},{48,56},{56,64},{64,7... | collective-permute-start | bytes 196616 | tf_op jit(solution)/shard_map/ppermute | solution.py:580
  129.8 1.0 shard_map.134
  130.8 0.3 collective-permute-done.9.pr_ref
  131.1 0.5 shard_map.135
  131.6 1.3 collective-permute-start.10
  132.9 4.3 %collective-permute-start.11 = (f32[32,512]{1,0:T(8,128)S(1)}, f32[32,512]{1,0:T(8,128)S(1)}, u32[]{:S(2)}, u32[]{:S(2)}) collective-permute-start(f32[32,512]{1,0:T(8,128)S(1)} %get-tuple-element.84.refs_3_), channel_id=1, source_target_pairs={{0,8},{8,16},{16,24},{24,32},{32,40},{40,48},{48,56},{56,64},{64,7... | collective-permute-start | bytes 196616 | tf_op jit(solution)/shard_map/ppermute | solution.py:580
  137.2 0.7 shard_map.136
  138.0 0.6 collective-permute-done.11.refs_5_
  138.6 1.3 shard_map.137
  139.8 23.9 %all_to_all.33.parts_ref = f32[64,8,128]{2,1,0:T(8,128)S(1)} all-to-all(f32[64,8,128]{2,1,0:T(8,128)S(1)} %bitcast.30), channel_id=1, replica_groups=mesh['y'=4,'zh'=8,'zl'=2,'x'=4,'c'=2] {'y','zl','x','c'}, dimensions={0} | all-to-all | bytes 524288 | tf_op jit(solution)/shard_map/all_to_all | solution.py:513
  163.7 0.1 shard_map.138
  163.8 14.4 %all_to_all.34.parts_ref = f32[8,8,128]{2,1,0:T(8,128)S(1)} all-to-all(f32[8,8,128]{2,1,0:T(8,128)S(1)} %shard_map.138), channel_id=1, replica_groups=mesh['y'=4,'zh'=8,'zl'=2,'x'=4,'c'=2] {'zh'}, dimensions={0} | all-to-all | bytes 65536 | tf_op jit(solution)/shard_map/all_to_all | solution.py:513
  178.2 15.0 %all_to_all.35 = f32[64,8,128]{2,1,0:T(8,128)S(1)} all-to-all(f32[64,8,128]{2,1,0:T(8,128)S(1)} %shard_map.139), channel_id=1, replica_groups=mesh['y'=4,'zh'=8,'zl'=2,'x'=4,'c'=2] {'y','zl','x','c'}, dimensions={0} | all-to-all | bytes 524288 | tf_op jit(solution)/shard_map/all_to_all | solution.py:513
  193.3 3.2 %shard_map.140 = (f32[32,1024]{1,0:T(8,128)}, f32[32,512]{1,0:T(8,128)}, f32[32,256]{1,0:T(8,128)}, f32[32,32]{1,0:T(8,128)}) custom-call(f32[512,128]{1,0:T(8,128)S(1)} %bitcast.28, f32[256,256]{1,0:T(8,128)S(1)} %get-tuple-element.87.refs_1_, f32[32,128]{1,0:T(8,128)S(1)} %get-tuple-element.66.scal_ref.refs_2_.refs_0_.refs_9_, ...), custom_call_target="tpu_custom_call" | custom-call | tf_op jit(solution)/shard_map/pallas_call | solution.py:657
  (23 shorter events, 0.1 us)
Async XLA Ops:
  0.6 8.9 %copy-start.6 = (s32[1,1,512]{2,1,0:T(1,128)S(1)}, s32[1,1,512]{2,1,0:T(1,128)}, u32[]{:S(2)}) copy-start(s32[1,1,512]{2,1,0:T(1,128)} %param.14) | copy-start | bytes 6148
  0.6 8.9 %copy-start.1 = (bf16[1,1,1024,1024]{3,2,1,0:T(8,128)(2,1)S(1)}, bf16[1,1,1024,1024]{3,2,1,0:T(8,128)(2,1)}, u32[]{:S(2)}) copy-start(bf16[1,1,1024,1024]{3,2,1,0:T(8,128)(2,1)} %param.10) | copy-start | bytes 6291460
  3.8 7.3 %collective-permute-start.1 = (f32[48,512]{1,0:T(8,128)}, f32[48,512]{1,0:T(8,128)S(1)}, u32[]{:S(2)}, u32[]{:S(2)}) collective-permute-start(f32[48,512]{1,0:T(8,128)} %get-tuple-element.52.refs_1_.refs_5_), channel_id=1, source_target_pairs={{0,8},{8,16},{16,24},{24,32},{32,40},{40,48},{48,56},{56,64},{64,7... | collective-permute-start | bytes 294920 | tf_op jit(solution)/shard_map/ppermute | solution.py:580
  8.2 5.8 %collective-permute-start = (f32[48,512]{1,0:T(8,128)}, f32[48,512]{1,0:T(8,128)S(1)}, u32[]{:S(2)}, u32[]{:S(2)}) collective-permute-start(f32[48,512]{1,0:T(8,128)} %get-tuple-element.50.refs_0_.refs_4_), channel_id=1, source_target_pairs={{8,0},{16,8},{24,16},{32,24},{40,32},{48,40},{56,48},{64,56},{72,6... | collective-permute-start | bytes 294920 | tf_op jit(solution)/shard_map/ppermute | solution.py:580
  9.5 4.4 %copy-start.3 = (f32[48,512]{1,0:T(8,128)S(1)}, f32[48,512]{1,0:T(8,128)}, u32[]{:S(2)}) copy-start(f32[48,512]{1,0:T(8,128)} %get-tuple-element.50.refs_0_.refs_4_) | copy-start | bytes 294916
  9.6 4.4 %copy-start.5 = (f32[48,512]{1,0:T(8,128)S(1)}, f32[48,512]{1,0:T(8,128)}, u32[]{:S(2)}) copy-start(f32[48,512]{1,0:T(8,128)} %get-tuple-element.52.refs_1_.refs_5_) | copy-start | bytes 294916
  11.1 9.3 %copy-start = (bf16[1,1,1024,1024]{3,2,1,0:T(8,128)(2,1)S(1)}, bf16[1,1,1024,1024]{3,2,1,0:T(8,128)(2,1)}, u32[]{:S(2)}) copy-start(bf16[1,1,1024,1024]{3,2,1,0:T(8,128)(2,1)} %param.9) | copy-start | bytes 6291460
  14.4 9.6 %collective-permute-start.2 = (f32[64,512]{1,0:T(8,128)S(1)}, f32[64,512]{1,0:T(8,128)S(1)}, u32[]{:S(2)}, u32[]{:S(2)}) collective-permute-start(f32[64,512]{1,0:T(8,128)S(1)} %get-tuple-element.53.refs_0_.refs_4_), channel_id=1, source_target_pairs={{8,0},{16,8},{24,16},{32,24},{40,32},{48,40},{56,48},{64,56},{72,6... | collective-permute-start | bytes 393224 | tf_op jit(solution)/shard_map/ppermute | solution.py:580
  15.7 6.2 %copy-start.4 = (bf16[1,1,1024,256]{3,2,1,0:T(8,128)(2,1)S(1)}, bf16[1,1,1024,256]{3,2,1,0:T(8,128)(2,1)}, u32[]{:S(2)}) copy-start(bf16[1,1,1024,256]{3,2,1,0:T(8,128)(2,1)} %param.16) | copy-start | bytes 1572868
  15.8 6.2 %copy-start.8 = (f32[1,1,1024]{2,1,0:T(1,128)S(1)}, f32[1,1,1024]{2,1,0:T(1,128)}, u32[]{:S(2)}) copy-start(f32[1,1,1024]{2,1,0:T(1,128)} %param.17) | copy-start | bytes 12292
  15.8 8.3 %collective-permute-start.3 = (f32[64,512]{1,0:T(8,128)S(1)}, f32[64,512]{1,0:T(8,128)S(1)}, u32[]{:S(2)}, u32[]{:S(2)}) collective-permute-start(f32[64,512]{1,0:T(8,128)S(1)} %get-tuple-element.54.refs_1_.refs_5_), channel_id=1, source_target_pairs={{0,8},{8,16},{16,24},{24,32},{32,40},{40,48},{48,56},{56,64},{64,7... | collective-permute-start | bytes 393224 | tf_op jit(solution)/shard_map/ppermute | solution.py:580
  21.9 9.1 %copy-start.7 = (f32[32,8]{1,0:T(8,128)S(1)}, f32[32,8]{1,0:T(8,128)}, u32[]{:S(2)}) copy-start(f32[32,8]{1,0:T(8,128)} %get-tuple-element.51.refs_1_) | copy-start | bytes 3076
  24.6 8.3 %collective-permute-start.4 = (f32[80,512]{1,0:T(8,128)S(1)}, f32[80,512]{1,0:T(8,128)S(1)}, u32[]{:S(2)}, u32[]{:S(2)}) collective-permute-start(f32[80,512]{1,0:T(8,128)S(1)} %get-tuple-element.61.refs_7_.refs_0_), channel_id=1, source_target_pairs={{8,0},{16,8},{24,16},{32,24},{40,32},{48,40},{56,48},{64,56},{72,6... | collective-permute-start | bytes 491528 | tf_op jit(solution)/shard_map/ppermute | solution.py:580
  25.9 7.3 %collective-permute-start.5 = (f32[80,512]{1,0:T(8,128)S(1)}, f32[80,512]{1,0:T(8,128)S(1)}, u32[]{:S(2)}, u32[]{:S(2)}) collective-permute-start(f32[80,512]{1,0:T(8,128)S(1)} %get-tuple-element.62.refs_8_.refs_1_), channel_id=1, source_target_pairs={{0,8},{8,16},{16,24},{24,32},{32,40},{40,48},{48,56},{56,64},{64,7... | collective-permute-start | bytes 491528 | tf_op jit(solution)/shard_map/ppermute | solution.py:580
  73.7 40.3 %copy-start.2 = (f32[256,256]{1,0:T(8,128)S(1)}, f32[256,256]{1,0:T(8,128)}, u32[]{:S(2)}) copy-start(f32[256,256]{1,0:T(8,128)} %refs_1_.3) | copy-start | bytes 786436
  115.8 8.2 %collective-permute-start.6 = (f32[32,512]{1,0:T(8,128)S(1)}, f32[32,512]{1,0:T(8,128)S(1)}, u32[]{:S(2)}, u32[]{:S(2)}) collective-permute-start(f32[32,512]{1,0:T(8,128)S(1)} %get-tuple-element.68.sl_ref), channel_id=1, source_target_pairs={{8,0},{16,8},{24,16},{32,24},{40,32},{48,40},{56,48},{64,56},{72,6... | collective-permute-start | bytes 196616 | tf_op jit(solution)/shard_map/ppermute | solution.py:580
  117.1 6.9 %collective-permute-start.7 = (f32[32,512]{1,0:T(8,128)S(1)}, f32[32,512]{1,0:T(8,128)S(1)}, u32[]{:S(2)}, u32[]{:S(2)}) collective-permute-start(f32[32,512]{1,0:T(8,128)S(1)} %get-tuple-element.69.sr_ref), channel_id=1, source_target_pairs={{0,8},{8,16},{16,24},{24,32},{32,40},{40,48},{48,56},{56,64},{64,7... | collective-permute-start | bytes 196616 | tf_op jit(solution)/shard_map/ppermute | solution.py:580
  124.5 6.3 %collective-permute-start.8 = (f32[32,512]{1,0:T(8,128)S(1)}, f32[32,512]{1,0:T(8,128)S(1)}, u32[]{:S(2)}, u32[]{:S(2)}) collective-permute-start(f32[32,512]{1,0:T(8,128)S(1)} %get-tuple-element.71.sl_ref.refs_3_), channel_id=1, source_target_pairs={{8,0},{16,8},{24,16},{32,24},{40,32},{48,40},{56,48},{64,56},{72,6... | collective-permute-start | bytes 196616 | tf_op jit(solution)/shard_map/ppermute | solution.py:580
  125.8 5.3 %collective-permute-start.9 = (f32[32,512]{1,0:T(8,128)S(1)}, f32[32,512]{1,0:T(8,128)S(1)}, u32[]{:S(2)}, u32[]{:S(2)}) collective-permute-start(f32[32,512]{1,0:T(8,128)S(1)} %get-tuple-element.72.sr_ref.refs_4_), channel_id=1, source_target_pairs={{0,8},{8,16},{16,24},{24,32},{32,40},{40,48},{48,56},{56,64},{64,7... | collective-permute-start | bytes 196616 | tf_op jit(solution)/shard_map/ppermute | solution.py:580
  131.6 6.3 %collective-permute-start.10 = (f32[32,512]{1,0:T(8,128)S(1)}, f32[32,512]{1,0:T(8,128)S(1)}, u32[]{:S(2)}, u32[]{:S(2)}) collective-permute-start(f32[32,512]{1,0:T(8,128)S(1)} %get-tuple-element.83.refs_2_), channel_id=1, source_target_pairs={{8,0},{16,8},{24,16},{32,24},{40,32},{48,40},{56,48},{64,56},{72,6... | collective-permute-start | bytes 196616 | tf_op jit(solution)/shard_map/ppermute | solution.py:580
  132.9 5.6 %collective-permute-start.11 = (f32[32,512]{1,0:T(8,128)S(1)}, f32[32,512]{1,0:T(8,128)S(1)}, u32[]{:S(2)}, u32[]{:S(2)}) collective-permute-start(f32[32,512]{1,0:T(8,128)S(1)} %get-tuple-element.84.refs_3_), channel_id=1, source_target_pairs={{0,8},{8,16},{16,24},{24,32},{32,40},{40,48},{48,56},{56,64},{64,7... | collective-permute-start | bytes 196616 | tf_op jit(solution)/shard_map/ppermute | solution.py:580

commit v9 on v8

--- a/solution.py
+++ b/solution.py
@@ -113,7 +113,7 @@
     dst[:face, :] = jnp.dot(back, dst[:face, :], preferred_element_type=F32).astype(BF16)
 
 
-def basis_kernel(prev_ref, nm_ref, mass_ref, prev_out, flip_out, mass_out, gram_out, *, total):
+def basis_kernel(prev_ref, nm_ref, mass_ref, prev_out, flip_out, mass_out, *, total):
     face = nm_ref.shape[1]
     back = from_order(nm_ref[...], face).astype(BF16)
     prev_out[face:, :] = prev_ref[face:, :]
@@ -123,6 +123,10 @@
     mass_out[:, face:] = mass[:, face:]
     left = jnp.broadcast_to(mass[:, :face], (8, face))
     mass_out[:, :face] = nn(left, to_order(nm_ref[...], face))[0:1]
+
+
+def gram_kernel(prev_ref, mass_ref, gram_out, *, total):
+    mass = mass_ref[...] / total
     column = jnp.transpose(jnp.broadcast_to(mass, (8, mass.shape[1])))[:, 0:1]
     wide = prev_ref[...].astype(F32)
     gram_out[...] = lax.dot_general(
@@ -596,15 +600,9 @@
         chain += [t, sl, sr]
         near = exchange(sl, sr)
         inv_p = call(matrix_kernel, square)(inverse_block, nm_row)
-        prev_p, prev_t, mass_p, gram = call(
-            lambda *refs: basis_kernel(*refs, total=total),
-            (
-                jax.ShapeDtypeStruct(earlier.shape, BF16),
-                jax.ShapeDtypeStruct(earlier.shape[::-1], BF16),
-                shape(1, rows),
-                shape(count, count),
-            ),
-        )(earlier, nm_row, weights[None, :])
+        gram = call(lambda *refs: gram_kernel(*refs, total=total), shape(count, count))(
+            earlier, weights[None, :]
+        )
         near, gram = lax.optimization_barrier((near, gram))
         t, sl, sr = step(2, sl, sr, near, inv_p)
         chain += [t, sl, sr]
@@ -635,6 +633,16 @@
             sl, sr, *near, mask, z0, scal, inv_p
         )
         near = exchange(ul, ur)
+        late, ul = lax.optimization_barrier((earlier, ul))
+        prev_p, prev_t, mass_p = call(
+            lambda *refs: basis_kernel(*refs, total=total),
+            (
+                jax.ShapeDtypeStruct(earlier.shape, BF16),
+                jax.ShapeDtypeStruct(earlier.shape[::-1], BF16),
+                shape(1, rows),
+            ),
+        )(late, nm_row, weights[None, :])
+        near, prev_p = lax.optimization_barrier((near, prev_p))
         w1c, r1, base, gram, back = call(
             lambda *refs: base_kernel(*refs, cols=cols, count=count),
             (wide, part, shape(4 * cols, rows), shape(count, count),

time: 197 us -> 197 us (level)
  transfers between devices with their start and end apart: 12 -> 12, of which waited for: 4 -> 3; matrix products, arithmetic and copies ran while one was open for 0% -> 0% of each run, Pallas kernels for 6% -> 6%
where the time goes in v9:
time: 197 us; the launch traced here: 196 us
  blocking collectives  132 us (67%)
  starting transfers between devices  34 us (17%)
  Pallas kernels  24.8 us (13%)
  waiting for transfers between devices  3.85 us (2%)
    all_to_all x6, blocking collectives, swap(): return lax.all_to_all(parts, axes, 0, 0, tiled=True)  132 us
    ppermute x12, starting transfers between devices, exchange(): return (lax.ppermute(sl, along, behind), lax.ppermute(sr, along, ahead))  34 us
  transfers between devices with their start and end apart: 12, of which 3 were waited for; matrix products, arithmetic and copies ran while one was open for 0% of the time, Pallas kernels for 6%

profile of v9, /device:TPU:1, one launch (start us, length us, event | category | flops | bytes accessed | tf_op | source)
XLA Modules:
  0.0 196.0 jit_solution(9663954234218227933)
XLA Ops:
  0.7 3.2 %shard_map.120 = (f32[48,512]{1,0:T(8,128)}, f32[48,512]{1,0:T(8,128)}, f32[32,8]{1,0:T(8,128)}) custom-call(bf16[1024,1024]{1,0:T(8,128)(2,1)} %bitcast.24, f32[32,1024]{1,0:T(8,128)} %bitcast.39, f32[8,1024]{1,0:T(8,128)} %bitcast.40, s32[1,512]{1,0:T(1,128)} %bitcast.32, s32[1,8]{1,0:T(1,128)} %bitcast.41), custom_call_target="tpu_custom_call" | custom-call | tf_op jit(solution)/shard_map/pallas_call | solution.py:567
  3.8 4.4 %collective-permute-start.1 = (f32[48,512]{1,0:T(8,128)}, f32[48,512]{1,0:T(8,128)S(1)}, u32[]{:S(2)}, u32[]{:S(2)}) collective-permute-start(f32[48,512]{1,0:T(8,128)} %get-tuple-element.56.refs_1_.refs_5_), channel_id=1, source_target_pairs={{0,8},{8,16},{16,24},{24,32},{32,40},{40,48},{48,56},{56,64},{64,7... | collective-permute-start | bytes 294920 | tf_op jit(solution)/shard_map/ppermute | solution.py:584
  8.2 1.3 collective-permute-start
  9.5 0.0 copy-start.4
  9.6 1.5 shard_map.121.refs_5_.refs_2_.mat_ref
  11.1 0.0 copy-start
  11.1 0.0 collective-permute-done.1.refs_3_
  11.1 2.9 %collective-permute-done.refs_2_ = f32[48,512]{1,0:T(8,128)S(1)} collective-permute-done((f32[48,512]{1,0:T(8,128)}, f32[48,512]{1,0:T(8,128)S(1)}, u32[]{:S(2)}, u32[]{:S(2)}) %collective-permute-start) | collective-permute-done | bytes 98336 | tf_op jit(solution)/shard_map/ppermute | solution.py:584
  14.0 0.5 shard_map.122
  14.5 1.3 collective-permute-start.2
  15.8 0.0 copy-start.1
  15.8 0.0 copy-start.8
  15.8 4.6 %collective-permute-start.3 = (f32[64,512]{1,0:T(8,128)S(1)}, f32[64,512]{1,0:T(8,128)S(1)}, u32[]{:S(2)}, u32[]{:S(2)}) collective-permute-start(f32[64,512]{1,0:T(8,128)S(1)} %get-tuple-element.58.refs_1_.refs_5_), channel_id=1, source_target_pairs={{0,8},{8,16},{16,24},{24,32},{32,40},{40,48},{48,56},{56,64},{64,7... | collective-permute-start | bytes 393224 | tf_op jit(solution)/shard_map/ppermute | solution.py:584
  20.4 1.5 shard_map.124.refs_5_.mat_ref.refs_8_
  21.9 0.0 copy-start.7
  21.9 1.4 shard_map.123.refs_2_
  23.4 0.5 shard_map.125
  23.9 1.3 collective-permute-start.4
  25.2 5.1 %collective-permute-start.5 = (f32[80,512]{1,0:T(8,128)S(1)}, f32[80,512]{1,0:T(8,128)S(1)}, u32[]{:S(2)}, u32[]{:S(2)}) collective-permute-start(f32[80,512]{1,0:T(8,128)S(1)} %get-tuple-element.65.refs_8_.refs_1_), channel_id=1, source_target_pairs={{0,8},{8,16},{16,24},{24,32},{32,40},{40,48},{48,56},{56,64},{64,7... | collective-permute-start | bytes 491528 | tf_op jit(solution)/shard_map/ppermute | solution.py:584
  30.3 1.8 shard_map.126.refs_0_
  32.1 0.4 collective-permute-done.5.refs_3_
  32.5 0.6 shard_map.127
  33.1 1.0 shard_map.128
  34.1 38.9 %all_to_all.30.parts_ref = f32[64,24,128]{2,1,0:T(8,128)S(1)} all-to-all(f32[64,24,128]{2,1,0:T(8,128)S(1)} %bitcast.26), channel_id=1, replica_groups=mesh['y'=4,'zh'=8,'zl'=2,'x'=4,'c'=2] {'y','zl','x','c'}, dimensions={0} | all-to-all | bytes 1572864 | tf_op jit(solution)/shard_map/all_to_all | solution.py:517
  73.0 0.1 shard_map.129
  73.1 18.3 %all_to_all.31.parts_ref = f32[8,24,128]{2,1,0:T(8,128)S(1)} all-to-all(f32[8,24,128]{2,1,0:T(8,128)S(1)} %shard_map.129), channel_id=1, replica_groups=mesh['y'=4,'zh'=8,'zl'=2,'x'=4,'c'=2] {'zh'}, dimensions={0} | all-to-all | bytes 196608 | tf_op jit(solution)/shard_map/all_to_all | solution.py:517
  91.4 0.1 shard_map.130
  91.4 22.1 %all_to_all.32 = f32[64,24,128]{2,1,0:T(8,128)S(1)} all-to-all(f32[64,24,128]{2,1,0:T(8,128)S(1)} %shard_map.130), channel_id=1, replica_groups=mesh['y'=4,'zh'=8,'zl'=2,'x'=4,'c'=2] {'y','zl','x','c'}, dimensions={0} | all-to-all | bytes 1572864 | tf_op jit(solution)/shard_map/all_to_all | solution.py:517
  113.5 1.8 shard_map.132
  115.3 1.3 collective-permute-start.6
  116.6 4.2 %collective-permute-start.7 = (f32[32,512]{1,0:T(8,128)S(1)}, f32[32,512]{1,0:T(8,128)S(1)}, u32[]{:S(2)}, u32[]{:S(2)}) collective-permute-start(f32[32,512]{1,0:T(8,128)S(1)} %get-tuple-element.72.sr_ref), channel_id=1, source_target_pairs={{0,8},{8,16},{16,24},{24,32},{32,40},{40,48},{48,56},{56,64},{64,7... | collective-permute-start | bytes 196616 | tf_op jit(solution)/shard_map/ppermute | solution.py:584
  120.8 2.7 %shard_map.131 = (f32[32,1024]{1,0:T(8,128)S(1)}, f32[128,128]{1,0:T(8,128)S(1)}, f32[32,128]{1,0:T(8,128)S(1)}) custom-call(f32[1536,128]{1,0:T(8,128)S(1)} %bitcast.22, f32[256,256]{1,0:T(8,128)S(1)} %copy-done.3, f32[72,1024]{1,0:T(8,128)S(1)} %get-tuple-element.63.refs_6_.refs_2_, f32[96,512]{1,0:T(8,128)S(1)} %get-tuple-element.67.refs_2_.refs_3_.refs_5_), custom_call_target="tpu_custom_call" | custom-call | tf_op jit(solution)/shard_map/pallas_call | solution.py:627
  123.5 0.5 shard_map.133
  124.0 1.3 collective-permute-start.8
  125.4 4.0 %collective-permute-start.9 = (f32[32,512]{1,0:T(8,128)S(1)}, f32[32,512]{1,0:T(8,128)S(1)}, u32[]{:S(2)}, u32[]{:S(2)}) collective-permute-start(f32[32,512]{1,0:T(8,128)S(1)} %get-tuple-element.76.sr_ref.refs_4_), channel_id=1, source_target_pairs={{0,8},{8,16},{16,24},{24,32},{32,40},{40,48},{48,56},{56,64},{64,7... | collective-permute-start | bytes 196616 | tf_op jit(solution)/shard_map/ppermute | solution.py:584
  129.3 1.0 shard_map.134
  130.3 0.9 shard_map.135
  131.3 0.5 shard_map.136
  131.7 1.3 collective-permute-start.10
  133.1 4.0 %collective-permute-start.11 = (f32[32,512]{1,0:T(8,128)S(1)}, f32[32,512]{1,0:T(8,128)S(1)}, u32[]{:S(2)}, u32[]{:S(2)}) collective-permute-start(f32[32,512]{1,0:T(8,128)S(1)} %get-tuple-element.92.refs_3_), channel_id=1, source_target_pairs={{0,8},{8,16},{16,24},{24,32},{32,40},{40,48},{48,56},{56,64},{64,7... | collective-permute-start | bytes 196616 | tf_op jit(solution)/shard_map/ppermute | solution.py:584
  137.1 0.7 shard_map.137
  137.8 0.6 collective-permute-done.11.refs_5_
  138.4 1.3 shard_map.138
  139.6 23.6 %all_to_all.33.parts_ref = f32[64,8,128]{2,1,0:T(8,128)S(1)} all-to-all(f32[64,8,128]{2,1,0:T(8,128)S(1)} %bitcast.31), channel_id=1, replica_groups=mesh['y'=4,'zh'=8,'zl'=2,'x'=4,'c'=2] {'y','zl','x','c'}, dimensions={0} | all-to-all | bytes 524288 | tf_op jit(solution)/shard_map/all_to_all | solution.py:517
  163.3 0.1 shard_map.139
  163.3 14.4 %all_to_all.34.parts_ref = f32[8,8,128]{2,1,0:T(8,128)S(1)} all-to-all(f32[8,8,128]{2,1,0:T(8,128)S(1)} %shard_map.139), channel_id=1, replica_groups=mesh['y'=4,'zh'=8,'zl'=2,'x'=4,'c'=2] {'zh'}, dimensions={0} | all-to-all | bytes 65536 | tf_op jit(solution)/shard_map/all_to_all | solution.py:517
  177.8 15.0 %all_to_all.35 = f32[64,8,128]{2,1,0:T(8,128)S(1)} all-to-all(f32[64,8,128]{2,1,0:T(8,128)S(1)} %shard_map.140), channel_id=1, replica_groups=mesh['y'=4,'zh'=8,'zl'=2,'x'=4,'c'=2] {'y','zl','x','c'}, dimensions={0} | all-to-all | bytes 524288 | tf_op jit(solution)/shard_map/all_to_all | solution.py:517
  192.8 3.2 %shard_map.141 = (f32[32,1024]{1,0:T(8,128)}, f32[32,512]{1,0:T(8,128)}, f32[32,256]{1,0:T(8,128)}, f32[32,32]{1,0:T(8,128)}) custom-call(f32[512,128]{1,0:T(8,128)S(1)} %bitcast.30, f32[256,256]{1,0:T(8,128)S(1)} %get-tuple-element.95.refs_1_, f32[32,128]{1,0:T(8,128)S(1)} %get-tuple-element.69.scal_ref.refs_2_.refs_0_.refs_9_, ...), custom_call_target="tpu_custom_call" | custom-call | tf_op jit(solution)/shard_map/pallas_call | solution.py:665
  (24 shorter events, 0.1 us)
Async XLA Ops:
  0.6 8.9 %copy-start.6 = (s32[1,1,512]{2,1,0:T(1,128)S(1)}, s32[1,1,512]{2,1,0:T(1,128)}, u32[]{:S(2)}) copy-start(s32[1,1,512]{2,1,0:T(1,128)} %param.14) | copy-start | bytes 6148
  0.6 8.9 %copy-start.2 = (bf16[1,1,1024,1024]{3,2,1,0:T(8,128)(2,1)S(1)}, bf16[1,1,1024,1024]{3,2,1,0:T(8,128)(2,1)}, u32[]{:S(2)}) copy-start(bf16[1,1,1024,1024]{3,2,1,0:T(8,128)(2,1)} %param.10) | copy-start | bytes 6291460
  3.8 7.3 %collective-permute-start.1 = (f32[48,512]{1,0:T(8,128)}, f32[48,512]{1,0:T(8,128)S(1)}, u32[]{:S(2)}, u32[]{:S(2)}) collective-permute-start(f32[48,512]{1,0:T(8,128)} %get-tuple-element.56.refs_1_.refs_5_), channel_id=1, source_target_pairs={{0,8},{8,16},{16,24},{24,32},{32,40},{40,48},{48,56},{56,64},{64,7... | collective-permute-start | bytes 294920 | tf_op jit(solution)/shard_map/ppermute | solution.py:584
  8.2 5.8 %collective-permute-start = (f32[48,512]{1,0:T(8,128)}, f32[48,512]{1,0:T(8,128)S(1)}, u32[]{:S(2)}, u32[]{:S(2)}) collective-permute-start(f32[48,512]{1,0:T(8,128)} %get-tuple-element.54.refs_0_.refs_4_), channel_id=1, source_target_pairs={{8,0},{16,8},{24,16},{32,24},{40,32},{48,40},{56,48},{64,56},{72,6... | collective-permute-start | bytes 294920 | tf_op jit(solution)/shard_map/ppermute | solution.py:584
  9.5 4.4 %copy-start.4 = (f32[48,512]{1,0:T(8,128)S(1)}, f32[48,512]{1,0:T(8,128)}, u32[]{:S(2)}) copy-start(f32[48,512]{1,0:T(8,128)} %get-tuple-element.54.refs_0_.refs_4_) | copy-start | bytes 294916
  9.6 4.4 %copy-start.5 = (f32[48,512]{1,0:T(8,128)S(1)}, f32[48,512]{1,0:T(8,128)}, u32[]{:S(2)}) copy-start(f32[48,512]{1,0:T(8,128)} %get-tuple-element.56.refs_1_.refs_5_) | copy-start | bytes 294916
  11.1 9.4 %copy-start = (bf16[1,1,1024,1024]{3,2,1,0:T(8,128)(2,1)S(1)}, bf16[1,1,1024,1024]{3,2,1,0:T(8,128)(2,1)}, u32[]{:S(2)}) copy-start(bf16[1,1,1024,1024]{3,2,1,0:T(8,128)(2,1)} %param.9) | copy-start | bytes 6291460
  14.5 8.9 %collective-permute-start.2 = (f32[64,512]{1,0:T(8,128)S(1)}, f32[64,512]{1,0:T(8,128)S(1)}, u32[]{:S(2)}, u32[]{:S(2)}) collective-permute-start(f32[64,512]{1,0:T(8,128)S(1)} %get-tuple-element.57.refs_0_.refs_4_), channel_id=1, source_target_pairs={{8,0},{16,8},{24,16},{32,24},{40,32},{48,40},{56,48},{64,56},{72,6... | collective-permute-start | bytes 393224 | tf_op jit(solution)/shard_map/ppermute | solution.py:584
  15.8 6.1 %copy-start.1 = (bf16[1,1,1024,256]{3,2,1,0:T(8,128)(2,1)S(1)}, bf16[1,1,1024,256]{3,2,1,0:T(8,128)(2,1)}, u32[]{:S(2)}) copy-start(bf16[1,1,1024,256]{3,2,1,0:T(8,128)(2,1)} %param.16) | copy-start | bytes 1572868
  15.8 6.1 %copy-start.8 = (f32[1,1,1024]{2,1,0:T(1,128)S(1)}, f32[1,1,1024]{2,1,0:T(1,128)}, u32[]{:S(2)}) copy-start(f32[1,1,1024]{2,1,0:T(1,128)} %param.17) | copy-start | bytes 12292
  15.8 7.6 %collective-permute-start.3 = (f32[64,512]{1,0:T(8,128)S(1)}, f32[64,512]{1,0:T(8,128)S(1)}, u32[]{:S(2)}, u32[]{:S(2)}) collective-permute-start(f32[64,512]{1,0:T(8,128)S(1)} %get-tuple-element.58.refs_1_.refs_5_), channel_id=1, source_target_pairs={{0,8},{8,16},{16,24},{24,32},{32,40},{40,48},{48,56},{56,64},{64,7... | collective-permute-start | bytes 393224 | tf_op jit(solution)/shard_map/ppermute | solution.py:584
  21.9 8.4 %copy-start.7 = (f32[32,8]{1,0:T(8,128)S(1)}, f32[32,8]{1,0:T(8,128)}, u32[]{:S(2)}) copy-start(f32[32,8]{1,0:T(8,128)} %get-tuple-element.55.refs_1_) | copy-start | bytes 3076
  23.9 8.2 %collective-permute-start.4 = (f32[80,512]{1,0:T(8,128)S(1)}, f32[80,512]{1,0:T(8,128)S(1)}, u32[]{:S(2)}, u32[]{:S(2)}) collective-permute-start(f32[80,512]{1,0:T(8,128)S(1)} %get-tuple-element.64.refs_7_.refs_0_), channel_id=1, source_target_pairs={{8,0},{16,8},{24,16},{32,24},{40,32},{48,40},{56,48},{64,56},{72,6... | collective-permute-start | bytes 491528 | tf_op jit(solution)/shard_map/ppermute | solution.py:584
  25.2 7.3 %collective-permute-start.5 = (f32[80,512]{1,0:T(8,128)S(1)}, f32[80,512]{1,0:T(8,128)S(1)}, u32[]{:S(2)}, u32[]{:S(2)}) collective-permute-start(f32[80,512]{1,0:T(8,128)S(1)} %get-tuple-element.65.refs_8_.refs_1_), channel_id=1, source_target_pairs={{0,8},{8,16},{16,24},{24,32},{32,40},{40,48},{48,56},{56,64},{64,7... | collective-permute-start | bytes 491528 | tf_op jit(solution)/shard_map/ppermute | solution.py:584
  73.0 40.5 %copy-start.3 = (f32[256,256]{1,0:T(8,128)S(1)}, f32[256,256]{1,0:T(8,128)}, u32[]{:S(2)}) copy-start(f32[256,256]{1,0:T(8,128)} %refs_1_.3) | copy-start | bytes 786436
  115.3 8.2 %collective-permute-start.6 = (f32[32,512]{1,0:T(8,128)S(1)}, f32[32,512]{1,0:T(8,128)S(1)}, u32[]{:S(2)}, u32[]{:S(2)}) collective-permute-start(f32[32,512]{1,0:T(8,128)S(1)} %get-tuple-element.71.sl_ref), channel_id=1, source_target_pairs={{8,0},{16,8},{24,16},{32,24},{40,32},{48,40},{56,48},{64,56},{72,6... | collective-permute-start | bytes 196616 | tf_op jit(solution)/shard_map/ppermute | solution.py:584
  116.6 6.9 %collective-permute-start.7 = (f32[32,512]{1,0:T(8,128)S(1)}, f32[32,512]{1,0:T(8,128)S(1)}, u32[]{:S(2)}, u32[]{:S(2)}) collective-permute-start(f32[32,512]{1,0:T(8,128)S(1)} %get-tuple-element.72.sr_ref), channel_id=1, source_target_pairs={{0,8},{8,16},{16,24},{24,32},{32,40},{40,48},{48,56},{56,64},{64,7... | collective-permute-start | bytes 196616 | tf_op jit(solution)/shard_map/ppermute | solution.py:584
  124.0 7.2 %collective-permute-start.8 = (f32[32,512]{1,0:T(8,128)S(1)}, f32[32,512]{1,0:T(8,128)S(1)}, u32[]{:S(2)}, u32[]{:S(2)}) collective-permute-start(f32[32,512]{1,0:T(8,128)S(1)} %get-tuple-element.75.sl_ref.refs_3_), channel_id=1, source_target_pairs={{8,0},{16,8},{24,16},{32,24},{40,32},{48,40},{56,48},{64,56},{72,6... | collective-permute-start | bytes 196616 | tf_op jit(solution)/shard_map/ppermute | solution.py:584
  125.4 5.9 %collective-permute-start.9 = (f32[32,512]{1,0:T(8,128)S(1)}, f32[32,512]{1,0:T(8,128)S(1)}, u32[]{:S(2)}, u32[]{:S(2)}) collective-permute-start(f32[32,512]{1,0:T(8,128)S(1)} %get-tuple-element.76.sr_ref.refs_4_), channel_id=1, source_target_pairs={{0,8},{8,16},{16,24},{24,32},{32,40},{40,48},{48,56},{56,64},{64,7... | collective-permute-start | bytes 196616 | tf_op jit(solution)/shard_map/ppermute | solution.py:584
  131.7 6.0 %collective-permute-start.10 = (f32[32,512]{1,0:T(8,128)S(1)}, f32[32,512]{1,0:T(8,128)S(1)}, u32[]{:S(2)}, u32[]{:S(2)}) collective-permute-start(f32[32,512]{1,0:T(8,128)S(1)} %get-tuple-element.91.refs_2_), channel_id=1, source_target_pairs={{8,0},{16,8},{24,16},{32,24},{40,32},{48,40},{56,48},{64,56},{72,6... | collective-permute-start | bytes 196616 | tf_op jit(solution)/shard_map/ppermute | solution.py:584
  133.1 5.3 %collective-permute-start.11 = (f32[32,512]{1,0:T(8,128)S(1)}, f32[32,512]{1,0:T(8,128)S(1)}, u32[]{:S(2)}, u32[]{:S(2)}) collective-permute-start(f32[32,512]{1,0:T(8,128)S(1)} %get-tuple-element.92.refs_3_), channel_id=1, source_target_pairs={{0,8},{8,16},{16,24},{24,32},{32,40},{40,48},{48,56},{56,64},{64,7... | collective-permute-start | bytes 196616 | tf_op jit(solution)/shard_map/ppermute | solution.py:584

commit v10 on v9

--- a/solution.py
+++ b/solution.py
@@ -596,14 +596,14 @@
         chain = [sl, sr]
         near = exchange(sl, sr)
         schur_p = call(matrix_kernel, square)(schur_block, nm_row)
+        gram = call(lambda *refs: gram_kernel(*refs, total=total), shape(count, count))(
+            earlier, weights[None, :]
+        )
+        near, gram = lax.optimization_barrier((near, gram))
         t, sl, sr = step(1, sl, sr, near, schur_p)
         chain += [t, sl, sr]
         near = exchange(sl, sr)
         inv_p = call(matrix_kernel, square)(inverse_block, nm_row)
-        gram = call(lambda *refs: gram_kernel(*refs, total=total), shape(count, count))(
-            earlier, weights[None, :]
-        )
-        near, gram = lax.optimization_barrier((near, gram))
         t, sl, sr = step(2, sl, sr, near, inv_p)
         chain += [t, sl, sr]
         near = exchange(sl, sr)

time: 197 us -> 196 us (level)
  transfers between devices with their start and end apart: 12 -> 12, of which waited for: 3 -> 4; matrix products, arithmetic and copies ran while one was open for 0% -> 0% of each run, Pallas kernels for 6% -> 6%
where the time goes in v10:
time: 196 us
  blocking collectives  133 us (68%)
  starting transfers between devices  33.9 us (17%)
  Pallas kernels  24.8 us (13%)
  waiting for transfers between devices  2.75 us (1%)
    all_to_all x6, blocking collectives, swap(): return lax.all_to_all(parts, axes, 0, 0, tiled=True)  133 us
    ppermute x12, starting transfers between devices, exchange(): return (lax.ppermute(sl, along, behind), lax.ppermute(sr, along, ahead))  33.9 us
  transfers between devices with their start and end apart: 12, of which 4 were waited for; matrix products, arithmetic and copies ran while one was open for 0% of the time, Pallas kernels for 6%

profile of v10, /device:TPU:1, one launch (start us, length us, event | category | flops | bytes accessed | tf_op | source)
XLA Modules:
  0.0 195.8 jit_solution(8073172448516617950)
XLA Ops:
  0.7 3.2 %shard_map.120 = (f32[48,512]{1,0:T(8,128)}, f32[48,512]{1,0:T(8,128)}, f32[32,8]{1,0:T(8,128)}) custom-call(bf16[1024,1024]{1,0:T(8,128)(2,1)} %bitcast.24, f32[32,1024]{1,0:T(8,128)} %bitcast.39, f32[8,1024]{1,0:T(8,128)} %bitcast.40, s32[1,512]{1,0:T(1,128)} %bitcast.32, s32[1,8]{1,0:T(1,128)} %bitcast.41), custom_call_target="tpu_custom_call" | custom-call | tf_op jit(solution)/shard_map/pallas_call | solution.py:567
  3.8 4.4 %collective-permute-start.1 = (f32[48,512]{1,0:T(8,128)}, f32[48,512]{1,0:T(8,128)S(1)}, u32[]{:S(2)}, u32[]{:S(2)}) collective-permute-start(f32[48,512]{1,0:T(8,128)} %get-tuple-element.56.refs_1_.refs_5_), channel_id=1, source_target_pairs={{0,8},{8,16},{16,24},{24,32},{32,40},{40,48},{48,56},{56,64},{64,7... | collective-permute-start | bytes 294920 | tf_op jit(solution)/shard_map/ppermute | solution.py:584
  8.2 1.3 collective-permute-start
  9.5 0.0 copy-start.1
  9.6 0.0 copy-start.8
  9.6 0.0 copy-start.4
  9.6 1.5 shard_map.122.refs_5_.refs_2_.mat_ref
  11.1 0.0 copy-start
  11.1 1.4 shard_map.121.refs_2_
  12.6 1.4 collective-permute-done.refs_2_
  14.0 0.5 shard_map.123
  14.4 1.3 collective-permute-start.2
  15.7 4.5 %collective-permute-start.3 = (f32[64,512]{1,0:T(8,128)S(1)}, f32[64,512]{1,0:T(8,128)S(1)}, u32[]{:S(2)}, u32[]{:S(2)}) collective-permute-start(f32[64,512]{1,0:T(8,128)S(1)} %get-tuple-element.62.refs_1_.refs_5_), channel_id=1, source_target_pairs={{0,8},{8,16},{16,24},{24,32},{32,40},{40,48},{48,56},{56,64},{64,7... | collective-permute-start | bytes 393224 | tf_op jit(solution)/shard_map/ppermute | solution.py:584
  20.2 1.5 shard_map.124.refs_5_.mat_ref.refs_8_
  21.7 0.0 copy-start.7
  21.8 0.4 collective-permute-done.3.refs_3_
  22.2 0.5 shard_map.125
  22.6 1.3 collective-permute-start.4
  23.9 5.1 %collective-permute-start.5 = (f32[80,512]{1,0:T(8,128)S(1)}, f32[80,512]{1,0:T(8,128)S(1)}, u32[]{:S(2)}, u32[]{:S(2)}) collective-permute-start(f32[80,512]{1,0:T(8,128)S(1)} %get-tuple-element.65.refs_8_.refs_1_), channel_id=1, source_target_pairs={{0,8},{8,16},{16,24},{24,32},{32,40},{40,48},{48,56},{56,64},{64,7... | collective-permute-start | bytes 491528 | tf_op jit(solution)/shard_map/ppermute | solution.py:584
  29.1 1.8 shard_map.126.refs_0_
  30.9 0.4 collective-permute-done.5.refs_3_
  31.3 0.6 shard_map.127
  31.8 1.0 shard_map.128
  32.9 39.9 %all_to_all.30.parts_ref = f32[64,24,128]{2,1,0:T(8,128)S(1)} all-to-all(f32[64,24,128]{2,1,0:T(8,128)S(1)} %bitcast.26), channel_id=1, replica_groups=mesh['y'=4,'zh'=8,'zl'=2,'x'=4,'c'=2] {'y','zl','x','c'}, dimensions={0} | all-to-all | bytes 1572864 | tf_op jit(solution)/shard_map/all_to_all | solution.py:517
  72.8 0.1 shard_map.129
  72.9 18.3 %all_to_all.31.parts_ref = f32[8,24,128]{2,1,0:T(8,128)S(1)} all-to-all(f32[8,24,128]{2,1,0:T(8,128)S(1)} %shard_map.129), channel_id=1, replica_groups=mesh['y'=4,'zh'=8,'zl'=2,'x'=4,'c'=2] {'zh'}, dimensions={0} | all-to-all | bytes 196608 | tf_op jit(solution)/shard_map/all_to_all | solution.py:517
  91.2 0.1 shard_map.130
  91.3 22.1 %all_to_all.32 = f32[64,24,128]{2,1,0:T(8,128)S(1)} all-to-all(f32[64,24,128]{2,1,0:T(8,128)S(1)} %shard_map.130), channel_id=1, replica_groups=mesh['y'=4,'zh'=8,'zl'=2,'x'=4,'c'=2] {'y','zl','x','c'}, dimensions={0} | all-to-all | bytes 1572864 | tf_op jit(solution)/shard_map/all_to_all | solution.py:517
  113.3 1.8 shard_map.132
  115.2 1.3 collective-permute-start.6
  116.5 4.2 %collective-permute-start.7 = (f32[32,512]{1,0:T(8,128)S(1)}, f32[32,512]{1,0:T(8,128)S(1)}, u32[]{:S(2)}, u32[]{:S(2)}) collective-permute-start(f32[32,512]{1,0:T(8,128)S(1)} %get-tuple-element.72.sr_ref), channel_id=1, source_target_pairs={{0,8},{8,16},{16,24},{24,32},{32,40},{40,48},{48,56},{56,64},{64,7... | collective-permute-start | bytes 196616 | tf_op jit(solution)/shard_map/ppermute | solution.py:584
  120.6 2.7 %shard_map.131 = (f32[32,1024]{1,0:T(8,128)S(1)}, f32[128,128]{1,0:T(8,128)S(1)}, f32[32,128]{1,0:T(8,128)S(1)}) custom-call(f32[1536,128]{1,0:T(8,128)S(1)} %bitcast.22, f32[256,256]{1,0:T(8,128)S(1)} %copy-done.3, f32[72,1024]{1,0:T(8,128)S(1)} %get-tuple-element.63.refs_6_.refs_2_, f32[96,512]{1,0:T(8,128)S(1)} %get-tuple-element.67.refs_2_.refs_3_.refs_5_), custom_call_target="tpu_custom_call" | custom-call | tf_op jit(solution)/shard_map/pallas_call | solution.py:627
  123.4 0.5 shard_map.133
  123.9 1.3 collective-permute-start.8
  125.2 4.0 %collective-permute-start.9 = (f32[32,512]{1,0:T(8,128)S(1)}, f32[32,512]{1,0:T(8,128)S(1)}, u32[]{:S(2)}, u32[]{:S(2)}) collective-permute-start(f32[32,512]{1,0:T(8,128)S(1)} %get-tuple-element.76.sr_ref.refs_4_), channel_id=1, source_target_pairs={{0,8},{8,16},{16,24},{24,32},{32,40},{40,48},{48,56},{56,64},{64,7... | collective-permute-start | bytes 196616 | tf_op jit(solution)/shard_map/ppermute | solution.py:584
  129.2 1.0 shard_map.134
  130.2 0.9 shard_map.135
  131.1 0.5 shard_map.136
  131.6 1.3 collective-permute-start.10
  132.9 4.0 %collective-permute-start.11 = (f32[32,512]{1,0:T(8,128)S(1)}, f32[32,512]{1,0:T(8,128)S(1)}, u32[]{:S(2)}, u32[]{:S(2)}) collective-permute-start(f32[32,512]{1,0:T(8,128)S(1)} %get-tuple-element.92.refs_3_), channel_id=1, source_target_pairs={{0,8},{8,16},{16,24},{24,32},{32,40},{40,48},{48,56},{56,64},{64,7... | collective-permute-start | bytes 196616 | tf_op jit(solution)/shard_map/ppermute | solution.py:584
  136.9 0.7 shard_map.137
  137.6 0.6 collective-permute-done.11.refs_5_
  138.2 1.3 shard_map.138
  139.5 23.6 %all_to_all.33.parts_ref = f32[64,8,128]{2,1,0:T(8,128)S(1)} all-to-all(f32[64,8,128]{2,1,0:T(8,128)S(1)} %bitcast.31), channel_id=1, replica_groups=mesh['y'=4,'zh'=8,'zl'=2,'x'=4,'c'=2] {'y','zl','x','c'}, dimensions={0} | all-to-all | bytes 524288 | tf_op jit(solution)/shard_map/all_to_all | solution.py:517
  163.1 0.1 shard_map.139
  163.2 14.4 %all_to_all.34.parts_ref = f32[8,8,128]{2,1,0:T(8,128)S(1)} all-to-all(f32[8,8,128]{2,1,0:T(8,128)S(1)} %shard_map.139), channel_id=1, replica_groups=mesh['y'=4,'zh'=8,'zl'=2,'x'=4,'c'=2] {'zh'}, dimensions={0} | all-to-all | bytes 65536 | tf_op jit(solution)/shard_map/all_to_all | solution.py:517
  177.6 15.0 %all_to_all.35 = f32[64,8,128]{2,1,0:T(8,128)S(1)} all-to-all(f32[64,8,128]{2,1,0:T(8,128)S(1)} %shard_map.140), channel_id=1, replica_groups=mesh['y'=4,'zh'=8,'zl'=2,'x'=4,'c'=2] {'y','zl','x','c'}, dimensions={0} | all-to-all | bytes 524288 | tf_op jit(solution)/shard_map/all_to_all | solution.py:517
  192.6 3.2 %shard_map.141 = (f32[32,1024]{1,0:T(8,128)}, f32[32,512]{1,0:T(8,128)}, f32[32,256]{1,0:T(8,128)}, f32[32,32]{1,0:T(8,128)}) custom-call(f32[512,128]{1,0:T(8,128)S(1)} %bitcast.30, f32[256,256]{1,0:T(8,128)S(1)} %get-tuple-element.95.refs_1_, f32[32,128]{1,0:T(8,128)S(1)} %get-tuple-element.69.scal_ref.refs_2_.refs_0_.refs_9_, ...), custom_call_target="tpu_custom_call" | custom-call | tf_op jit(solution)/shard_map/pallas_call | solution.py:665
  (24 shorter events, 0.1 us)
Async XLA Ops:
  0.6 8.9 %copy-start.6 = (s32[1,1,512]{2,1,0:T(1,128)S(1)}, s32[1,1,512]{2,1,0:T(1,128)}, u32[]{:S(2)}) copy-start(s32[1,1,512]{2,1,0:T(1,128)} %param.14) | copy-start | bytes 6148
  0.6 8.9 %copy-start.2 = (bf16[1,1,1024,1024]{3,2,1,0:T(8,128)(2,1)S(1)}, bf16[1,1,1024,1024]{3,2,1,0:T(8,128)(2,1)}, u32[]{:S(2)}) copy-start(bf16[1,1,1024,1024]{3,2,1,0:T(8,128)(2,1)} %param.10) | copy-start | bytes 6291460
  3.8 8.8 %collective-permute-start.1 = (f32[48,512]{1,0:T(8,128)}, f32[48,512]{1,0:T(8,128)S(1)}, u32[]{:S(2)}, u32[]{:S(2)}) collective-permute-start(f32[48,512]{1,0:T(8,128)} %get-tuple-element.56.refs_1_.refs_5_), channel_id=1, source_target_pairs={{0,8},{8,16},{16,24},{24,32},{32,40},{40,48},{48,56},{56,64},{64,7... | collective-permute-start | bytes 294920 | tf_op jit(solution)/shard_map/ppermute | solution.py:584
  8.2 5.8 %collective-permute-start = (f32[48,512]{1,0:T(8,128)}, f32[48,512]{1,0:T(8,128)S(1)}, u32[]{:S(2)}, u32[]{:S(2)}) collective-permute-start(f32[48,512]{1,0:T(8,128)} %get-tuple-element.54.refs_0_.refs_4_), channel_id=1, source_target_pairs={{8,0},{16,8},{24,16},{32,24},{40,32},{48,40},{56,48},{64,56},{72,6... | collective-permute-start | bytes 294920 | tf_op jit(solution)/shard_map/ppermute | solution.py:584
  9.5 1.6 copy-start.1
  9.6 1.6 copy-start.8
  9.6 4.4 %copy-start.4 = (f32[48,512]{1,0:T(8,128)S(1)}, f32[48,512]{1,0:T(8,128)}, u32[]{:S(2)}) copy-start(f32[48,512]{1,0:T(8,128)} %get-tuple-element.54.refs_0_.refs_4_) | copy-start | bytes 294916
  9.6 4.4 %copy-start.5 = (f32[48,512]{1,0:T(8,128)S(1)}, f32[48,512]{1,0:T(8,128)}, u32[]{:S(2)}) copy-start(f32[48,512]{1,0:T(8,128)} %get-tuple-element.56.refs_1_.refs_5_) | copy-start | bytes 294916
  11.1 9.1 %copy-start = (bf16[1,1,1024,1024]{3,2,1,0:T(8,128)(2,1)S(1)}, bf16[1,1,1024,1024]{3,2,1,0:T(8,128)(2,1)}, u32[]{:S(2)}) copy-start(bf16[1,1,1024,1024]{3,2,1,0:T(8,128)(2,1)} %param.9) | copy-start | bytes 6291460
  14.4 7.3 %collective-permute-start.2 = (f32[64,512]{1,0:T(8,128)S(1)}, f32[64,512]{1,0:T(8,128)S(1)}, u32[]{:S(2)}, u32[]{:S(2)}) collective-permute-start(f32[64,512]{1,0:T(8,128)S(1)} %get-tuple-element.61.refs_0_.refs_4_), channel_id=1, source_target_pairs={{8,0},{16,8},{24,16},{32,24},{40,32},{48,40},{56,48},{64,56},{72,6... | collective-permute-start | bytes 393224 | tf_op jit(solution)/shard_map/ppermute | solution.py:584
  15.7 6.4 %collective-permute-start.3 = (f32[64,512]{1,0:T(8,128)S(1)}, f32[64,512]{1,0:T(8,128)S(1)}, u32[]{:S(2)}, u32[]{:S(2)}) collective-permute-start(f32[64,512]{1,0:T(8,128)S(1)} %get-tuple-element.62.refs_1_.refs_5_), channel_id=1, source_target_pairs={{0,8},{8,16},{16,24},{24,32},{32,40},{40,48},{48,56},{56,64},{64,7... | collective-permute-start | bytes 393224 | tf_op jit(solution)/shard_map/ppermute | solution.py:584
  21.7 7.3 %copy-start.7 = (f32[32,8]{1,0:T(8,128)S(1)}, f32[32,8]{1,0:T(8,128)}, u32[]{:S(2)}) copy-start(f32[32,8]{1,0:T(8,128)} %get-tuple-element.55.refs_1_) | copy-start | bytes 3076
  22.6 8.3 %collective-permute-start.4 = (f32[80,512]{1,0:T(8,128)S(1)}, f32[80,512]{1,0:T(8,128)S(1)}, u32[]{:S(2)}, u32[]{:S(2)}) collective-permute-start(f32[80,512]{1,0:T(8,128)S(1)} %get-tuple-element.64.refs_7_.refs_0_), channel_id=1, source_target_pairs={{8,0},{16,8},{24,16},{32,24},{40,32},{48,40},{56,48},{64,56},{72,6... | collective-permute-start | bytes 491528 | tf_op jit(solution)/shard_map/ppermute | solution.py:584
  23.9 7.3 %collective-permute-start.5 = (f32[80,512]{1,0:T(8,128)S(1)}, f32[80,512]{1,0:T(8,128)S(1)}, u32[]{:S(2)}, u32[]{:S(2)}) collective-permute-start(f32[80,512]{1,0:T(8,128)S(1)} %get-tuple-element.65.refs_8_.refs_1_), channel_id=1, source_target_pairs={{0,8},{8,16},{16,24},{24,32},{32,40},{40,48},{48,56},{56,64},{64,7... | collective-permute-start | bytes 491528 | tf_op jit(solution)/shard_map/ppermute | solution.py:584
  72.8 40.6 %copy-start.3 = (f32[256,256]{1,0:T(8,128)S(1)}, f32[256,256]{1,0:T(8,128)}, u32[]{:S(2)}) copy-start(f32[256,256]{1,0:T(8,128)} %refs_1_.3) | copy-start | bytes 786436
  115.2 8.2 %collective-permute-start.6 = (f32[32,512]{1,0:T(8,128)S(1)}, f32[32,512]{1,0:T(8,128)S(1)}, u32[]{:S(2)}, u32[]{:S(2)}) collective-permute-start(f32[32,512]{1,0:T(8,128)S(1)} %get-tuple-element.71.sl_ref), channel_id=1, source_target_pairs={{8,0},{16,8},{24,16},{32,24},{40,32},{48,40},{56,48},{64,56},{72,6... | collective-permute-start | bytes 196616 | tf_op jit(solution)/shard_map/ppermute | solution.py:584
  116.5 6.9 %collective-permute-start.7 = (f32[32,512]{1,0:T(8,128)S(1)}, f32[32,512]{1,0:T(8,128)S(1)}, u32[]{:S(2)}, u32[]{:S(2)}) collective-permute-start(f32[32,512]{1,0:T(8,128)S(1)} %get-tuple-element.72.sr_ref), channel_id=1, source_target_pairs={{0,8},{8,16},{16,24},{24,32},{32,40},{40,48},{48,56},{56,64},{64,7... | collective-permute-start | bytes 196616 | tf_op jit(solution)/shard_map/ppermute | solution.py:584
  123.9 7.2 %collective-permute-start.8 = (f32[32,512]{1,0:T(8,128)S(1)}, f32[32,512]{1,0:T(8,128)S(1)}, u32[]{:S(2)}, u32[]{:S(2)}) collective-permute-start(f32[32,512]{1,0:T(8,128)S(1)} %get-tuple-element.75.sl_ref.refs_3_), channel_id=1, source_target_pairs={{8,0},{16,8},{24,16},{32,24},{40,32},{48,40},{56,48},{64,56},{72,6... | collective-permute-start | bytes 196616 | tf_op jit(solution)/shard_map/ppermute | solution.py:584
  125.2 5.9 %collective-permute-start.9 = (f32[32,512]{1,0:T(8,128)S(1)}, f32[32,512]{1,0:T(8,128)S(1)}, u32[]{:S(2)}, u32[]{:S(2)}) collective-permute-start(f32[32,512]{1,0:T(8,128)S(1)} %get-tuple-element.76.sr_ref.refs_4_), channel_id=1, source_target_pairs={{0,8},{8,16},{16,24},{24,32},{32,40},{40,48},{48,56},{56,64},{64,7... | collective-permute-start | bytes 196616 | tf_op jit(solution)/shard_map/ppermute | solution.py:584
  131.6 6.0 %collective-permute-start.10 = (f32[32,512]{1,0:T(8,128)S(1)}, f32[32,512]{1,0:T(8,128)S(1)}, u32[]{:S(2)}, u32[]{:S(2)}) collective-permute-start(f32[32,512]{1,0:T(8,128)S(1)} %get-tuple-element.91.refs_2_), channel_id=1, source_target_pairs={{8,0},{16,8},{24,16},{32,24},{40,32},{48,40},{56,48},{64,56},{72,6... | collective-permute-start | bytes 196616 | tf_op jit(solution)/shard_map/ppermute | solution.py:584
  132.9 5.3 %collective-permute-start.11 = (f32[32,512]{1,0:T(8,128)S(1)}, f32[32,512]{1,0:T(8,128)S(1)}, u32[]{:S(2)}, u32[]{:S(2)}) collective-permute-start(f32[32,512]{1,0:T(8,128)S(1)} %get-tuple-element.92.refs_3_), channel_id=1, source_target_pairs={{0,8},{8,16},{16,24},{24,32},{32,40},{40,48},{48,56},{56,64},{64,7... | collective-permute-start | bytes 196616 | tf_op jit(solution)/shard_map/ppermute | solution.py:584
